TPU v7x, 32 devices: a whole 2x2x4 slice. The times are simulated.
32 devices in a mesh: section: 8 (over z, y), dp: 4 (over x, core).
Axes of the slice: x: 2, y: 2, z: 4, core: 2. Of those that a mesh axis runs over, the one named last changes fastest.
Arguments:
- tokens: bfloat16 [4, 4, 128, 768], P(None, 'dp', 'section'), may hold values from -6 to 6
- lengths: int32 [4, 4, 4], P(None, 'dp'), may hold values from 1 to 96, 128 in all within a row
- cotangent: bfloat16 [4, 4, 128, 768], P(None, 'dp', 'section'), may hold values from -6 to 6
- first_gain: float32 [768], replicated, may hold values from 0.5 to 1.5
- first_shift: float32 [768], replicated, may hold values from -3 to 3
- qkv_weight: bfloat16 [768, 2304], replicated, may hold values from -0.21875 to 0.21875
- qv_bias: float32 [1536], replicated, may hold values from -3 to 3
- out_weight: bfloat16 [768, 768], replicated, may hold values from -0.625 to 0.625
- out_bias: float32 [768], replicated, may hold values from -3 to 3
- second_gain: float32 [768], replicated, may hold values from 0.5 to 1.5
- second_shift: float32 [768], replicated, may hold values from -3 to 3
- expand_weight: bfloat16 [768, 3072], replicated, may hold values from -0.21875 to 0.21875
- expand_bias: float32 [3072], replicated, may hold values from -3 to 3
- contract_weight: bfloat16 [3072, 768], replicated, may hold values from -0.15625 to 0.15625
- contract_bias: float32 [768], replicated, may hold values from -3 to 3
Outputs:
- result_tokens: bfloat16 [4, 4, 128, 768], P(None, 'dp', 'section')
- grad_tokens: float32 [4, 4, 128, 768], P(None, 'dp', 'section')
- grad_first_gain: float32 [768], P('dp')
- grad_first_shift: float32 [768], P('dp')
- grad_qkv_weight: float32 [768, 2304], P('dp')
- grad_qv_bias: float32 [1536], P('dp')
- grad_out_weight: float32 [768, 768], P('dp')
- grad_out_bias: float32 [768], P('dp')
- grad_second_gain: float32 [768], P('dp')
- grad_second_shift: float32 [768], P('dp')
- grad_expand_weight: float32 [768, 3072], P('dp')
- grad_expand_bias: float32 [3072], P('dp')
- grad_contract_weight: float32 [3072, 768], P('dp')
- grad_contract_bias: float32 [768], P('dp')
Inputs may be any that keep to these rules, and one draw needn't show every extreme that they name: Each row of 4 lengths sums to 128, and its largest is exactly 96.
All inputs are finite; a program needn't handle non-finite values.
Results may differ from a plain program's by a relative error of at most 0.017.
Values may be sent and summed in bfloat16 or wider, within the bound.
No kernel may reach another device: no remote copies, remote signals or barrier semaphores. Data moves between devices by JAX's collectives and lax.ppermute only.
A program may use at most 384 MiB of HBM per device.

v0:
```python
from functools import partial

import jax
import jax.numpy as jnp
from jax import lax
from jax.sharding import PartitionSpec as P

HEADS = 12
HEAD_DIM = 64


EPSILON = 1e-05
SCORE_SCALE = 0.125
MASKED = -1e30


def from_behind(array, axis, by):
    count = lax.axis_size(axis)
    pairs = [(i, i + by) for i in range(count) if 0 <= i + by < count]
    return lax.ppermute(array, axis, pairs)


def layer_norm(values, gain_row, shift_row):
    center = values - jnp.mean(values, axis=-1, keepdims=True)
    inverse = lax.rsqrt(jnp.mean(center * center, axis=-1, keepdims=True) + EPSILON)
    normed = center * inverse
    return (normed * gain_row + shift_row, normed, inverse)


def norm_back(upstream, normed, inverse, gain_row):
    scaled = upstream * gain_row
    return inverse * (
        scaled
        - jnp.mean(scaled, axis=-1, keepdims=True)
        - normed * jnp.mean(scaled * normed, axis=-1, keepdims=True)
    )


def allowed_from(length_row, row_count):
    seq_ends = jnp.cumsum(length_row)
    places = jnp.arange(row_count, dtype=jnp.int32)
    owners = jnp.sum((places[:, None] >= seq_ends[None, :]).astype(jnp.int32), axis=1)
    return (owners[:, None] == owners[None, :]) & (places[None, :] <= places[:, None])


def split_heads(matrix, row_count):
    return matrix.reshape(row_count, HEADS, HEAD_DIM)


def masked_scores(queries, key_rows, allowed):
    scores = (
        jnp.einsum("qhd,khd->hqk", queries, key_rows, preferred_element_type=jnp.float32)
        * SCORE_SCALE
    )
    return jnp.where(allowed[None], scores, MASKED)


def transpose_dot(left_side, right_side):
    return lax.dot_general(
        left_side, right_side, (((1,), (1,)), ((), ())), preferred_element_type=jnp.float32
    )


def column_outer(left_side, right_side):
    return lax.dot_general(
        left_side, right_side, (((0,), (0,)), ((), ())), preferred_element_type=jnp.float32
    )


def forward_layer(hidden, allowed, weights):
    (
        first_gain,
        first_shift,
        qkv_weight,
        qv_bias,
        out_weight,
        out_bias,
        second_gain,
        second_shift,
        expand_weight,
        expand_bias,
        contract_weight,
        contract_bias,
    ) = weights
    row_count, model_width = hidden.shape
    first_in, normed_one, inverse_one = layer_norm(hidden, first_gain, first_shift)
    first_low = first_in.astype(jnp.bfloat16)
    full_bias = jnp.concatenate(
        [qv_bias[:model_width], jnp.zeros((model_width,), jnp.float32), qv_bias[model_width:]]
    )
    projected = (
        jnp.dot(first_low, qkv_weight, preferred_element_type=jnp.float32) + full_bias
    ).astype(jnp.bfloat16)
    queries = split_heads(projected[:, :model_width], row_count)
    key_rows = split_heads(projected[:, model_width : 2 * model_width], row_count)
    value_rows = split_heads(projected[:, 2 * model_width :], row_count)
    scores = masked_scores(queries, key_rows, allowed)
    highest = jnp.max(scores, axis=-1, keepdims=True)
    log_total = highest + jnp.log(jnp.sum(jnp.exp(scores - highest), axis=-1, keepdims=True))
    probs_low = jnp.exp(scores - log_total).astype(jnp.bfloat16)
    attended = jnp.einsum("hqk,khd->qhd", probs_low, value_rows, preferred_element_type=jnp.float32)
    attended = attended.reshape(row_count, model_width).astype(jnp.bfloat16)
    middle = hidden + (jnp.dot(attended, out_weight, preferred_element_type=jnp.float32) + out_bias)
    second_in, normed_two, inverse_two = layer_norm(middle, second_gain, second_shift)
    second_low = second_in.astype(jnp.bfloat16)
    pre_act = jnp.dot(second_low, expand_weight, preferred_element_type=jnp.float32) + expand_bias
    activated = jax.nn.gelu(pre_act, approximate=True).astype(jnp.bfloat16)
    result = middle + (
        jnp.dot(activated, contract_weight, preferred_element_type=jnp.float32) + contract_bias
    )
    kept_state = (
        normed_one,
        inverse_one,
        first_low,
        projected,
        log_total,
        attended,
        normed_two,
        inverse_two,
        second_low,
        pre_act,
        activated,
    )
    return (result, kept_state)


def backward_layer(upstream, kept_state, allowed, weights):
    (
        first_gain,
        first_shift,
        qkv_weight,
        qv_bias,
        out_weight,
        out_bias,
        second_gain,
        second_shift,
        expand_weight,
        expand_bias,
        contract_weight,
        contract_bias,
    ) = weights
    (
        normed_one,
        inverse_one,
        first_low,
        projected,
        log_total,
        attended,
        normed_two,
        inverse_two,
        second_low,
        pre_act,
        activated,
    ) = kept_state
    row_count, model_width = upstream.shape
    grad_mlp = upstream.astype(jnp.bfloat16)
    grad_act = transpose_dot(grad_mlp, contract_weight)
    gelu_pull = jax.vjp(partial(jax.nn.gelu, approximate=True), pre_act)[1]
    grad_pre = gelu_pull(grad_act)[0].astype(jnp.bfloat16)
    grad_second = transpose_dot(grad_pre, expand_weight)
    grad_middle = upstream + norm_back(grad_second, normed_two, inverse_two, second_gain)
    grad_attn = grad_middle.astype(jnp.bfloat16)
    grad_attended = split_heads(
        transpose_dot(grad_attn, out_weight).astype(jnp.bfloat16), row_count
    )
    queries = split_heads(projected[:, :model_width], row_count)
    key_rows = split_heads(projected[:, model_width : 2 * model_width], row_count)
    value_rows = split_heads(projected[:, 2 * model_width :], row_count)
    probability = jnp.exp(masked_scores(queries, key_rows, allowed) - log_total)
    probs_low = probability.astype(jnp.bfloat16)
    grad_probs = jnp.einsum(
        "qhd,khd->hqk", grad_attended, value_rows, preferred_element_type=jnp.float32
    )
    grad_scores = probability * (
        grad_probs - jnp.sum(probability * grad_probs, axis=-1, keepdims=True)
    )
    grad_scores = grad_scores.astype(jnp.bfloat16)
    grad_queries = (
        jnp.einsum("hqk,khd->qhd", grad_scores, key_rows, preferred_element_type=jnp.float32)
        * SCORE_SCALE
    )
    grad_keys = (
        jnp.einsum("hqk,qhd->khd", grad_scores, queries, preferred_element_type=jnp.float32)
        * SCORE_SCALE
    )
    grad_values = jnp.einsum(
        "hqk,qhd->khd", probs_low, grad_attended, preferred_element_type=jnp.float32
    )
    grad_proj = jnp.concatenate(
        [
            grad_queries.reshape(row_count, model_width),
            grad_keys.reshape(row_count, model_width),
            grad_values.reshape(row_count, model_width),
        ],
        axis=1,
    ).astype(jnp.bfloat16)
    grad_first = transpose_dot(grad_proj, qkv_weight)
    grad_input = grad_middle + norm_back(grad_first, normed_one, inverse_one, first_gain)
    proj_sums = jnp.sum(grad_proj, axis=0, dtype=jnp.float32)
    small_grads = (
        jnp.sum(grad_first * normed_one, axis=0),
        jnp.sum(grad_first, axis=0),
        jnp.concatenate([proj_sums[:model_width], proj_sums[2 * model_width :]]),
        jnp.sum(grad_attn, axis=0, dtype=jnp.float32),
        jnp.sum(grad_second * normed_two, axis=0),
        jnp.sum(grad_second, axis=0),
        jnp.sum(grad_pre, axis=0, dtype=jnp.float32),
        jnp.sum(grad_mlp, axis=0, dtype=jnp.float32),
    )
    operands = (
        first_low,
        grad_proj,
        attended,
        grad_attn,
        second_low,
        grad_pre,
        activated,
        grad_mlp,
    )
    return (grad_input, small_grads, operands)


def zeros_of(leading, shape_rest, kind):
    return jnp.zeros(tuple(leading) + tuple(shape_rest), kind)


def kept_blank(leading, row_count, model_width, ff_width):
    single = jnp.float32
    half = jnp.bfloat16
    return (
        zeros_of(leading, (row_count, model_width), single),
        zeros_of(leading, (row_count, 1), single),
        zeros_of(leading, (row_count, model_width), half),
        zeros_of(leading, (row_count, 3 * model_width), half),
        zeros_of(leading, (HEADS, row_count, 1), single),
        zeros_of(leading, (row_count, model_width), half),
        zeros_of(leading, (row_count, model_width), single),
        zeros_of(leading, (row_count, 1), single),
        zeros_of(leading, (row_count, model_width), half),
        zeros_of(leading, (row_count, ff_width), single),
        zeros_of(leading, (row_count, ff_width), half),
    )


def stored_blank(leading, row_count, model_width, ff_width):
    return keep_for_back(
        zeros_of(leading, (row_count, model_width), jnp.float32),
        kept_blank(leading, row_count, model_width, ff_width),
    )


def small_blank(model_width, ff_width):
    return (
        jnp.zeros((model_width,), jnp.float32),
        jnp.zeros((model_width,), jnp.float32),
        jnp.zeros((2 * model_width,), jnp.float32),
        jnp.zeros((model_width,), jnp.float32),
        jnp.zeros((model_width,), jnp.float32),
        jnp.zeros((model_width,), jnp.float32),
        jnp.zeros((ff_width,), jnp.float32),
        jnp.zeros((model_width,), jnp.float32),
    )


def operand_blank(leading, row_count, model_width, ff_width):
    half = jnp.bfloat16
    return (
        zeros_of(leading, (row_count, model_width), half),
        zeros_of(leading, (row_count, 3 * model_width), half),
        zeros_of(leading, (row_count, model_width), half),
        zeros_of(leading, (row_count, model_width), half),
        zeros_of(leading, (row_count, model_width), half),
        zeros_of(leading, (row_count, ff_width), half),
        zeros_of(leading, (row_count, ff_width), half),
        zeros_of(leading, (row_count, model_width), half),
    )


def keep_for_back(layer_input, kept_state):
    return (layer_input, kept_state)


def recover_state(stored):
    return stored[1]


def store_at(stack, item, index_value, keep_old, spare_slot):
    target = jnp.where(keep_old, spare_slot, index_value)
    return jax.tree.map(
        lambda whole, member: lax.dynamic_update_index_in_dim(whole, member, target, 0), stack, item
    )


def weight_grads(small_total, operand_stack):
    flattened = [member.reshape(-1, member.shape[-1]) for member in operand_stack]
    return (
        small_total[0],
        small_total[1],
        column_outer(flattened[0], flattened[1]),
        small_total[2],
        column_outer(flattened[2], flattened[3]),
        small_total[3],
        small_total[4],
        small_total[5],
        column_outer(flattened[4], flattened[5]),
        small_total[6],
        column_outer(flattened[6], flattened[7]),
        small_total[7],
    )


def relay_layers(
    all_tokens, all_cotangent, allowed_all, weights, section_count, section_index, ff_width
):
    micro_count, row_count, model_width = all_tokens.shape
    slot_total = micro_count + 1

    def run_layer(layer_input, allowed):
        result, kept_state = forward_layer(layer_input, allowed, weights)
        return (result, keep_for_back(layer_input, kept_state))

    def skip_layer(layer_input, allowed):
        return (
            jnp.zeros((row_count, model_width), jnp.float32),
            stored_blank((), row_count, model_width, ff_width),
        )

    def forward_turn(turn_index, carry):
        outgoing, stash_now, finals = carry
        incoming = from_behind(outgoing, "section", 1)
        micro_index = turn_index - section_index
        active = (micro_index >= 0) & (micro_index < micro_count)
        slot_index = jnp.clip(micro_index, 0, micro_count - 1)
        layer_input = jnp.where(section_index == 0, all_tokens[slot_index], incoming).astype(
            jnp.float32
        )
        result, stored = lax.cond(
            active, run_layer, skip_layer, layer_input, allowed_all[slot_index]
        )
        stash_now = store_at(stash_now, stored, slot_index, jnp.logical_not(active), micro_count)
        is_last = active & (section_index == section_count - 1)
        finals = store_at(finals, result, slot_index, jnp.logical_not(is_last), micro_count)
        return (result.astype(jnp.bfloat16), stash_now, finals)

    turn_count = micro_count + section_count - 1
    finals_blank = jnp.zeros((slot_total, row_count, model_width), jnp.float32)
    firsts_blank = jnp.zeros((slot_total, row_count, model_width), jnp.float32)
    initial = (
        jnp.zeros((row_count, model_width), jnp.bfloat16),
        stored_blank((slot_total,), row_count, model_width, ff_width),
        finals_blank,
    )
    outgoing, stash, finals = lax.fori_loop(0, turn_count, forward_turn, initial)

    def run_back(upstream, stored, allowed):
        return backward_layer(upstream, recover_state(stored), allowed, weights)

    def skip_back(upstream, stored, allowed):
        return (
            jnp.zeros((row_count, model_width), jnp.float32),
            small_blank(model_width, ff_width),
            operand_blank((), row_count, model_width, ff_width),
        )

    def backward_turn(turn_index, carry):
        outgoing_grad, small_total, operand_stack, grads_first = carry
        incoming = from_behind(outgoing_grad, "section", -1)
        micro_index = turn_index - (section_count - 1 - section_index)
        active = (micro_index >= 0) & (micro_index < micro_count)
        slot_index = jnp.clip(micro_index, 0, micro_count - 1)
        upstream = jnp.where(
            section_index == section_count - 1, all_cotangent[slot_index], incoming
        ).astype(jnp.float32)
        stored = jax.tree.map(lambda whole: whole[slot_index], stash)
        grad_input, small_grads, operands = lax.cond(
            active, run_back, skip_back, upstream, stored, allowed_all[slot_index]
        )
        small_total = jax.tree.map(jnp.add, small_total, small_grads)
        operand_stack = store_at(
            operand_stack, operands, slot_index, jnp.logical_not(active), micro_count
        )
        is_first = active & (section_index == 0)
        grads_first = store_at(
            grads_first, grad_input, slot_index, jnp.logical_not(is_first), micro_count
        )
        return (grad_input.astype(jnp.bfloat16), small_total, operand_stack, grads_first)

    initial = (
        jnp.zeros((row_count, model_width), jnp.bfloat16),
        small_blank(model_width, ff_width),
        operand_blank((slot_total,), row_count, model_width, ff_width),
        firsts_blank,
    )
    outgoing, small_total, operand_stack, grads_first = lax.fori_loop(
        0, turn_count, backward_turn, initial
    )
    return (finals[:micro_count], grads_first[:micro_count], small_total, operand_stack)


def body(
    tokens,
    lengths,
    cotangent,
    first_gain,
    first_shift,
    qkv_weight,
    qv_bias,
    out_weight,
    out_bias,
    second_gain,
    second_shift,
    expand_weight,
    expand_bias,
    contract_weight,
    contract_bias,
):
    weights = (
        first_gain,
        first_shift,
        qkv_weight,
        qv_bias,
        out_weight,
        out_bias,
        second_gain,
        second_shift,
        expand_weight,
        expand_bias,
        contract_weight,
        contract_bias,
    )
    ff_width = expand_weight.shape[1]
    section_count = lax.axis_size("section")
    section_index = lax.axis_index("section")
    whole_tokens, whole_cotangent = (
        lax.all_gather(tokens, "section", axis=2, tiled=True),
        lax.all_gather(cotangent, "section", axis=2, tiled=True),
    )
    all_tokens = whole_tokens[:, 0]
    all_cotangent = whole_cotangent[:, 0]
    row_count = all_tokens.shape[1]
    allowed_all = jax.vmap(lambda length_row: allowed_from(length_row, row_count))(lengths[:, 0])
    finals, grads_first, small_total, operand_stack = relay_layers(
        all_tokens, all_cotangent, allowed_all, weights, section_count, section_index, ff_width
    )
    final_sum, grad_sum = (
        lax.psum_scatter(
            finals[:, None].astype(jnp.bfloat16), "section", scatter_dimension=2, tiled=True
        ).astype(jnp.float32),
        lax.psum_scatter(
            grads_first[:, None].astype(jnp.bfloat16), "section", scatter_dimension=2, tiled=True
        ).astype(jnp.float32),
    )
    result_out = final_sum.astype(jnp.bfloat16)
    grads = weight_grads(small_total, operand_stack)
    shards = (
        lax.psum_scatter(
            grads[0].astype(jnp.bfloat16), "dp", scatter_dimension=0, tiled=True
        ).astype(jnp.float32),
        lax.psum_scatter(
            grads[1].astype(jnp.bfloat16), "dp", scatter_dimension=0, tiled=True
        ).astype(jnp.float32),
        lax.psum_scatter(
            grads[2].astype(jnp.bfloat16), "dp", scatter_dimension=0, tiled=True
        ).astype(jnp.float32),
        lax.psum_scatter(
            grads[3].astype(jnp.bfloat16), "dp", scatter_dimension=0, tiled=True
        ).astype(jnp.float32),
        lax.psum_scatter(
            grads[4].astype(jnp.bfloat16), "dp", scatter_dimension=0, tiled=True
        ).astype(jnp.float32),
        lax.psum_scatter(
            grads[5].astype(jnp.bfloat16), "dp", scatter_dimension=0, tiled=True
        ).astype(jnp.float32),
        lax.psum_scatter(
            grads[6].astype(jnp.bfloat16), "dp", scatter_dimension=0, tiled=True
        ).astype(jnp.float32),
        lax.psum_scatter(
            grads[7].astype(jnp.bfloat16), "dp", scatter_dimension=0, tiled=True
        ).astype(jnp.float32),
        lax.psum_scatter(
            grads[8].astype(jnp.bfloat16), "dp", scatter_dimension=0, tiled=True
        ).astype(jnp.float32),
        lax.psum_scatter(
            grads[9].astype(jnp.bfloat16), "dp", scatter_dimension=0, tiled=True
        ).astype(jnp.float32),
        lax.psum_scatter(
            grads[10].astype(jnp.bfloat16), "dp", scatter_dimension=0, tiled=True
        ).astype(jnp.float32),
        lax.psum_scatter(
            grads[11].astype(jnp.bfloat16), "dp", scatter_dimension=0, tiled=True
        ).astype(jnp.float32),
    )
    totals = (
        lax.psum(shards[0].astype(jnp.bfloat16), "section").astype(jnp.float32),
        lax.psum(shards[1].astype(jnp.bfloat16), "section").astype(jnp.float32),
        lax.psum(shards[2].astype(jnp.bfloat16), "section").astype(jnp.float32),
        lax.psum(shards[3].astype(jnp.bfloat16), "section").astype(jnp.float32),
        lax.psum(shards[4].astype(jnp.bfloat16), "section").astype(jnp.float32),
        lax.psum(shards[5].astype(jnp.bfloat16), "section").astype(jnp.float32),
        lax.psum(shards[6].astype(jnp.bfloat16), "section").astype(jnp.float32),
        lax.psum(shards[7].astype(jnp.bfloat16), "section").astype(jnp.float32),
        lax.psum(shards[8].astype(jnp.bfloat16), "section").astype(jnp.float32),
        lax.psum(shards[9].astype(jnp.bfloat16), "section").astype(jnp.float32),
        lax.psum(shards[10].astype(jnp.bfloat16), "section").astype(jnp.float32),
        lax.psum(shards[11].astype(jnp.bfloat16), "section").astype(jnp.float32),
    )
    return (result_out, grad_sum) + tuple(totals)


def solution(mesh):
    placed = (
        P(None, "dp", "section", None),
        P(None, "dp", None),
        P(None, "dp", "section", None),
        P(),
        P(),
        P(),
        P(),
        P(),
        P(),
        P(),
        P(),
        P(),
        P(),
        P(),
        P(),
    )
    return jax.shard_map(
        body,
        mesh=mesh,
        in_specs=placed,
        out_specs=(
            P(None, "dp", "section", None),
            P(None, "dp", "section", None),
            P("dp"),
            P("dp"),
            P("dp", None),
            P("dp"),
            P("dp", None),
            P("dp"),
            P("dp"),
            P("dp"),
            P("dp", None),
            P("dp"),
            P("dp", None),
            P("dp"),
        ),
        check_vma=False,
    )
```

profile of v0, /device:TPU:0, one launch (start us, length us, event | category | flops | bytes accessed | tf_op | source)
XLA Modules:
  0.0 1597.5 jit_solution(12136220271906748592)
XLA Ops:
  8.5 36.0 %all_gather.6 = bf16[4,1,128,768]{3,2,0,1:T(8,128)(2,1)} all-gather(bf16[4,1,16,768]{3,2,0,1:T(8,128)(2,1)S(1)} %bitcast.188), channel_id=1, replica_groups=mesh['section'=8,'dp'=4] {'section'}, dimensions={2}, use_global_device_ids=true | all-gather | bytes 884736 | tf_op jit(solution)/shard_map/all_gather | solution.py:435
  45.4 34.0 %all_gather.7 = bf16[4,1,128,768]{3,2,0,1:T(8,128)(2,1)} all-gather(bf16[4,1,16,768]{3,2,0,1:T(8,128)(2,1)S(1)} %bitcast.189), channel_id=1, replica_groups=mesh['section'=8,'dp'=4] {'section'}, dimensions={2}, use_global_device_ids=true | all-gather | bytes 884736 | tf_op jit(solution)/shard_map/all_gather | solution.py:436
  96.3 403.4 %while.89 = (s32[]{:T(128)}, bf16[128,768]{1,0:T(8,128)(2,1)}, f32[5,128,768]{2,1,0:T(8,128)}, f32[5,128,1]{1,2,0:T(1,128)}, bf16[5,128,768]{2,1,0:T(8,128)(2,1)...) while((s32[]{:T(128)}, bf16[128,768]{1,0:T(8,128)(2,1)}, ...), condition=%wide.region_11.12_spmd.clone, body=%wide.region_2.11_spmd.clone.sunk | while | flops 1875283200 | bytes 74465464 | solution.py:353
  104.6 19.2 %conditional.6 = (bf16[128,768]{1,0:T(8,128)(2,1)}, f32[1,128,768]{2,1,0:T(8,128)S(1)}, f32[1,128,768]{2,1,0:T(8,128)}, f32[1,128,1]{1,2,0:T(1,128)}, bf16[1,128...) conditional(s32[]{:T(128)} %convert_element_type.377, ...), branch_computations={%region_3.3_spmd, %region_4.10_spmd} | conditional | flops 1875086592 | bytes 57144800 | solution.py:337
  143.7 19.2 %conditional.6 = (bf16[128,768]{1,0:T(8,128)(2,1)}, f32[1,128,768]{2,1,0:T(8,128)S(1)}, f32[1,128,768]{2,1,0:T(8,128)}, f32[1,128,1]{1,2,0:T(1,128)}, bf16[1,128...) conditional(s32[]{:T(128)} %convert_element_type.377, ...), branch_computations={%region_3.3_spmd, %region_4.10_spmd} | conditional | flops 1875086592 | bytes 57144800 | solution.py:337
  185.7 19.2 %conditional.6 = (bf16[128,768]{1,0:T(8,128)(2,1)}, f32[1,128,768]{2,1,0:T(8,128)S(1)}, f32[1,128,768]{2,1,0:T(8,128)}, f32[1,128,1]{1,2,0:T(1,128)}, bf16[1,128...) conditional(s32[]{:T(128)} %convert_element_type.377, ...), branch_computations={%region_3.3_spmd, %region_4.10_spmd} | conditional | flops 1875086592 | bytes 57144800 | solution.py:337
  227.7 19.2 %conditional.6 = (bf16[128,768]{1,0:T(8,128)(2,1)}, f32[1,128,768]{2,1,0:T(8,128)S(1)}, f32[1,128,768]{2,1,0:T(8,128)}, f32[1,128,1]{1,2,0:T(1,128)}, bf16[1,128...) conditional(s32[]{:T(128)} %convert_element_type.377, ...), branch_computations={%region_3.3_spmd, %region_4.10_spmd} | conditional | flops 1875086592 | bytes 57144800 | solution.py:337
  289.1 18.2 %collective-permute-start = (bf16[128,768]{1,0:T(8,128)(2,1)}, bf16[128,768]{1,0:T(8,128)(2,1)S(1)}, u32[]{:S(2)}, u32[]{:S(2)}) collective-permute-start(bf16[128,768]{1,0:T(8,128)(2,1)} %get-tuple-element.3475), channel_id=1, source_target_pairs={{0,4},{4,8},{8,12},{12,16},{16,20},{20,24},{24,28},{1,5},{5,9},{9,... | collective-permute-start | bytes 589832 | tf_op jit(solution)/shard_map/while/body/eval_jaxpr/ppermute | solution.py:20
  359.6 19.1 %collective-permute-start = (bf16[128,768]{1,0:T(8,128)(2,1)}, bf16[128,768]{1,0:T(8,128)(2,1)S(1)}, u32[]{:S(2)}, u32[]{:S(2)}) collective-permute-start(bf16[128,768]{1,0:T(8,128)(2,1)} %get-tuple-element.3475), channel_id=1, source_target_pairs={{0,4},{4,8},{8,12},{12,16},{16,20},{20,24},{24,28},{1,5},{5,9},{9,... | collective-permute-start | bytes 589832 | tf_op jit(solution)/shard_map/while/body/eval_jaxpr/ppermute | solution.py:20
  431.8 14.9 collective-permute-start
  512.4 631.9 %while.90 = (s32[]{:T(128)}, bf16[128,768]{1,0:T(8,128)(2,1)}, f32[768]{0:T(1024)}, f32[768]{0:T(1024)}, f32[1536]{0:T(1024)}, /*index=5*/f32[768]{0:T(1024)}, f...) while((s32[]{:T(128)}, bf16[128,768]{1,0:T(8,128)(2,1)}, ...), condition=%wide.region_29.30_spmd.clone, body=%wide.region_13.29_spmd.clone.sunk | while | flops 1958158592 | bytes 87609424 | solution.py:394
  513.8 18.4 %collective-permute-done.1 = bf16[128,768]{1,0:T(8,128)(2,1)S(1)} collective-permute-done((bf16[128,768]{1,0:T(8,128)(2,1)}, bf16[128,768]{1,0:T(8,128)(2,1)S(1)}, u32[]{:S(2)}, u32[]{:S(2)}) %collective-permute-start.1) | collective-permute-done | bytes 196640 | tf_op jit(solution)/shard_map/while/body/eval_jaxpr/ppermute | solution.py:20
  533.1 9.2 conditional.7
  557.5 7.7 collective-permute-done.1
  566.2 9.2 conditional.7
  590.8 17.5 %collective-permute-done.1 = bf16[128,768]{1,0:T(8,128)(2,1)S(1)} collective-permute-done((bf16[128,768]{1,0:T(8,128)(2,1)}, bf16[128,768]{1,0:T(8,128)(2,1)S(1)}, u32[]{:S(2)}, u32[]{:S(2)}) %collective-permute-start.1) | collective-permute-done | bytes 196640 | tf_op jit(solution)/shard_map/while/body/eval_jaxpr/ppermute | solution.py:20
  609.2 9.2 conditional.7
  633.8 7.7 collective-permute-done.1
  642.4 9.2 conditional.7
  667.0 18.4 %collective-permute-done.1 = bf16[128,768]{1,0:T(8,128)(2,1)S(1)} collective-permute-done((bf16[128,768]{1,0:T(8,128)(2,1)}, bf16[128,768]{1,0:T(8,128)(2,1)S(1)}, u32[]{:S(2)}, u32[]{:S(2)}) %collective-permute-start.1) | collective-permute-done | bytes 196640 | tf_op jit(solution)/shard_map/while/body/eval_jaxpr/ppermute | solution.py:20
  686.3 9.2 conditional.7
  710.9 7.7 collective-permute-done.1
  719.5 9.2 conditional.7
  744.1 16.8 %collective-permute-done.1 = bf16[128,768]{1,0:T(8,128)(2,1)S(1)} collective-permute-done((bf16[128,768]{1,0:T(8,128)(2,1)}, bf16[128,768]{1,0:T(8,128)(2,1)S(1)}, u32[]{:S(2)}, u32[]{:S(2)}) %collective-permute-start.1) | collective-permute-done | bytes 196640 | tf_op jit(solution)/shard_map/while/body/eval_jaxpr/ppermute | solution.py:20
  761.9 9.2 conditional.7
  786.5 150.9 %collective-permute-done.1 = bf16[128,768]{1,0:T(8,128)(2,1)S(1)} collective-permute-done((bf16[128,768]{1,0:T(8,128)(2,1)}, bf16[128,768]{1,0:T(8,128)(2,1)S(1)}, u32[]{:S(2)}, u32[]{:S(2)}) %collective-permute-start.1) | collective-permute-done | bytes 196640 | tf_op jit(solution)/shard_map/while/body/eval_jaxpr/ppermute | solution.py:20
  938.3 30.2 %conditional.7 = (f32[768]{0:T(1024)}, f32[768]{0:T(1024)}, f32[1536]{0:T(1024)}, f32[768]{0:T(1024)}, f32[768]{0:T(1024)}, /*index=5*/f32[768]{0:T(1024)}, f32[...) conditional(s32[]{:T(128)} %convert_element_type.379, ...), branch_computations={%region_14.14_spmd, %region_15.28_spmd} | conditional | flops 1957943552 | bytes 79240576 | solution.py:375
  938.4 5.5 convert_reduce_fusion
  984.0 7.3 collective-permute-done.1
  992.2 30.2 %conditional.7 = (f32[768]{0:T(1024)}, f32[768]{0:T(1024)}, f32[1536]{0:T(1024)}, f32[768]{0:T(1024)}, f32[768]{0:T(1024)}, /*index=5*/f32[768]{0:T(1024)}, f32[...) conditional(s32[]{:T(128)} %convert_element_type.379, ...), branch_computations={%region_14.14_spmd, %region_15.28_spmd} | conditional | flops 1957943552 | bytes 79240576 | solution.py:375
  992.3 5.5 convert_reduce_fusion
  1037.8 7.4 collective-permute-done.1
  1046.1 30.2 %conditional.7 = (f32[768]{0:T(1024)}, f32[768]{0:T(1024)}, f32[1536]{0:T(1024)}, f32[768]{0:T(1024)}, f32[768]{0:T(1024)}, /*index=5*/f32[768]{0:T(1024)}, f32[...) conditional(s32[]{:T(128)} %convert_element_type.379, ...), branch_computations={%region_14.14_spmd, %region_15.28_spmd} | conditional | flops 1957943552 | bytes 79240576 | solution.py:375
  1046.2 5.5 convert_reduce_fusion
  1091.8 7.3 collective-permute-done.1
  1100.0 30.3 %conditional.7 = (f32[768]{0:T(1024)}, f32[768]{0:T(1024)}, f32[1536]{0:T(1024)}, f32[768]{0:T(1024)}, f32[768]{0:T(1024)}, /*index=5*/f32[768]{0:T(1024)}, f32[...) conditional(s32[]{:T(128)} %convert_element_type.379, ...), branch_computations={%region_14.14_spmd, %region_15.28_spmd} | conditional | flops 1957943552 | bytes 79240576 | solution.py:375
  1100.1 5.5 convert_reduce_fusion
  1148.1 6.3 bitcast_convert_fusion.2
  1155.6 7.6 bitcast_convert_fusion.1
  1164.5 7.7 bitcast_convert_fusion
  1174.5 39.8 %reduce-scatter.11.cloned.1.call-done = bf16[192,2304]{1,0:T(8,128)(2,1)} async-done(((bf16[768,2304]{1,0:T(8,128)(2,1)}), bf16[192,2304]{1,0:T(8,128)(2,1)}) %reduce-scatter.11.cloned.1.call-update) | async-done | bytes 884752 | tf_op jit(solution)/shard_map/reduce_scatter | solution.py:462
  1214.3 50.4 %reduce-scatter.15.cloned.1.call-done = bf16[192,3072]{1,0:T(8,128)(2,1)} async-done(((bf16[768,3072]{1,0:T(8,128)(2,1)}), bf16[192,3072]{1,0:T(8,128)(2,1)}) %reduce-scatter.15.cloned.1.call-update) | async-done | bytes 1179664 | tf_op jit(solution)/shard_map/reduce_scatter | solution.py:480
  1264.7 50.4 %reduce-scatter.17.cloned.1.call-done = bf16[768,768]{1,0:T(8,128)(2,1)} async-done(((bf16[3072,768]{1,0:T(8,128)(2,1)}), bf16[768,768]{1,0:T(8,128)(2,1)}) %reduce-scatter.17.cloned.1.call-update) | async-done | bytes 1179664 | tf_op jit(solution)/shard_map/reduce_scatter | solution.py:486
  1317.7 10.3 all-reduce.10
  1329.9 21.8 %all-reduce.8 = (bf16[192]{0:T(256)(128)(2,1)S(1)}, bf16[192]{0:T(256)(128)(2,1)S(1)}, bf16[384]{0:T(512)(128)(2,1)S(1)}, bf16[192]{0:T(256)(128)(2,1)S(1)}, bf1...) all-reduce(bf16[192]{0:T(256)(128)(2,1)S(1)} %dynamic-slice.1, ...), channel_id=1, replica_groups=mesh['section'=8,'dp'=4] {'section'}, use_global_device_ids=true, to_apply=%region_32.33 | all-reduce | flops 2304 | bytes 9216 | tf_op jit(solution)/shard_map/psum | solution.py:494
  1356.3 25.2 %reduce-scatter.9.cloned.1.call-done = bf16[4,1,16,768]{3,2,1,0:T(8,128)(2,1)} async-done(((bf16[4,1,128,768]{3,2,1,0:T(8,128)(2,1)}), bf16[4,1,16,768]{3,2,1,0:T(8,128)(2,1)}) %reduce-scatter.9.cloned.1.call-update) | async-done | bytes 98320 | tf_op jit(solution)/shard_map/reduce_scatter | solution.py:449
  1383.0 142.3 %all-reduce.13.cloned.1.call-done = (bf16[192,2304]{1,0:T(8,128)(2,1)}, bf16[192,768]{1,0:T(8,128)(2,1)}, bf16[192,3072]{1,0:T(8,128)(2,1)}, bf16[768,768]{1,0:T(8,128)(2,1)}) async-done(((bf16[192,2304]{1,0:T(8,128)(2,1)}, bf16[192,768]{1,0:T(8,128)(2,1)}, bf16[192,3072]{1,0:T(8,128)(2,1)}, bf16[768,768]{1,0:T(8,128)(2,1)}), (bf16[192,2304]{1,0:T(8,128)(2,1)}, bf16[192,768]{1,0:T(8,128)(2,1)}, ...) | async-done | bytes 3538960 | tf_op jit(solution)/shard_map/psum | solution.py:496
  1532.0 58.7 %reduce-scatter.7.cloned.1.call-done = bf16[4,1,16,768]{3,2,1,0:T(8,128)(2,1)} async-done(((bf16[4,1,128,768]{3,2,1,0:T(8,128)(2,1)}), bf16[4,1,16,768]{3,2,1,0:T(8,128)(2,1)}) %reduce-scatter.7.cloned.1.call-update) | async-done | bytes 98320 | tf_op jit(solution)/shard_map/reduce_scatter | solution.py:446
  (1109 shorter events, 784.0 us)
Async XLA Ops:
  7.2 37.3 %copy-start.43 = (s32[4,1,4]{2,1,0:T(1,128)S(1)}, s32[4,1,4]{2,1,0:T(1,128)}, u32[]{:S(2)}) copy-start(s32[4,1,4]{2,1,0:T(1,128)} %param.24) | copy-start | bytes 196
  7.2 38.2 %copy-start.40 = (bf16[4,1,16,768]{3,2,1,0:T(8,128)(2,1)S(1)}, bf16[4,1,16,768]{3,2,1,0:T(8,128)(2,1)}, u32[]{:S(2)}) copy-start(bf16[4,1,16,768]{3,2,1,0:T(8,128)(2,1)} %param.25) | copy-start | bytes 294916
  7.2 1167.2 %reduce-scatter.13.cloned.1.call-start = ((), (), s32[]{:S(2)}) async-start(), calls=%async_computation.9 | async-start | bytes 1474560 | tf_op jit(solution)/shard_map/reduce_scatter | solution.py:468
  7.3 80.9 %copy-start.14 = (bf16[5,128,768]{2,1,0:T(8,128)(2,1)}, bf16[5,128,768]{2,1,0:T(8,128)(2,1)S(1)}, u32[]{:S(2)}) copy-start(bf16[5,128,768]{2,1,0:T(8,128)(2,1)S(1)} %fusion.71) | copy-start | bytes 2949124
  96.3 7.4 collective-permute-start
  112.3 7.8 copy-start.8
  130.4 4.9 copy-start.13
  137.9 4.8 collective-permute-start
  151.3 7.8 copy-start.8
  176.9 7.8 collective-permute-start
  193.3 7.8 copy-start.8
  211.4 4.9 copy-start.13
  218.9 7.8 collective-permute-start
  235.3 7.8 copy-start.8
  253.4 5.0 copy-start.13
  261.0 7.6 collective-permute-start
  289.1 21.7 %collective-permute-start = (bf16[128,768]{1,0:T(8,128)(2,1)}, bf16[128,768]{1,0:T(8,128)(2,1)S(1)}, u32[]{:S(2)}, u32[]{:S(2)}) collective-permute-start(bf16[128,768]{1,0:T(8,128)(2,1)} %get-tuple-element.3475), channel_id=1, source_target_pairs={{0,4},{4,8},{8,12},{12,16},{16,20},{20,24},{24,28},{1,5},{5,9},{9,... | collective-permute-start | bytes 589832 | tf_op jit(solution)/shard_map/while/body/eval_jaxpr/ppermute | solution.py:20
  331.2 8.0 collective-permute-start
  359.6 22.6 %collective-permute-start = (bf16[128,768]{1,0:T(8,128)(2,1)}, bf16[128,768]{1,0:T(8,128)(2,1)S(1)}, u32[]{:S(2)}, u32[]{:S(2)}) collective-permute-start(bf16[128,768]{1,0:T(8,128)(2,1)} %get-tuple-element.3475), channel_id=1, source_target_pairs={{0,4},{4,8},{8,12},{12,16},{16,20},{20,24},{24,28},{1,5},{5,9},{9,... | collective-permute-start | bytes 589832 | tf_op jit(solution)/shard_map/while/body/eval_jaxpr/ppermute | solution.py:20
  402.7 8.7 collective-permute-start
  431.8 18.4 %collective-permute-start = (bf16[128,768]{1,0:T(8,128)(2,1)}, bf16[128,768]{1,0:T(8,128)(2,1)S(1)}, u32[]{:S(2)}, u32[]{:S(2)}) collective-permute-start(bf16[128,768]{1,0:T(8,128)(2,1)} %get-tuple-element.3475), channel_id=1, source_target_pairs={{0,4},{4,8},{8,12},{12,16},{16,20},{20,24},{24,28},{1,5},{5,9},{9,... | collective-permute-start | bytes 589832 | tf_op jit(solution)/shard_map/while/body/eval_jaxpr/ppermute | solution.py:20
  470.6 8.7 collective-permute-start
  512.4 19.7 %collective-permute-start.1 = (bf16[128,768]{1,0:T(8,128)(2,1)}, bf16[128,768]{1,0:T(8,128)(2,1)S(1)}, u32[]{:S(2)}, u32[]{:S(2)}) collective-permute-start(bf16[128,768]{1,0:T(8,128)(2,1)} %get-tuple-element.3593), channel_id=1, source_target_pairs={{4,0},{8,4},{12,8},{16,12},{20,16},{24,20},{28,24},{5,1},{9,5},{13... | collective-permute-start | bytes 589832 | tf_op jit(solution)/shard_map/while/body/eval_jaxpr/ppermute | solution.py:20
  556.2 9.0 collective-permute-start.1
  589.5 18.8 %collective-permute-start.1 = (bf16[128,768]{1,0:T(8,128)(2,1)}, bf16[128,768]{1,0:T(8,128)(2,1)S(1)}, u32[]{:S(2)}, u32[]{:S(2)}) collective-permute-start(bf16[128,768]{1,0:T(8,128)(2,1)} %get-tuple-element.3593), channel_id=1, source_target_pairs={{4,0},{8,4},{12,8},{16,12},{20,16},{24,20},{28,24},{5,1},{9,5},{13... | collective-permute-start | bytes 589832 | tf_op jit(solution)/shard_map/while/body/eval_jaxpr/ppermute | solution.py:20
  632.4 9.0 collective-permute-start.1
  665.7 19.7 %collective-permute-start.1 = (bf16[128,768]{1,0:T(8,128)(2,1)}, bf16[128,768]{1,0:T(8,128)(2,1)S(1)}, u32[]{:S(2)}, u32[]{:S(2)}) collective-permute-start(bf16[128,768]{1,0:T(8,128)(2,1)} %get-tuple-element.3593), channel_id=1, source_target_pairs={{4,0},{8,4},{12,8},{16,12},{20,16},{24,20},{28,24},{5,1},{9,5},{13... | collective-permute-start | bytes 589832 | tf_op jit(solution)/shard_map/while/body/eval_jaxpr/ppermute | solution.py:20
  709.6 9.0 collective-permute-start.1
  742.8 18.2 %collective-permute-start.1 = (bf16[128,768]{1,0:T(8,128)(2,1)}, bf16[128,768]{1,0:T(8,128)(2,1)S(1)}, u32[]{:S(2)}, u32[]{:S(2)}) collective-permute-start(bf16[128,768]{1,0:T(8,128)(2,1)} %get-tuple-element.3593), channel_id=1, source_target_pairs={{4,0},{8,4},{12,8},{16,12},{20,16},{24,20},{28,24},{5,1},{9,5},{13... | collective-permute-start | bytes 589832 | tf_op jit(solution)/shard_map/while/body/eval_jaxpr/ppermute | solution.py:20
  785.2 152.2 %collective-permute-start.1 = (bf16[128,768]{1,0:T(8,128)(2,1)}, bf16[128,768]{1,0:T(8,128)(2,1)S(1)}, u32[]{:S(2)}, u32[]{:S(2)}) collective-permute-start(bf16[128,768]{1,0:T(8,128)(2,1)} %get-tuple-element.3593), channel_id=1, source_target_pairs={{4,0},{8,4},{12,8},{16,12},{20,16},{24,20},{28,24},{5,1},{9,5},{13... | collective-permute-start | bytes 589832 | tf_op jit(solution)/shard_map/while/body/eval_jaxpr/ppermute | solution.py:20
  938.3 5.6 copy-start.1
  938.4 5.6 copy-start.18
  982.7 8.6 collective-permute-start.1
  992.2 5.6 copy-start.1
  992.3 5.6 copy-start.18
  1036.5 8.7 collective-permute-start.1
  1046.2 5.6 copy-start.1
  1046.2 5.6 copy-start.18
  1090.4 8.6 collective-permute-start.1
  1100.0 5.6 copy-start.1
  1100.1 5.6 copy-start.18
  1148.0 66.3 %reduce-scatter.11.cloned.1.call-start = ((), (), s32[]{:S(2)}) async-start(), calls=%async_computation.8 | async-start | bytes 4423680 | tf_op jit(solution)/shard_map/reduce_scatter | solution.py:462
  1154.5 110.3 %reduce-scatter.15.cloned.1.call-start = ((), (), s32[]{:S(2)}) async-start(), calls=%async_computation.10 | async-start | bytes 5898240 | tf_op jit(solution)/shard_map/reduce_scatter | solution.py:480
  1163.3 151.8 %reduce-scatter.17.cloned.1.call-start = ((), (), s32[]{:S(2)}) async-start(), calls=%async_computation.11 | async-start | bytes 5898240 | tf_op jit(solution)/shard_map/reduce_scatter | solution.py:486
  1172.2 209.2 %reduce-scatter.9.cloned.1.call-start = ((), (), s32[]{:S(2)}) async-start(), calls=%async_computation.7 | async-start | bytes 884736 | tf_op jit(solution)/shard_map/reduce_scatter | solution.py:449
  1174.4 140.9 %copy-start.16 = (bf16[5,128,768]{2,1,0:T(8,128)(2,1)S(1)}, bf16[5,128,768]{2,1,0:T(8,128)(2,1)}, u32[]{:S(2)}) copy-start(bf16[5,128,768]{2,1,0:T(8,128)(2,1)} %get-tuple-element.1961) | copy-start | bytes 2949124
  1174.4 351.0 %all-reduce.13.cloned.1.call-start = ((), (), s32[]{:S(2)}) async-start(), calls=%async_computation.12 | async-start | bytes 7077888 | tf_op jit(solution)/shard_map/psum | solution.py:496
  1315.2 275.5 %reduce-scatter.7.cloned.1.call-start = ((), (), s32[]{:S(2)}) async-start(), calls=%async_computation.6 | async-start | bytes 884736 | tf_op jit(solution)/shard_map/reduce_scatter | solution.py:446
  (127 other events, 322.0 us)
Sparse Core Ops, SparseCore 0:
  1148.2 22.9 reduce-scatter.12
  1173.9 40.3 reduce-scatter.10
  1216.8 47.8 reduce-scatter.14
  1267.3 47.7 reduce-scatter.16
  1318.8 62.5 reduce-scatter.8
  1385.8 139.4 all-reduce.12
  1529.2 61.4 reduce-scatter.6
where the time goes:
time: 1610 us; the launch traced here: 1600 us
  waiting for transfers between devices  672 us (42%)
  local copies, waits for them, and re-layouts  420 us (26%)
  other arithmetic  156 us (10%)
  matrix products  129 us (8%)
  blocking collectives  102 us (6%)
  starting transfers between devices  99.3 us (6%)
  between operations  16.5 us (1%)
    ppermute x22, waiting for transfers between devices, from_behind(): return lax.ppermute(array, axis, pairs)  305 us
    dynamic_update_slice x176, local copies, waits for them, and re-layouts, store_at(): lax.dynamic_update_index_in_dim(whole, member, target, 0)  221 us
    psum x1, waiting for transfers between devices, body(): lax.psum(shards[2].astype(jnp.bfloat16), 'section').astype(jnp.float32)  142 us
    ppermute x22, starting transfers between devices, from_behind(): return lax.ppermute(array, axis, pairs)  99.1 us
    add x55, other arithmetic, backward_turn(): small_total = jax.tree.map(jnp.add, small_total, small_grads)  72.4 us
    another operation x93, local copies, waits for them, and re-layouts  67.9 us
    broadcast_in_dim x147, local copies, waits for them, and re-layouts, store_at(): lax.dynamic_update_index_in_dim(whole, member, target, 0)  59 us
    reduce_scatter x1, waiting for transfers between devices, body(): lax.psum_scatter(finals[:, None].astype(jnp.bfloat16), 'section', scatter...  58.7 us
  transfers between devices with their start and end apart: 29, of which 28 were waited for; matrix products, arithmetic and copies ran while one was open for 2% of the time, Pallas kernels for 0%

commit v1 on v0

v1 whole, which is shorter than its diff:
```python
from functools import partial

import jax
import jax.numpy as jnp
from jax import lax
from jax.experimental import pallas as pl
from jax.experimental.pallas import tpu as pltpu
from jax.sharding import PartitionSpec as P

HEAD_DIM = 64
EPSILON = 1e-05
SCORE_SCALE = 0.125
MASKED = -1e30
GELU_A = 0.7978845608028654
GELU_B = 0.044715
BF = jnp.bfloat16
F32 = jnp.float32
AXES = ("section", "dp")
VMEM_LIMIT = 60 * 2**20


def nn(left, right):
    return jnp.dot(left, right, preferred_element_type=F32)


def nt(left, right):
    return lax.dot_general(left, right, (((1,), (1,)), ((), ())), preferred_element_type=F32)


def tn(left, right):
    return lax.dot_general(left, right, (((0,), (0,)), ((), ())), preferred_element_type=F32)


def normed_of(values):
    center = values - jnp.mean(values, axis=-1, keepdims=True)
    inverse = lax.rsqrt(jnp.mean(center * center, axis=-1, keepdims=True) + EPSILON)
    return center * inverse, inverse


def norm_back(upstream, normed, inverse, gain_row):
    scaled = upstream * gain_row
    return inverse * (
        scaled
        - jnp.mean(scaled, axis=-1, keepdims=True)
        - normed * jnp.mean(scaled * normed, axis=-1, keepdims=True)
    )


def lane_split(pair):
    lane = lax.broadcasted_iota(jnp.int32, pair.shape, 1)
    zero = jnp.zeros_like(pair)
    return jnp.where(lane < HEAD_DIM, pair, zero), jnp.where(lane < HEAD_DIM, zero, pair)


def forward_kernel(
    ends_ref, x_ref, vec_ref, ebias_ref, qkvb_ref, wq_ref, wo_ref, we_ref, wc_ref,
    first_ref, n1_ref, proj_ref, probs_ref, att_ref, n2_ref, second_ref, slope_ref, act_ref,
    inv_ref, last_ref, h_scr, mask_scr,
):
    step = pl.program_id(0)
    rows, width = h_scr.shape
    pairs = width // 128
    ff = we_ref.shape[1]

    @pl.when(step == 0)
    def _():
        h_scr[...] = x_ref[...].astype(F32)
        query = lax.broadcasted_iota(jnp.int32, (rows, rows), 0)
        key = lax.broadcasted_iota(jnp.int32, (rows, rows), 1)
        own_q = jnp.zeros((rows, rows), jnp.int32)
        own_k = jnp.zeros((rows, rows), jnp.int32)
        for slot in range(ends_ref.shape[0]):
            end = ends_ref[slot]
            own_q += (query >= end).astype(jnp.int32)
            own_k += (key >= end).astype(jnp.int32)
        mask_scr[...] = ((own_q == own_k) & (key <= query)).astype(F32)

    h = h_scr[...]
    n1, inv1 = normed_of(h)
    first_low = (n1 * vec_ref[0:1, :] + vec_ref[1:2, :]).astype(BF)
    first_ref[0] = first_low
    n1_ref[0] = n1.astype(BF)
    proj = (nn(first_low, wq_ref[...]) + qkvb_ref[...]).astype(BF)
    proj_ref[0] = proj
    allowed = jnp.concatenate([mask_scr[...], mask_scr[...]], axis=0) > 0.5
    outs = []
    for p in range(pairs):
        q = proj[:, 128 * p : 128 * (p + 1)]
        k = proj[:, width + 128 * p : width + 128 * (p + 1)]
        v = proj[:, 2 * width + 128 * p : 2 * width + 128 * (p + 1)]
        scores = nt(jnp.concatenate(lane_split(q), axis=0), k) * SCORE_SCALE
        scores = jnp.where(allowed, scores, MASKED)
        highest = jnp.max(scores, axis=-1, keepdims=True)
        weight = jnp.exp(scores - highest)
        low = (weight / jnp.sum(weight, axis=-1, keepdims=True)).astype(BF)
        probs_ref[0, 2 * rows * p : 2 * rows * (p + 1), :] = low
        both = jnp.concatenate([low[:rows], low[rows:]], axis=1)
        outs.append(nn(both, jnp.concatenate(lane_split(v), axis=0)).astype(BF))
    attended = jnp.concatenate(outs, axis=1)
    att_ref[0] = attended
    middle = h + (nn(attended, wo_ref[...]) + vec_ref[2:3, :])
    n2, inv2 = normed_of(middle)
    second_low = (n2 * vec_ref[3:4, :] + vec_ref[4:5, :]).astype(BF)
    second_ref[0] = second_low
    n2_ref[0] = n2.astype(BF)
    inv_ref[0] = jnp.concatenate(
        [jnp.broadcast_to(inv1, (rows, 128)), jnp.broadcast_to(inv2, (rows, 128))], axis=1
    )
    total = middle + vec_ref[5:6, :]
    chunk = 1024
    for j in range(ff // chunk):
        cols = slice(chunk * j, chunk * (j + 1))
        pre = nn(second_low, we_ref[:, cols]) + ebias_ref[:, cols]
        square = pre * pre
        t = jnp.tanh(GELU_A * pre * (1.0 + GELU_B * square))
        half = 0.5 * (1.0 + t)
        act = (pre * half).astype(BF)
        slope = half + 0.5 * GELU_A * pre * (1.0 - t * t) * (1.0 + 3.0 * GELU_B * square)
        slope_ref[0, :, cols] = slope.astype(BF)
        act_ref[0, :, cols] = act
        total = total + nn(act, wc_ref[cols, :])
    low_out = total.astype(BF)
    h_scr[...] = low_out.astype(F32)

    @pl.when(step == pl.num_programs(0) - 1)
    def _():
        last_ref[...] = low_out


def fold(values):
    return jnp.sum(values.reshape(-1, 8, values.shape[-1]), axis=0)


def backward_kernel(
    cot_ref, vec_ref, wqt_ref, wot_ref, wet_ref, wct_ref,
    n1_ref, proj_ref, probs_ref, n2_ref, slope_ref, inv_ref,
    gproj_ref, gattn_ref, gpre_ref, gmlp_ref, gtok_ref, sums_ref,
    g_scr, s768_scr, s2304_scr, s3072_scr,
):
    step = pl.program_id(0)
    rows, width = g_scr.shape
    pairs = width // 128
    ff = wct_ref.shape[1]

    @pl.when(step == 0)
    def _():
        g_scr[...] = cot_ref[...].astype(F32)
        s768_scr[...] = jnp.zeros_like(s768_scr)
        s2304_scr[...] = jnp.zeros_like(s2304_scr)
        s3072_scr[...] = jnp.zeros_like(s3072_scr)

    g = g_scr[...]
    gmlp = g.astype(BF)
    gmlp_ref[0] = gmlp
    gsec = jnp.zeros((rows, width), F32)
    chunk = 1024
    for j in range(ff // chunk):
        cols = slice(chunk * j, chunk * (j + 1))
        gpre = (nn(gmlp, wct_ref[:, cols]) * slope_ref[0, :, cols].astype(F32)).astype(BF)
        gpre_ref[0, :, cols] = gpre
        s3072_scr[:, cols] += fold(gpre.astype(F32))
        gsec = gsec + nn(gpre, wet_ref[cols, :])
    n2 = n2_ref[0].astype(F32)
    gmid = g + norm_back(gsec, n2, inv_ref[0, :, 128:129], vec_ref[3:4, :])
    gattn = gmid.astype(BF)
    gattn_ref[0] = gattn
    gatt = nn(gattn, wot_ref[...]).astype(BF)
    dqs, dks, dvs = [], [], []
    for p in range(pairs):
        q = proj_ref[0, :, 128 * p : 128 * (p + 1)]
        k = proj_ref[0, :, width + 128 * p : width + 128 * (p + 1)]
        v = proj_ref[0, :, 2 * width + 128 * p : 2 * width + 128 * (p + 1)]
        out2 = jnp.concatenate(lane_split(gatt[:, 128 * p : 128 * (p + 1)]), axis=0)
        low = probs_ref[0, 2 * rows * p : 2 * rows * (p + 1), :]
        prob = low.astype(F32)
        gprob = nt(out2, v)
        gscore = prob * (gprob - jnp.sum(prob * gprob, axis=-1, keepdims=True))
        gscore = gscore.astype(BF)
        both = jnp.concatenate([gscore[:rows], gscore[rows:]], axis=1)
        k2 = jnp.concatenate(lane_split(k), axis=0)
        q2 = jnp.concatenate(lane_split(q), axis=0)
        dqs.append((nn(both, k2) * SCORE_SCALE).astype(BF))
        dks.append((tn(gscore, q2) * SCORE_SCALE).astype(BF))
        dvs.append(tn(low, out2).astype(BF))
    gproj = jnp.concatenate(dqs + dks + dvs, axis=1)
    gproj_ref[0] = gproj
    gfirst = nn(gproj, wqt_ref[...])
    n1 = n1_ref[0].astype(F32)
    gin = gmid + norm_back(gfirst, n1, inv_ref[0, :, 0:1], vec_ref[0:1, :])
    s768_scr[0] += fold(gfirst * n1)
    s768_scr[1] += fold(gfirst)
    s768_scr[2] += fold(gattn.astype(F32))
    s768_scr[3] += fold(gsec * n2)
    s768_scr[4] += fold(gsec)
    s768_scr[5] += fold(gmlp.astype(F32))
    s2304_scr[...] += fold(gproj.astype(F32))
    low_out = gin.astype(BF)
    g_scr[...] = low_out.astype(F32)

    @pl.when(step == pl.num_programs(0) - 1)
    def _():
        gtok_ref[...] = low_out
        row = lambda v: jnp.sum(v, axis=0, keepdims=True)
        sums_ref[0:1, 0:width] = row(s768_scr[0])
        sums_ref[1:2, 0:width] = row(s768_scr[1])
        sums_ref[2:3, 0:width] = row(s2304_scr[:, 0:width])
        sums_ref[2:3, width : 2 * width] = row(s2304_scr[:, 2 * width : 3 * width])
        sums_ref[3:4, 0:width] = row(s768_scr[2])
        sums_ref[4:5, 0:width] = row(s768_scr[3])
        sums_ref[5:6, 0:width] = row(s768_scr[4])
        sums_ref[6:7, :] = row(s3072_scr[...])
        sums_ref[7:8, 0:width] = row(s768_scr[5])


def whole_spec(shape):
    zeros = (0,) * len(shape)
    return pl.BlockSpec(shape, lambda i, *_: zeros, pipeline_mode=pl.Buffered(1))


def forward_all(ends, x, vec, ebias, qkvb, wq, wo, we, wc, layers):
    rows, width = x.shape
    ff = we.shape[1]
    pairs = width // 128
    stack = lambda cols, r=rows, t=BF: jax.ShapeDtypeStruct((layers, r, cols), t)
    outs = [
        stack(width), stack(width), stack(3 * width), stack(rows, 2 * rows * pairs), stack(width),
        stack(width), stack(width), stack(ff), stack(ff), stack(256, rows, F32),
    ]
    per_layer = lambda s: pl.BlockSpec((1,) + s.shape[1:], lambda i, *_: (i, 0, 0))
    last = jax.ShapeDtypeStruct((rows, width), BF)
    return pl.pallas_call(
        forward_kernel,
        grid_spec=pltpu.PrefetchScalarGridSpec(
            num_scalar_prefetch=1,
            grid=(layers,),
            in_specs=[whole_spec(a.shape) for a in (x, vec, ebias, qkvb, wq, wo, we, wc)],
            out_specs=[per_layer(s) for s in outs] + [whole_spec(last.shape)],
            scratch_shapes=[pltpu.VMEM((rows, width), F32), pltpu.VMEM((rows, rows), F32)],
        ),
        out_shape=outs + [last],
        compiler_params=pltpu.CompilerParams(vmem_limit_bytes=VMEM_LIMIT),
    )(ends, x, vec, ebias, qkvb, wq, wo, we, wc)


def backward_all(cot, vec, wqt, wot, wet, wct, n1, proj, probs, n2, slope, inv):
    layers, rows, width = n1.shape
    ff = wct.shape[1]
    stack = lambda cols: jax.ShapeDtypeStruct((layers, rows, cols), BF)
    outs = [stack(3 * width), stack(width), stack(ff), stack(width)]
    per_layer = lambda s: pl.BlockSpec((1,) + s.shape[1:], lambda i: (layers - 1 - i, 0, 0))
    last = [jax.ShapeDtypeStruct((rows, width), BF), jax.ShapeDtypeStruct((8, ff), F32)]
    return pl.pallas_call(
        backward_kernel,
        grid=(layers,),
        in_specs=[whole_spec(a.shape) for a in (cot, vec, wqt, wot, wet, wct)]
        + [per_layer(a) for a in (n1, proj, probs, n2, slope, inv)],
        out_specs=[per_layer(s) for s in outs] + [whole_spec(s.shape) for s in last],
        out_shape=outs + last,
        scratch_shapes=[
            pltpu.VMEM((rows, width), F32),
            pltpu.VMEM((6, 8, width), F32),
            pltpu.VMEM((8, 3 * width), F32),
            pltpu.VMEM((8, ff), F32),
        ],
        compiler_params=pltpu.CompilerParams(vmem_limit_bytes=VMEM_LIMIT),
    )(cot, vec, wqt, wot, wet, wct, n1, proj, probs, n2, slope, inv)


def outer_kernel(start_ref, left_ref, right_ref, out_ref):
    out_ref[...] = tn(left_ref[...], right_ref[...]).astype(BF)


def outer(left, right, start, count, tile_m=384, tile_n=768):
    depth, cols = right.shape
    return pl.pallas_call(
        outer_kernel,
        grid_spec=pltpu.PrefetchScalarGridSpec(
            num_scalar_prefetch=1,
            grid=(count, cols // tile_n),
            in_specs=[
                pl.BlockSpec((depth, tile_m), lambda i, j, s: (0, s[0] + i)),
                pl.BlockSpec((depth, tile_n), lambda i, j, s: (0, j)),
            ],
            out_specs=pl.BlockSpec((tile_m, tile_n), lambda i, j, s: (i, j)),
        ),
        out_shape=jax.ShapeDtypeStruct((count * tile_m, cols), BF),
        compiler_params=pltpu.CompilerParams(vmem_limit_bytes=VMEM_LIMIT),
    )(start, left, right)


def xor_order(stacked, flips):
    count = stacked.shape[0]
    rest = stacked.shape[1:]
    bit = 1
    while bit < count:
        split = stacked.reshape((count // (2 * bit), 2, bit) + rest)
        split = jnp.where((flips & bit) != 0, split[:, ::-1], split)
        stacked = split.reshape((count,) + rest)
        bit *= 2
    return stacked


class Places:
    def __init__(self, sections, dps):
        self.sections, self.dps = sections, dps

    def spread(self, k):
        pairs = []
        for i in range(self.sections):
            for d in range(self.dps):
                own_x = (d >> 1) & 1
                label = i ^ k
                target = (label & ~1) | own_x
                to = (d & ~2) | ((label & 1) << 1)
                pairs.append((i * self.dps + d, target * self.dps + to))
        return pairs

    def collect(self, k):
        return [(b, a) for a, b in self.spread(k)]

    def other_core(self):
        return [(d, d ^ 1) for d in range(self.dps)]


def body(
    tokens, lengths, cotangent, first_gain, first_shift, qkv_weight, qv_bias, out_weight, out_bias,
    second_gain, second_shift, expand_weight, expand_bias, contract_weight, contract_bias,
):
    sections, dps = lax.axis_size("section"), lax.axis_size("dp")
    section, dp = lax.axis_index("section"), lax.axis_index("dp")
    micro, _, piece_rows, width = tokens.shape
    rows = piece_rows * sections
    ff = expand_weight.shape[1]
    places = Places(sections, dps)
    core, own_x, high = dp & 1, (dp >> 1) & 1, dp >> 2
    highs = dps // 4

    ends = jnp.cumsum(lengths[:, 0], axis=-1).astype(BF)
    slots = ends.shape[-1]
    ends = jnp.pad(ends, ((0, 0), (0, 128 - slots)))
    ends = jnp.broadcast_to(ends[:, None], (micro, piece_rows, 128))
    sent = jnp.concatenate([tokens[:, 0], cotangent[:, 0], ends], axis=-1)
    got = []
    for k in range(sections):
        block = lax.dynamic_index_in_dim(sent, (section ^ k) >> 1, 0, keepdims=False)
        got.append(lax.ppermute(block, AXES, places.spread(k)))
    label = (section & ~1) | own_x
    shard = xor_order(jnp.stack(got), label).reshape(rows, -1)
    x, cot = shard[:, :width], shard[:, width : 2 * width]
    ends_here = shard[0, 2 * width : 2 * width + slots].astype(jnp.int32)

    vec = jnp.stack(
        [first_gain, first_shift, out_bias, second_gain, second_shift, contract_bias, out_bias, out_bias]
    )
    qkvb = jnp.concatenate([qv_bias[:width], jnp.zeros((width,), F32), qv_bias[width:]])[None]
    first, n1, proj, probs, att, n2, second, slope, act, inv, last = forward_all(
        ends_here, x, vec, expand_bias[None], qkvb,
        qkv_weight, out_weight, expand_weight, contract_weight, sections,
    )
    gproj, gattn, gpre, gmlp, gtok, sums = backward_all(
        cot, vec, qkv_weight.T, out_weight.T, expand_weight.T, contract_weight.T,
        n1, proj, probs, n2, slope, inv,
    )

    flat = lambda a: a.reshape(-1, a.shape[-1])

    def own_half(left, right):
        left, right = flat(left), flat(right)
        cols = left.shape[1]
        if highs == 1:
            count = cols // 768
            start = (own_x * count)[None].astype(jnp.int32)
        else:
            left = left.reshape(-1, highs, 2, 2, cols // dps)
            left = lax.dynamic_index_in_dim(left, own_x, 2, keepdims=False).reshape(-1, cols // 2)
            count, start = cols // 768, jnp.zeros((1,), jnp.int32)
        out = outer(left, right, start, count)
        return out.reshape(highs, 2, cols // dps, right.shape[1])

    def vector_half(row):
        parts = row.reshape(highs, 2, 2, -1)
        return lax.dynamic_index_in_dim(parts, own_x, 1, keepdims=False)

    small_sizes = [width, width, 2 * width, width, width, width, ff, width]
    small = jnp.concatenate(
        [vector_half(sums[i, :n]) for i, n in enumerate(small_sizes)], axis=-1
    ).astype(BF)[:, :, None]
    pieces = [own_half(first, gproj), own_half(att, gattn), own_half(second, gpre), own_half(act, gmlp), small]
    totals = []
    for part in pieces:
        give = lax.dynamic_index_in_dim(part, 1 - core, 1, keepdims=False)
        keep = lax.dynamic_index_in_dim(part, core, 1, keepdims=False)
        part = keep + lax.ppermute(give, "dp", places.other_core())
        if highs > 1:
            groups = [[4 * h + low for h in range(highs)] for low in range(4)]
            part = lax.psum_scatter(part, "dp", scatter_dimension=0, tiled=False, axis_index_groups=groups)
        else:
            part = part[0]
        totals.append(lax.psum(part, "section").astype(F32))
    g_qkv, g_out, g_exp, g_con, g_small = totals
    g_small = g_small[0]
    vectors, at = [], 0
    for n in small_sizes:
        vectors.append(g_small[at : at + n // dps])
        at += n // dps

    both = jnp.concatenate([last, gtok], axis=1).reshape(sections, piece_rows, 2 * width)
    back = []
    for k in range(0, sections, 2):
        block = lax.dynamic_index_in_dim(both, label ^ k, 0, keepdims=False)
        pairs = [p for p in places.collect(k)]
        back.append(lax.ppermute(block, AXES, pairs))
    back = xor_order(jnp.stack(back), section >> 1)
    result = back[:, None, :, :width]
    grad_tokens = back[:, None, :, width:].astype(F32)
    return (
        result, grad_tokens, vectors[0], vectors[1], g_qkv, vectors[2], g_out, vectors[3],
        vectors[4], vectors[5], g_exp, vectors[6], g_con, vectors[7],
    )


def solution(mesh):
    tok = P(None, "dp", "section", None)
    return jax.shard_map(
        body,
        mesh=mesh,
        in_specs=(tok, P(None, "dp", None), tok) + (P(),) * 12,
        out_specs=(
            tok, tok, P("dp"), P("dp"), P("dp", None), P("dp"), P("dp", None), P("dp"),
            P("dp"), P("dp"), P("dp", None), P("dp"), P("dp", None), P("dp"),
        ),
        check_vma=False,
    )
```

time: 1610 us -> 360 us (0.22)
  waiting for transfers between devices: 672 us -> 111 us
  local copies, waits for them, and re-layouts: 420 us -> 54.3 us
  other arithmetic: 156 us -> 19.4 us
  matrix products: 129 us -> 0 us
  Pallas kernels: 0 us -> 110 us
  blocking collectives: 102 us -> 25.8 us
  starting transfers between devices: 99.3 us -> 23.9 us
    ppermute x22 -> x17, waiting for transfers between devices: 305 us -> 3.61 us  [the longest x8 3.58 us: body(): got.append(lax.ppermute(block, AXES, places.spread(k)))]
    reduce_scatter x6 -> x0, waiting for transfers between devices: 225 us -> none  [the longest x1 58.7 us: body(): lax.psum_scatter(finals[:, None].astype(jnp.bfloat16), 'section', scatter...]
    dynamic_update_slice x176 -> x0, local copies, waits for them, and re-layouts: 221 us -> none  [store_at(): lax.dynamic_update_index_in_dim(whole, member, target, 0)]
    dot_general x64 -> x0, matrix products: 129 us -> none  [the longest x16 51.1 us: transpose_dot(): lax.dot_general(left_side, right_side, (((1,), (1,)), ((), ())), preferre...]
    pallas_call x0 -> x6, Pallas kernels: none -> 110 us  [the longest x1 46 us: backward_all(): pl.pallas_call(backward_kernel, grid=(layers,), in_specs=[whole_spec(a.sh...]
    add x63 -> x0, other arithmetic: 82.1 us -> none  [the longest x55 72.4 us: backward_turn(): small_total = jax.tree.map(jnp.add, small_total, small_grads)]
    ppermute x22 -> x17, starting transfers between devices: 99.1 us -> 23.9 us  [the longest x8 17.6 us: body(): got.append(lax.ppermute(block, AXES, places.spread(k)))]
    all_gather x2 -> x0, blocking collectives: 70 us -> none  [the longest x1 36 us: body(): lax.all_gather(tokens, 'section', axis=2, tiled=True)]
  transfers between devices with their start and end apart: 29 -> 18, of which waited for: 28 -> 2; matrix products, arithmetic and copies ran while one was open for 2% -> 16% of each run, Pallas kernels for 0% -> 4%
where the time goes in v1:
time: 360 us; the launch traced here: 359 us
  waiting for transfers between devices  111 us (31%)
  Pallas kernels  110 us (31%)
  local copies, waits for them, and re-layouts  54.3 us (15%)
  blocking collectives  25.8 us (7%)
  starting transfers between devices  23.9 us (7%)
  other arithmetic  19.4 us (5%)
  between operations  14.4 us (4%)
    psum x1, waiting for transfers between devices, body(): totals.append(lax.psum(part, 'section').astype(F32))  107 us
    pallas_call x1, Pallas kernels, backward_all(): pl.pallas_call(backward_kernel, grid=(layers,), in_specs=[whole_spec(a.sh...  46 us
    pallas_call x1, Pallas kernels, forward_all(): pl.pallas_call(forward_kernel, grid_spec=pltpu.PrefetchScalarGridSpec(num...  42.3 us
    psum x1, blocking collectives, body(): totals.append(lax.psum(part, 'section').astype(F32))  25.8 us
    unnamed x55, local copies, waits for them, and re-layouts  24.4 us
    pallas_call x4, Pallas kernels, outer(): pl.pallas_call(outer_kernel, grid_spec=pltpu.PrefetchScalarGridSpec(num_s...  22.2 us
    ppermute x8, starting transfers between devices, body(): got.append(lax.ppermute(block, AXES, places.spread(k)))  17.6 us
    squeeze x5, other arithmetic, body(): part = part[0]  9.12 us
  transfers between devices with their start and end apart: 18, of which 2 were waited for; matrix products, arithmetic and copies ran while one was open for 16% of the time, Pallas kernels for 4%

profile of v1, /device:TPU:0, one launch (start us, length us, event | category | flops | bytes accessed | tf_op | source)
XLA Modules:
  0.0 358.8 jit_solution(14906275437139400260)
XLA Ops:
  7.3 0.9 reduce_window_sum.11
  8.2 1.0 pad_maximum_fusion.1
  9.9 2.1 collective-permute-start
  12.0 4.3 %collective-permute-start.1 = (bf16[16,1664]{1,0:T(8,128)(2,1)}, bf16[16,1664]{1,0:T(8,128)(2,1)}, u32[]{:S(2)}, u32[]{:S(2)}) collective-permute-start(bf16[16,1664]{1,0:T(8,128)(2,1)} %get-tuple-element.70), channel_id=1, source_target_pairs={{0,2},{1,3},{2,6},{3,7},{4,0},{5,1},{6,4},{7,5},{8,10},{9,11},{10,... | collective-permute-start | bytes 159752 | tf_op jit(solution)/shard_map/ppermute | solution.py:346
  16.3 1.6 collective-permute-start.2
  17.9 0.8 collective-permute-start.3
  18.7 2.6 collective-permute-start.4
  26.7 6.6 %copy.31 = bf16[768,3072]{0,1:T(8,128)(2,1)} copy(bf16[768,3072]{1,0:T(8,128)(2,1)} %we_ref.1) | data formatting | bytes 9437184 | tf_op args[11]
  33.3 6.9 %copy.32 = bf16[3072,768]{0,1:T(8,128)(2,1)} copy(bf16[3072,768]{1,0:T(8,128)(2,1)} %wc_ref.1) | data formatting | bytes 9437184 | tf_op args[13]
  40.1 3.6 %copy.29 = bf16[768,2304]{0,1:T(8,128)(2,1)} copy(bf16[768,2304]{1,0:T(8,128)(2,1)S(1)} %copy-done) | data formatting | bytes 7077888 | tf_op args[5]
  43.7 2.4 copy.30
  46.8 1.7 collective-permute-start.5
  48.6 0.8 bitcast_dynamic-update-slice_fusion.7
  49.4 3.7 %collective-permute-start.6 = (bf16[16,1664]{1,0:T(8,128)(2,1)S(1)}, bf16[16,1664]{1,0:T(8,128)(2,1)S(1)}, u32[]{:S(2)}, u32[]{:S(2)}) collective-permute-start(bf16[16,1664]{1,0:T(8,128)(2,1)S(1)} %copy-done.11), channel_id=1, source_target_pairs={{0,24},{1,25},{2,28},{3,29},{4,26},{5,27},{6,30},{7,31},{8,16},{9,... | collective-permute-start | bytes 159752 | tf_op jit(solution)/shard_map/ppermute | solution.py:346
  53.1 0.8 bitcast_dynamic-update-slice_fusion.6
  54.7 0.8 bitcast_dynamic-update-slice_fusion.5
  55.5 0.8 bitcast_dynamic-update-slice_fusion.4
  56.4 0.8 bitcast_dynamic-update-slice_fusion.3
  57.2 3.6 collective-permute-done.7
  62.3 42.3 %shard_map.254 = (bf16[8,128,768]{2,1,0:T(8,128)(2,1)}, bf16[8,128,768]{2,1,0:T(8,128)(2,1)}, bf16[8,128,2304]{2,1,0:T(8,128)(2,1)}, bf16[8,1536,128]{2,1,0:T(8,...) custom-call(s32[4]{0:T(128)} %fusion.22.ends_ref, ...), custom_call_target="tpu_custom_call" | custom-call | tf_op jit(solution)/shard_map/pallas_call | solution.py:231
  104.6 46.0 %shard_map.255 = (bf16[8,128,2304]{2,1,0:T(8,128)(2,1)}, bf16[8,128,768]{2,1,0:T(8,128)(2,1)}, bf16[8,128,3072]{2,1,0:T(8,128)(2,1)}, bf16[8,128,768]{2,1,0:T(8,...) custom-call(bf16[128,768]{1,0:T(8,128)(2,1)} %get-tuple-element.59.cot_ref, f32[8,768]{1,0:T(8,128)} %stack.80.vec_ref, ...), custom_call_target="tpu_custom_call" | custom-call | tf_op jit(solution)/shard_map/pallas_call | solution.py:252
  150.6 6.4 %shard_map.259 = bf16[1536,768]{1,0:T(8,128)(2,1)} custom-call(s32[1]{0:T(128)} %bitcast.76.start_ref, bf16[1024,3072]{1,0:T(8,128)(2,1)} %bitcast.152, bf16[1024,768]{1,0:T(8,128)(2,1)} %bitcast.163), custom_call_target="tpu_custom_call" | custom-call | tf_op jit(solution)/shard_map/pallas_call | solution.py:275
  157.0 1.3 dynamic-slice_bitcast_fusion
  158.5 6.7 %shard_map.258 = bf16[384,3072]{1,0:T(8,128)(2,1)} custom-call(s32[1]{0:T(128)} %bitcast.54.start_ref, bf16[1024,768]{1,0:T(8,128)(2,1)} %bitcast.162, bf16[1024,3072]{1,0:T(8,128)(2,1)} %bitcast.153), custom_call_target="tpu_custom_call" | custom-call | tf_op jit(solution)/shard_map/pallas_call | solution.py:275
  165.2 2.4 dynamic-slice_bitcast_fusion.1
  168.0 3.3 shard_map.257
  171.3 1.7 dynamic-slice_bitcast_fusion.3
  173.0 5.8 %shard_map.256 = bf16[384,2304]{1,0:T(8,128)(2,1)} custom-call(s32[1]{0:T(128)} %bitcast.54.start_ref, bf16[1024,768]{1,0:T(8,128)(2,1)} %bitcast.166, bf16[1024,2304]{1,0:T(8,128)(2,1)} %bitcast.155), custom_call_target="tpu_custom_call" | custom-call | tf_op jit(solution)/shard_map/pallas_call | solution.py:275
  178.8 2.3 dynamic-slice_bitcast_fusion.2
  181.6 1.6 slice_reduce_fusion.3
  183.2 1.3 reshape_squeeze.29
  184.5 1.3 reshape_squeeze.31
  188.5 0.9 slice_reduce_fusion
  189.5 0.8 slice_reduce_fusion.1
  190.3 1.2 fusion.16
  191.6 1.2 fusion.18
  192.8 1.3 fusion.20
  194.1 1.9 fusion.3
  196.0 2.2 fusion.2
  198.2 2.6 fusion
  200.8 2.5 fusion.1
  205.9 3.6 %collective-permute-start.11 = (bf16[16,1536]{1,0:T(8,128)(2,1)S(1)}, bf16[16,1536]{1,0:T(8,128)(2,1)S(1)}, u32[]{:S(2)}, u32[]{:S(2)}) collective-permute-start(bf16[16,1536]{1,0:T(8,128)(2,1)S(1)} %get-tuple-element.61), channel_id=1, source_target_pairs={{24,0},{25,1},{28,2},{29,3},{26,4},{27,5},{30,6},{31,7},{16,8},{17... | collective-permute-start | bytes 147464 | tf_op jit(solution)/shard_map/ppermute | solution.py:412
  209.6 25.8 %psum.35 = bf16[1,2304]{1,0:T(2,128)(2,1)S(1)} all-reduce(bf16[1,2304]{1,0:T(2,128)(2,1)S(1)} %add_bitcast_fusion), channel_id=1, replica_groups=mesh['section'=8,'dp'=4] {'section'}, use_global_device_ids=true, to_apply=%region_1.2 | all-reduce | flops 2304 | bytes 9216 | tf_op jit(solution)/shard_map/psum | solution.py:399
  238.2 106.9 %all-reduce.4.cloned.1.call-done = (bf16[192,2304]{1,0:T(8,128)(2,1)}, bf16[192,768]{1,0:T(8,128)(2,1)}, bf16[192,3072]{1,0:T(8,128)(2,1)}, bf16[768,768]{1,0:T(8,128)(2,1)}) async-done(((bf16[192,2304]{1,0:T(8,128)(2,1)}, bf16[192,768]{1,0:T(8,128)(2,1)}, bf16[192,3072]{1,0:T(8,128)(2,1)}, bf16[768,768]{1,0:T(8,128)(2,1)}), (bf16[192,2304]{1,0:T(8,128)(2,1)}, bf16[192,768]{1,0:T(8,128)(2,1)}, ...) | async-done | bytes 3538960 | tf_op jit(solution)/shard_map/psum | solution.py:399
  345.1 3.0 convert_element_type.48
  348.2 1.6 convert_element_type.49
  349.7 1.3 convert_element_type.46
  351.1 0.9 convert_element_type.47
  (115 shorter events, 18.4 us)
Async XLA Ops:
  7.2 18.3 %copy-start.15 = (f32[768]{0:T(1024)S(1)}, f32[768]{0:T(1024)}, u32[]{:S(2)}) copy-start(f32[768]{0:T(1024)} %param.25) | copy-start | bytes 9220
  7.2 18.9 %copy-start.16 = (f32[768]{0:T(1024)S(1)}, f32[768]{0:T(1024)}, u32[]{:S(2)}) copy-start(f32[768]{0:T(1024)} %param.29) | copy-start | bytes 9220
  7.2 337.9 %all-reduce.4.cloned.1.call-start = ((), (), s32[]{:S(2)}) async-start(), calls=%async_computation | async-start | bytes 7077888 | tf_op jit(solution)/shard_map/psum | solution.py:399
  9.9 36.9 %collective-permute-start = (bf16[16,1664]{1,0:T(8,128)(2,1)}, bf16[16,1664]{1,0:T(8,128)(2,1)}, u32[]{:S(2)}, u32[]{:S(2)}) collective-permute-start(bf16[16,1664]{1,0:T(8,128)(2,1)} %get-tuple-element.71), channel_id=1, source_target_pairs={{0,0},{1,1},{2,4},{3,5},{4,2},{5,3},{6,6},{7,7},{8,8},{9,9},{10,12... | collective-permute-start | bytes 159752 | tf_op jit(solution)/shard_map/ppermute | solution.py:346
  12.0 37.4 %collective-permute-start.1 = (bf16[16,1664]{1,0:T(8,128)(2,1)}, bf16[16,1664]{1,0:T(8,128)(2,1)}, u32[]{:S(2)}, u32[]{:S(2)}) collective-permute-start(bf16[16,1664]{1,0:T(8,128)(2,1)} %get-tuple-element.70), channel_id=1, source_target_pairs={{0,2},{1,3},{2,6},{3,7},{4,0},{5,1},{6,4},{7,5},{8,10},{9,11},{10,... | collective-permute-start | bytes 159752 | tf_op jit(solution)/shard_map/ppermute | solution.py:346
  16.3 37.6 %collective-permute-start.2 = (bf16[16,1664]{1,0:T(8,128)(2,1)}, bf16[16,1664]{1,0:T(8,128)(2,1)}, u32[]{:S(2)}, u32[]{:S(2)}) collective-permute-start(bf16[16,1664]{1,0:T(8,128)(2,1)} %get-tuple-element.69), channel_id=1, source_target_pairs={{0,8},{1,9},{2,12},{3,13},{4,10},{5,11},{6,14},{7,15},{8,0},{9,1},... | collective-permute-start | bytes 159752 | tf_op jit(solution)/shard_map/ppermute | solution.py:346
  17.9 37.7 %collective-permute-start.3 = (bf16[16,1664]{1,0:T(8,128)(2,1)}, bf16[16,1664]{1,0:T(8,128)(2,1)}, u32[]{:S(2)}, u32[]{:S(2)}) collective-permute-start(bf16[16,1664]{1,0:T(8,128)(2,1)} %get-tuple-element.68), channel_id=1, source_target_pairs={{0,10},{1,11},{2,14},{3,15},{4,8},{5,9},{6,12},{7,13},{8,2},{9,3},... | collective-permute-start | bytes 159752 | tf_op jit(solution)/shard_map/ppermute | solution.py:346
  18.7 37.7 %collective-permute-start.4 = (bf16[16,1664]{1,0:T(8,128)(2,1)}, bf16[16,1664]{1,0:T(8,128)(2,1)}, u32[]{:S(2)}, u32[]{:S(2)}) collective-permute-start(bf16[16,1664]{1,0:T(8,128)(2,1)} %get-tuple-element.67), channel_id=1, source_target_pairs={{0,16},{1,17},{2,20},{3,21},{4,18},{5,19},{6,22},{7,23},{8,24},{9,... | collective-permute-start | bytes 159752 | tf_op jit(solution)/shard_map/ppermute | solution.py:346
  33.3 6.9 %copy-start = (bf16[768,2304]{1,0:T(8,128)(2,1)S(1)}, bf16[768,2304]{1,0:T(8,128)(2,1)}, u32[]{:S(2)}) copy-start(bf16[768,2304]{1,0:T(8,128)(2,1)} %wq_ref.1) | copy-start | bytes 10616836
  43.7 2.5 copy-start.13
  43.7 2.5 copy-start.14
  43.7 3.1 copy-start.12
  43.7 5.7 %copy-start.11 = (bf16[16,1664]{1,0:T(8,128)(2,1)S(1)}, bf16[16,1664]{1,0:T(8,128)(2,1)}, u32[]{:S(2)}) copy-start(bf16[16,1664]{1,0:T(8,128)(2,1)} %get-tuple-element.65) | copy-start | bytes 159748
  43.7 10.2 %copy-start.10 = (bf16[16,1664]{1,0:T(8,128)(2,1)S(1)}, bf16[16,1664]{1,0:T(8,128)(2,1)}, u32[]{:S(2)}) copy-start(bf16[16,1664]{1,0:T(8,128)(2,1)} %get-tuple-element.64) | copy-start | bytes 159748
  46.8 10.3 %collective-permute-start.5 = (bf16[16,1664]{1,0:T(8,128)(2,1)S(1)}, bf16[16,1664]{1,0:T(8,128)(2,1)S(1)}, u32[]{:S(2)}, u32[]{:S(2)}) collective-permute-start(bf16[16,1664]{1,0:T(8,128)(2,1)S(1)} %copy-done.12), channel_id=1, source_target_pairs={{0,18},{1,19},{2,22},{3,23},{4,16},{5,17},{6,20},{7,21},{8,26},{9,... | collective-permute-start | bytes 159752 | tf_op jit(solution)/shard_map/ppermute | solution.py:346
  49.4 7.8 %collective-permute-start.6 = (bf16[16,1664]{1,0:T(8,128)(2,1)S(1)}, bf16[16,1664]{1,0:T(8,128)(2,1)S(1)}, u32[]{:S(2)}, u32[]{:S(2)}) collective-permute-start(bf16[16,1664]{1,0:T(8,128)(2,1)S(1)} %copy-done.11), channel_id=1, source_target_pairs={{0,24},{1,25},{2,28},{3,29},{4,26},{5,27},{6,30},{7,31},{8,16},{9,... | collective-permute-start | bytes 159752 | tf_op jit(solution)/shard_map/ppermute | solution.py:346
  53.9 6.9 %collective-permute-start.7 = (bf16[16,1664]{1,0:T(8,128)(2,1)S(1)}, bf16[16,1664]{1,0:T(8,128)(2,1)S(1)}, u32[]{:S(2)}, u32[]{:S(2)}) collective-permute-start(bf16[16,1664]{1,0:T(8,128)(2,1)S(1)} %copy-done.10), channel_id=1, source_target_pairs={{0,26},{1,27},{2,30},{3,31},{4,24},{5,25},{6,28},{7,29},{8,18},{9,... | collective-permute-start | bytes 159752 | tf_op jit(solution)/shard_map/ppermute | solution.py:346
  158.4 39.8 %collective-permute-start.16 = (bf16[1,768,768]{2,1,0:T(8,128)(2,1)S(1)}, bf16[1,768,768]{2,1,0:T(8,128)(2,1)}, u32[]{:S(2)}, u32[]{:S(2)}) collective-permute-start(bf16[1,768,768]{2,1,0:T(8,128)(2,1)S(1)} %dynamic-slice_bitcast_fusion), channel_id=1, source_target_pairs={{0,1},{1,0},{2,3},{3,2},{4,5},{5,4},{6,7},{7,6},{8,9},{9,8},{10,11... | collective-permute-start | bytes 3538952 | tf_op jit(solution)/shard_map/ppermute | solution.py:393
  167.5 33.2 %collective-permute-start.15 = (bf16[1,192,3072]{2,1,0:T(8,128)(2,1)}, bf16[1,192,3072]{2,1,0:T(8,128)(2,1)}, u32[]{:S(2)}, u32[]{:S(2)}) collective-permute-start(bf16[1,192,3072]{2,1,0:T(8,128)(2,1)} %dynamic-slice_bitcast_fusion.1), channel_id=1, source_target_pairs={{0,1},{1,0},{2,3},{3,2},{4,5},{5,4},{6,7},{7,6},{8,9},{9,8},{10,11... | collective-permute-start | bytes 3538952 | tf_op jit(solution)/shard_map/ppermute | solution.py:393
  173.0 21.1 %collective-permute-start.14 = (bf16[1,192,768]{2,1,0:T(8,128)(2,1)}, bf16[1,192,768]{2,1,0:T(8,128)(2,1)}, u32[]{:S(2)}, u32[]{:S(2)}) collective-permute-start(bf16[1,192,768]{2,1,0:T(8,128)(2,1)} %dynamic-slice_bitcast_fusion.3), channel_id=1, source_target_pairs={{0,1},{1,0},{2,3},{3,2},{4,5},{5,4},{6,7},{7,6},{8,9},{9,8},{10,11... | collective-permute-start | bytes 884744 | tf_op jit(solution)/shard_map/ppermute | solution.py:393
  173.0 21.1 %copy-start.4 = (bf16[384,768]{1,0:T(8,128)(2,1)S(1)}, bf16[384,768]{1,0:T(8,128)(2,1)}, u32[]{:S(2)}) copy-start(bf16[384,768]{1,0:T(8,128)(2,1)} %shard_map.257) | copy-start | bytes 1769476
  178.8 17.2 %copy-start.3 = (bf16[384,2304]{1,0:T(8,128)(2,1)S(1)}, bf16[384,2304]{1,0:T(8,128)(2,1)}, u32[]{:S(2)}) copy-start(bf16[384,2304]{1,0:T(8,128)(2,1)} %shard_map.256) | copy-start | bytes 5308420
  181.1 14.8 %collective-permute-start.13 = (bf16[1,192,2304]{2,1,0:T(8,128)(2,1)}, bf16[1,192,2304]{2,1,0:T(8,128)(2,1)}, u32[]{:S(2)}, u32[]{:S(2)}) collective-permute-start(bf16[1,192,2304]{2,1,0:T(8,128)(2,1)} %dynamic-slice_bitcast_fusion.2), channel_id=1, source_target_pairs={{0,1},{1,0},{2,3},{3,2},{4,5},{5,4},{6,7},{7,6},{8,9},{9,8},{10,11... | collective-permute-start | bytes 2654216 | tf_op jit(solution)/shard_map/ppermute | solution.py:393
  194.1 4.1 %copy-start.1 = (bf16[1536,768]{1,0:T(8,128)(2,1)S(1)}, bf16[1536,768]{1,0:T(8,128)(2,1)}, u32[]{:S(2)}) copy-start(bf16[1536,768]{1,0:T(8,128)(2,1)} %shard_map.259) | copy-start | bytes 7077892
  198.1 2.6 copy-start.2
  203.2 0.7 copy-start.17
  203.2 0.7 copy-start.18
  203.2 0.7 copy-start.19
  203.2 0.7 copy-start.20
  203.2 0.7 copy-start.21
  203.2 1.0 copy-start.8
  203.3 1.1 copy-start.9
  204.1 5.4 %collective-permute-start.12 = (bf16[1,1,2304]{2,1,0:T(2,128)(2,1)S(1)}, bf16[1,1,2304]{2,1,0:T(2,128)(2,1)S(1)}, u32[]{:S(2)}, u32[]{:S(2)}) collective-permute-start(bf16[1,1,2304]{2,1,0:T(2,128)(2,1)S(1)} %constant_dynamic-slice_fusion), channel_id=1, source_target_pairs={{0,1},{1,0},{2,3},{3,2},{4,5},{5,4},{6,7},{7,6},{8,9},{9,8},{10,11... | collective-permute-start | bytes 13832 | tf_op jit(solution)/shard_map/ppermute | solution.py:393
  204.4 32.9 %collective-permute-start.8 = (bf16[16,1536]{1,0:T(8,128)(2,1)S(1)}, bf16[16,1536]{1,0:T(8,128)(2,1)S(1)}, u32[]{:S(2)}, u32[]{:S(2)}) collective-permute-start(bf16[16,1536]{1,0:T(8,128)(2,1)S(1)} %get-tuple-element.60), channel_id=1, source_target_pairs={{0,0},{1,1},{4,2},{5,3},{2,4},{3,5},{6,6},{7,7},{8,8},{9,9},{12,10... | collective-permute-start | bytes 147464 | tf_op jit(solution)/shard_map/ppermute | solution.py:412
  205.1 32.2 %collective-permute-start.9 = (bf16[16,1536]{1,0:T(8,128)(2,1)S(1)}, bf16[16,1536]{1,0:T(8,128)(2,1)S(1)}, u32[]{:S(2)}, u32[]{:S(2)}) collective-permute-start(bf16[16,1536]{1,0:T(8,128)(2,1)S(1)} %get-tuple-element.63), channel_id=1, source_target_pairs={{8,0},{9,1},{12,2},{13,3},{10,4},{11,5},{14,6},{15,7},{0,8},{1,9},... | collective-permute-start | bytes 147464 | tf_op jit(solution)/shard_map/ppermute | solution.py:412
  205.1 32.2 %collective-permute-start.10 = (bf16[16,1536]{1,0:T(8,128)(2,1)S(1)}, bf16[16,1536]{1,0:T(8,128)(2,1)S(1)}, u32[]{:S(2)}, u32[]{:S(2)}) collective-permute-start(bf16[16,1536]{1,0:T(8,128)(2,1)S(1)} %get-tuple-element.62), channel_id=1, source_target_pairs={{16,0},{17,1},{20,2},{21,3},{18,4},{19,5},{22,6},{23,7},{24,8},{25... | collective-permute-start | bytes 147464 | tf_op jit(solution)/shard_map/ppermute | solution.py:412
  205.9 31.4 %collective-permute-start.11 = (bf16[16,1536]{1,0:T(8,128)(2,1)S(1)}, bf16[16,1536]{1,0:T(8,128)(2,1)S(1)}, u32[]{:S(2)}, u32[]{:S(2)}) collective-permute-start(bf16[16,1536]{1,0:T(8,128)(2,1)S(1)} %get-tuple-element.61), channel_id=1, source_target_pairs={{24,0},{25,1},{28,2},{29,3},{26,4},{27,5},{30,6},{31,7},{16,8},{17... | collective-permute-start | bytes 147464 | tf_op jit(solution)/shard_map/ppermute | solution.py:412
  345.1 3.0 copy-start.5
  348.2 1.6 copy-start.6
  349.7 1.3 copy-start.7
Sparse Core Ops, SparseCore 0:
  203.4 141.6 all-reduce.3

commit v2 on v1

--- a/solution.py
+++ b/solution.py
@@ -201,15 +201,11 @@
     def _():
         gtok_ref[...] = low_out
         row = lambda v: jnp.sum(v, axis=0, keepdims=True)
-        sums_ref[0:1, 0:width] = row(s768_scr[0])
-        sums_ref[1:2, 0:width] = row(s768_scr[1])
-        sums_ref[2:3, 0:width] = row(s2304_scr[:, 0:width])
-        sums_ref[2:3, width : 2 * width] = row(s2304_scr[:, 2 * width : 3 * width])
-        sums_ref[3:4, 0:width] = row(s768_scr[2])
-        sums_ref[4:5, 0:width] = row(s768_scr[3])
-        sums_ref[5:6, 0:width] = row(s768_scr[4])
-        sums_ref[6:7, :] = row(s3072_scr[...])
-        sums_ref[7:8, 0:width] = row(s768_scr[5])
+        for i in range(6):
+            sums_ref[i : i + 1, 0:width] = row(s768_scr[i])
+        sums_ref[6:7, 0:width] = row(s2304_scr[:, 0:width])
+        sums_ref[6:7, width : 2 * width] = row(s2304_scr[:, 2 * width : 3 * width])
+        sums_ref[7:8, :] = row(s3072_scr[...])
 
 
 def whole_spec(shape):
@@ -266,26 +262,156 @@
     )(cot, vec, wqt, wot, wet, wct, n1, proj, probs, n2, slope, inv)
 
 
-def outer_kernel(start_ref, left_ref, right_ref, out_ref):
-    out_ref[...] = tn(left_ref[...], right_ref[...]).astype(BF)
-
-
-def outer(left, right, start, count, tile_m=384, tile_n=768):
-    depth, cols = right.shape
+def outer_kernel(spot_ref, left_ref, right_ref, give_ref, keep_ref, scr, *, tall):
+    scr[...] = tn(left_ref[...], right_ref[...]).astype(BF)
+    split_out(spot_ref, scr, give_ref, keep_ref, 0, scr.shape[1], tall)
+
+
+def split_out(spot_ref, scr, give_ref, keep_ref, at, cols, tall):
+    x, c, y = spot_ref[0], spot_ref[1], spot_ref[2]
+    for crel in (1, 0):
+        out = give_ref if crel else keep_ref
+        for xrel in (0, 1):
+            for yrel in (0, 1):
+                part = ((x ^ xrel) * 2 + (c ^ crel)) * 2 + (y ^ yrel)
+                start = pl.multiple_of(part * tall, tall)
+                out[xrel, yrel, 0:tall, at : at + cols] = scr[pl.ds(start, tall), :]
+
+
+def parts_of(rows, cols):
+    return jax.ShapeDtypeStruct((2, 2, rows, cols), BF)
+
+
+def expand_grads(spot, left, right, tile=768):
+    depth, width = left.shape
+    half = right.shape[1] // 2
+    steps = half // tile
+    out = parts_of(width // 8, half)
+    out_spec = pl.BlockSpec((2, 2, width // 8, tile), lambda j, s: (0, 0, 0, j))
     return pl.pallas_call(
-        outer_kernel,
+        partial(outer_kernel, tall=width // 8),
         grid_spec=pltpu.PrefetchScalarGridSpec(
             num_scalar_prefetch=1,
-            grid=(count, cols // tile_n),
+            grid=(steps,),
             in_specs=[
-                pl.BlockSpec((depth, tile_m), lambda i, j, s: (0, s[0] + i)),
-                pl.BlockSpec((depth, tile_n), lambda i, j, s: (0, j)),
+                pl.BlockSpec((depth, width), lambda j, s: (0, 0)),
+                pl.BlockSpec((depth, tile), lambda j, s: (0, s[3] * steps + j)),
             ],
-            out_specs=pl.BlockSpec((tile_m, tile_n), lambda i, j, s: (i, j)),
+            out_specs=[out_spec, out_spec],
+            scratch_shapes=[pltpu.VMEM((width, tile), BF)],
         ),
-        out_shape=jax.ShapeDtypeStruct((count * tile_m, cols), BF),
+        out_shape=[out, out],
+        cost_estimate=cost_of(depth, width, half),
         compiler_params=pltpu.CompilerParams(vmem_limit_bytes=VMEM_LIMIT),
-    )(start, left, right)
+    )(spot, left, right)
+
+
+def cost_of(depth, rows, cols):
+    return pl.CostEstimate(
+        flops=2 * depth * rows * cols, transcendentals=0, bytes_accessed=2 * depth * (rows + cols) + 2 * rows * cols
+    )
+
+
+def contract_kernel(spot_ref, left_ref, right_ref, give_ref, keep_ref, scr):
+    step = pl.program_id(0)
+    y = spot_ref[2]
+    tall = scr.shape[0] // 2
+    scr[...] = tn(left_ref[...], right_ref[...]).astype(BF)
+    for yrel in (0, 1):
+        start = pl.multiple_of((y ^ yrel) * tall, tall)
+
+        @pl.when(step < 2)
+        def _():
+            give_ref[0, yrel] = scr[pl.ds(start, tall), :]
+
+        @pl.when(step >= 2)
+        def _():
+            keep_ref[0, yrel] = scr[pl.ds(start, tall), :]
+
+
+def contract_grads(spot, left, right):
+    depth, ff = left.shape
+    width = right.shape[1]
+    tall = ff // 8
+
+    def column(i, s):
+        return (0, (((i & 1) ^ s[0]) * 2 + ((1 - (i >> 1)) ^ s[1])) * 2 + s[3])
+
+    out = parts_of(tall // 2, width)
+    return pl.pallas_call(
+        contract_kernel,
+        grid_spec=pltpu.PrefetchScalarGridSpec(
+            num_scalar_prefetch=1,
+            grid=(4,),
+            in_specs=[
+                pl.BlockSpec((depth, tall), column),
+                pl.BlockSpec((depth, width), lambda i, s: (0, 0)),
+            ],
+            out_specs=[
+                pl.BlockSpec((1, 2, tall // 2, width), lambda i, s: (jnp.minimum(i, 1), 0, 0, 0)),
+                pl.BlockSpec((1, 2, tall // 2, width), lambda i, s: (jnp.maximum(i - 2, 0), 0, 0, 0)),
+            ],
+            scratch_shapes=[pltpu.VMEM((tall, width), BF)],
+        ),
+        out_shape=[out, out],
+        cost_estimate=cost_of(depth, ff // 2, width),
+        compiler_params=pltpu.CompilerParams(vmem_limit_bytes=VMEM_LIMIT),
+    )(spot, left, right)
+
+
+def attention_kernel(
+    spot_ref, first_ref, gproj_ref, att_ref, gattn_ref, sums_ref, give_ref, keep_ref, qkv_scr, out_scr,
+):
+    tall = qkv_scr.shape[0] // 8
+    wide = qkv_scr.shape[1]
+    qkv_scr[...] = tn(first_ref[...], gproj_ref[...]).astype(BF)
+    split_out(spot_ref, qkv_scr, give_ref, keep_ref, 0, wide, tall)
+    out_scr[...] = tn(att_ref[...], gattn_ref[...]).astype(BF)
+    split_out(spot_ref, out_scr, give_ref, keep_ref, wide, out_scr.shape[1], tall)
+    x, c = spot_ref[0], spot_ref[1]
+    width, cols = qkv_scr.shape[0], give_ref.shape[3]
+    for crel, out in ((1, give_ref), (0, keep_ref)):
+        for xrel in (0, 1):
+            place = (x ^ xrel) * 2 + (c ^ crel)
+            window = lambda i, start, size: sums_ref[i : i + 1, pl.ds(pl.multiple_of(start, 128), size)]
+            low = ((place * 3) >> 1) * 128
+            singles = [window(i, low, 256) for i in range(6)]
+            doubles = [window(6, place * (width // 2), width // 2), window(7, place * width, width)]
+            used = (width // 2) * 3
+            doubles.append(jnp.zeros((1, cols - used), F32))
+            block = jnp.concatenate(
+                [
+                    jnp.concatenate(singles, axis=1),
+                    jnp.concatenate(doubles, axis=1),
+                    jnp.zeros((14, cols), F32),
+                ],
+                axis=0,
+            ).astype(BF)
+            for yrel in (0, 1):
+                out[xrel, yrel, tall : tall + 16, :] = block
+
+
+def attention_grads(spot, first, gproj, att, gattn, sums):
+    depth, width = first.shape
+    wide, thin = gproj.shape[1] // 2, gattn.shape[1] // 2
+    out = parts_of(width // 8 + 16, wide + thin)
+    whole = lambda shape: pl.BlockSpec(shape, lambda i, s: (0,) * len(shape))
+    half = lambda cols: pl.BlockSpec((depth, cols), lambda i, s: (0, s[3]))
+    return pl.pallas_call(
+        attention_kernel,
+        grid_spec=pltpu.PrefetchScalarGridSpec(
+            num_scalar_prefetch=1,
+            grid=(1,),
+            in_specs=[
+                whole(first.shape), half(wide), whole(att.shape), half(thin), whole(sums.shape),
+            ],
+            out_specs=[whole(out.shape), whole(out.shape)],
+            scratch_shapes=[pltpu.VMEM((width, wide), BF), pltpu.VMEM((width, thin), BF)],
+        ),
+        out_shape=[out, out],
+        cost_estimate=cost_of(depth, width, wide + thin),
+        compiler_params=pltpu.CompilerParams(vmem_limit_bytes=VMEM_LIMIT),
+    )(spot, first, gproj, att, gattn, sums)
 
 
 def xor_order(stacked, flips):
@@ -300,26 +426,47 @@
     return stacked
 
 
-class Places:
-    def __init__(self, sections, dps):
-        self.sections, self.dps = sections, dps
-
-    def spread(self, k):
-        pairs = []
-        for i in range(self.sections):
-            for d in range(self.dps):
-                own_x = (d >> 1) & 1
-                label = i ^ k
-                target = (label & ~1) | own_x
-                to = (d & ~2) | ((label & 1) << 1)
-                pairs.append((i * self.dps + d, target * self.dps + to))
-        return pairs
-
-    def collect(self, k):
-        return [(b, a) for a, b in self.spread(k)]
-
-    def other_core(self):
-        return [(d, d ^ 1) for d in range(self.dps)]
+def label_of(section):
+    return (section & ~3) | ((section & 1) << 1) | ((section >> 1) & 1)
+
+
+def by_label(k, sections):
+    return [(s, label_of(label_of(s) ^ k)) for s in range(sections)]
+
+
+def move(array, flip_x, flip_y, flip_z, sections, dps):
+    flip = flip_z * 2 + flip_y
+    pairs = [
+        (s * dps + d, (s ^ flip) * dps + (d ^ (flip_x * 2))) for s in range(sections) for d in range(dps)
+    ]
+    return lax.ppermute(array, AXES, pairs)
+
+
+def over_core(give, keep, dps):
+    return keep + lax.ppermute(give, "dp", [(d, d ^ 1) for d in range(dps)])
+
+
+def plane_parts(both, hop):
+    return hop(both[1, 0], 1, 0, 0), hop(both[0, 1], 0, 1, 0), hop(both[1, 1], 1, 1, 0)
+
+
+def plane_sum(both, parts):
+    return (both[0, 0].astype(F32) + parts[0] + parts[1] + parts[2]).astype(BF)
+
+
+def all_parts(total, hop):
+    return total, hop(total, 0, 1, 0), hop(total, 0, 0, 1), hop(total, 0, 1, 1)
+
+
+def in_order(pieces, y, r):
+    own, other_y, other_r, other_both = (p.astype(F32) for p in pieces)
+    low = jnp.where(y == 0, own, other_y), jnp.where(y == 0, other_y, own)
+    high = jnp.where(y == 0, other_r, other_both), jnp.where(y == 0, other_both, other_r)
+    pick = lambda a, b: jnp.where(r == 0, a, b)
+    return (
+        (pick(low[0], high[0]), pick(low[1], high[1])),
+        (pick(high[0], low[0]), pick(high[1], low[1])),
+    )
 
 
 def body(
@@ -331,30 +478,24 @@
     micro, _, piece_rows, width = tokens.shape
     rows = piece_rows * sections
     ff = expand_weight.shape[1]
-    places = Places(sections, dps)
-    core, own_x, high = dp & 1, (dp >> 1) & 1, dp >> 2
-    highs = dps // 4
-
-    ends = jnp.cumsum(lengths[:, 0], axis=-1).astype(BF)
-    slots = ends.shape[-1]
-    ends = jnp.pad(ends, ((0, 0), (0, 128 - slots)))
-    ends = jnp.broadcast_to(ends[:, None], (micro, piece_rows, 128))
-    sent = jnp.concatenate([tokens[:, 0], cotangent[:, 0], ends], axis=-1)
+    label = label_of(section)
+
+    sent = jnp.concatenate([tokens[:, 0], cotangent[:, 0]], axis=-1)
     got = []
     for k in range(sections):
-        block = lax.dynamic_index_in_dim(sent, (section ^ k) >> 1, 0, keepdims=False)
-        got.append(lax.ppermute(block, AXES, places.spread(k)))
-    label = (section & ~1) | own_x
-    shard = xor_order(jnp.stack(got), label).reshape(rows, -1)
-    x, cot = shard[:, :width], shard[:, width : 2 * width]
-    ends_here = shard[0, 2 * width : 2 * width + slots].astype(jnp.int32)
+        block = lax.dynamic_index_in_dim(sent, (label ^ k) >> 1, 0, keepdims=False)
+        got.append(block if k == 0 else lax.ppermute(block, "section", by_label(k, sections)))
+    shard = xor_order(jnp.stack(got), label)
+    shard = shard.reshape(sections // 4, 2, 2, piece_rows, 2 * width).swapaxes(1, 2).reshape(rows, 2 * width)
+    x, cot = shard[:, :width], shard[:, width:]
+    ends = jnp.cumsum(lax.dynamic_index_in_dim(lengths, label >> 1, 0, keepdims=False)[0])
 
     vec = jnp.stack(
         [first_gain, first_shift, out_bias, second_gain, second_shift, contract_bias, out_bias, out_bias]
     )
     qkvb = jnp.concatenate([qv_bias[:width], jnp.zeros((width,), F32), qv_bias[width:]])[None]
     first, n1, proj, probs, att, n2, second, slope, act, inv, last = forward_all(
-        ends_here, x, vec, expand_bias[None], qkvb,
+        ends, x, vec, expand_bias[None], qkvb,
         qkv_weight, out_weight, expand_weight, contract_weight, sections,
     )
     gproj, gattn, gpre, gmlp, gtok, sums = backward_all(
@@ -363,60 +504,88 @@
     )
 
     flat = lambda a: a.reshape(-1, a.shape[-1])
-
-    def own_half(left, right):
-        left, right = flat(left), flat(right)
-        cols = left.shape[1]
-        if highs == 1:
-            count = cols // 768
-            start = (own_x * count)[None].astype(jnp.int32)
-        else:
-            left = left.reshape(-1, highs, 2, 2, cols // dps)
-            left = lax.dynamic_index_in_dim(left, own_x, 2, keepdims=False).reshape(-1, cols // 2)
-            count, start = cols // 768, jnp.zeros((1,), jnp.int32)
-        out = outer(left, right, start, count)
-        return out.reshape(highs, 2, cols // dps, right.shape[1])
-
-    def vector_half(row):
-        parts = row.reshape(highs, 2, 2, -1)
-        return lax.dynamic_index_in_dim(parts, own_x, 1, keepdims=False)
-
-    small_sizes = [width, width, 2 * width, width, width, width, ff, width]
-    small = jnp.concatenate(
-        [vector_half(sums[i, :n]) for i, n in enumerate(small_sizes)], axis=-1
-    ).astype(BF)[:, :, None]
-    pieces = [own_half(first, gproj), own_half(att, gattn), own_half(second, gpre), own_half(act, gmlp), small]
-    totals = []
-    for part in pieces:
-        give = lax.dynamic_index_in_dim(part, 1 - core, 1, keepdims=False)
-        keep = lax.dynamic_index_in_dim(part, core, 1, keepdims=False)
-        part = keep + lax.ppermute(give, "dp", places.other_core())
-        if highs > 1:
-            groups = [[4 * h + low for h in range(highs)] for low in range(4)]
-            part = lax.psum_scatter(part, "dp", scatter_dimension=0, tiled=False, axis_index_groups=groups)
-        else:
-            part = part[0]
-        totals.append(lax.psum(part, "section").astype(F32))
-    g_qkv, g_out, g_exp, g_con, g_small = totals
-    g_small = g_small[0]
-    vectors, at = [], 0
-    for n in small_sizes:
-        vectors.append(g_small[at : at + n // dps])
-        at += n // dps
-
+    first, att, second, act = flat(first), flat(att), flat(second), flat(act)
+    gproj, gattn, gpre, gmlp = flat(gproj), flat(gattn), flat(gpre), flat(gmlp)
     both = jnp.concatenate([last, gtok], axis=1).reshape(sections, piece_rows, 2 * width)
-    back = []
-    for k in range(0, sections, 2):
-        block = lax.dynamic_index_in_dim(both, label ^ k, 0, keepdims=False)
-        pairs = [p for p in places.collect(k)]
-        back.append(lax.ppermute(block, AXES, pairs))
-    back = xor_order(jnp.stack(back), section >> 1)
+    blocks = [
+        lax.dynamic_index_in_dim(both, label_of(label ^ k), 0, keepdims=False) for k in range(0, sections, 2)
+    ]
+    if (sections, dps) == (8, 4):
+        g_qkv, g_out, g_exp, g_con, v, back = grads_small_slice(
+            section, dp, first, att, second, act, gproj, gattn, gpre, gmlp, sums, blocks
+        )
+    else:
+        half = (label & 1) == 0
+
+        def everywhere(whole):
+            whole = jnp.where(half, whole, 0.0).astype(BF)
+            own = lax.psum_scatter(whole, "dp", scatter_dimension=0, tiled=True)
+            return lax.psum(own, "section").astype(F32)
+
+        g_qkv, g_out = everywhere(tn(first, gproj)), everywhere(tn(att, gattn))
+        g_exp, g_con = everywhere(tn(second, gpre)), everywhere(tn(act, gmlp))
+        v = [everywhere(sums[i, :n]) for i, n in enumerate([width] * 6 + [2 * width, ff])]
+        back = blocks[:1] + [
+            lax.ppermute(block, "section", by_label(2 * i + 2, sections)) for i, block in enumerate(blocks[1:])
+        ]
+
+    back = xor_order(jnp.stack(back), label >> 1)
     result = back[:, None, :, :width]
     grad_tokens = back[:, None, :, width:].astype(F32)
     return (
-        result, grad_tokens, vectors[0], vectors[1], g_qkv, vectors[2], g_out, vectors[3],
-        vectors[4], vectors[5], g_exp, vectors[6], g_con, vectors[7],
-    )
+        result, grad_tokens, v[0], v[1], g_qkv, v[6], g_out, v[2], v[3], v[4], g_exp, v[7], g_con, v[5],
+    )
+
+
+def grads_small_slice(section, dp, first, att, second, act, gproj, gattn, gpre, gmlp, sums, blocks):
+    sections, dps = 8, 4
+    y, r, x, core = section & 1, (section >> 1) & 1, dp >> 1, dp & 1
+    spot = jnp.stack([x, core, y, r]).astype(jnp.int32)
+    width, ff = first.shape[1], act.shape[1]
+    hop = partial(move, sections=sections, dps=dps)
+    cols = 2 * width
+    tall = width // 8
+    tie = lax.optimization_barrier
+    add_a = over_core(*contract_grads(spot, act, gmlp), dps)
+    second, gpre, add_a = tie((second, gpre, add_a))
+    from_a, out_b = plane_parts(add_a, hop), expand_grads(spot, second, gpre)
+    from_a, out_b = tie((from_a, out_b))
+    plane_a = plane_sum(add_a, from_a)
+    z_a, add_b = hop(plane_a, 0, 0, 2), over_core(*out_b, dps)
+    first, gproj, att, gattn, add_b = tie((first, gproj, att, gattn, add_b))
+    from_b, out_c = plane_parts(add_b, hop), attention_grads(spot, first, gproj, att, gattn, sums)
+    from_b, out_c, z_a = tie((from_b, out_c, z_a))
+    plane_b, total_a = plane_sum(add_b, from_b), plane_a + z_a
+    z_b = hop(jnp.concatenate([plane_b, blocks[2], blocks[3]], axis=0), 0, 0, 2)
+    y_a, add_c = hop(total_a, 0, 1, 0), over_core(*out_c, dps)
+    from_c = plane_parts(add_c, hop)
+    from_c, z_b, y_a = tie((from_c, z_b, y_a))
+    pieces = z_b.shape[0] - tall
+    z_b, from_z, through_z = z_b[:tall], z_b[tall : tall + pieces // 2], z_b[tall + pieces // 2 :]
+    plane_c, total_b = plane_sum(add_c, from_c), plane_b + z_b
+    z_c = hop(plane_c, 0, 0, 2)
+    y_b = hop(jnp.concatenate([total_b, blocks[1], through_z], axis=0), 0, 1, 0)
+    far_a = hop(jnp.stack([total_a, y_a]), 0, 0, 1)
+    z_c, y_b, far_a = tie((z_c, y_b, far_a))
+    y_b, from_y, from_both = y_b[:tall], y_b[tall : tall + pieces // 2], y_b[tall + pieces // 2 :]
+    back = [blocks[0], from_y, from_z, from_both]
+    total_c = plane_c + z_c
+    rest = all_parts(total_c, hop)
+    far_b = hop(jnp.stack([total_b, y_b]), 0, 0, 1)
+    con, exp = (total_a, y_a, far_a[0], far_a[1]), (total_b, y_b, far_b[0], far_b[1])
+    con, exp, att_part = in_order(con, y, r), in_order(exp, y, r), in_order([p[:tall] for p in rest], y, r)
+    g_con = jnp.concatenate([con[0][0], con[0][1], con[1][0], con[1][1]], axis=0)
+    g_exp = jnp.concatenate([jnp.concatenate([exp[0][j], exp[1][j]], axis=1) for j in (0, 1)], axis=0)
+    wide = gproj.shape[1] // 2
+    side = lambda a, b: jnp.concatenate(
+        [jnp.concatenate([att_part[0][j][:, a:b], att_part[1][j][:, a:b]], axis=1) for j in (0, 1)], axis=0
+    )
+    vectors = rest[0][tall:].astype(F32)
+    windows = vectors[0].reshape(6, -1)
+    quarter = width // 4
+    windows = jnp.where(core == 0, windows[:, :quarter], windows[:, 64 : 64 + quarter])
+    v = [windows[i] for i in range(6)] + [vectors[1, : 2 * quarter], vectors[1, 2 * quarter : 2 * quarter + ff // 4]]
+    return side(0, wide), side(wide, cols), g_exp, g_con, v, back
 
 
 def solution(mesh):

time: 360 us -> 277 us (0.77)
  waiting for transfers between devices: 111 us -> 75.5 us
  blocking collectives: 25.8 us -> 0 us
  local copies, waits for them, and re-layouts: 54.3 us -> 35.3 us
  between operations: 14.4 us -> 1.03 us
  starting transfers between devices: 23.9 us -> 35.7 us
    psum x1 -> x0, waiting for transfers between devices: 107 us -> none  [body(): totals.append(lax.psum(part, 'section').astype(F32))]
    ppermute x17 -> x29, waiting for transfers between devices: 3.61 us -> 75.5 us  [the longest x19 65.1 us: move(): return lax.ppermute(array, AXES, pairs)]
    psum x1 -> x0, blocking collectives: 25.8 us -> none  [body(): totals.append(lax.psum(part, 'section').astype(F32))]
    ppermute x17 -> x29, starting transfers between devices: 23.9 us -> 35.7 us  [the longest x19 23.2 us: move(): return lax.ppermute(array, AXES, pairs)]
    squeeze x7 -> x3, local copies, waits for them, and re-layouts: 8.55 us -> 0.93 us  [plane_parts(): both[1, 1]]
    squeeze x5 -> x2, other arithmetic: 9.12 us -> 1.73 us  [body(): block = lax.dynamic_index_in_dim(sent, (label ^ k) >> 1, 0, keepdims=False)]
    convert_element_type x7 -> x4, other arithmetic: 7.32 us -> 1.66 us  [the longest x3 1.65 us: plane_sum(): return (both[0, 0].astype(F32) + parts[0] + parts[1] + parts[2]).astype(BF)]
    concatenate x1 -> x6, other arithmetic: 0.96 us -> 5.39 us  [the longest x2 2.18 us: grads_small_slice(): jnp.concatenate([jnp.concatenate([att_part[0][j][:, a:b], att_part[1][j][...]
  transfers between devices with their start and end apart: 18 -> 29, of which waited for: 2 -> 14; matrix products, arithmetic and copies ran while one was open for 16% -> 16% of each run, Pallas kernels for 4% -> 5%
where the time goes in v2:
time: 277 us; the launch traced here: 276 us
  Pallas kernels  110 us (40%)
  waiting for transfers between devices  75.5 us (27%)
  starting transfers between devices  35.7 us (13%)
  local copies, waits for them, and re-layouts  35.3 us (13%)
  other arithmetic  17.8 us (6%)
    ppermute x19, waiting for transfers between devices, move(): return lax.ppermute(array, AXES, pairs)  65.1 us
    pallas_call x1, Pallas kernels, backward_all(): pl.pallas_call(backward_kernel, grid=(layers,), in_specs=[whole_spec(a.sh...  45.8 us
    pallas_call x1, Pallas kernels, forward_all(): pl.pallas_call(forward_kernel, grid_spec=pltpu.PrefetchScalarGridSpec(num...  42.1 us
    ppermute x19, starting transfers between devices, move(): return lax.ppermute(array, AXES, pairs)  23.2 us
    unnamed x20, local copies, waits for them, and re-layouts  21.5 us
    ppermute x7, starting transfers between devices, body(): lax.ppermute(block, 'section', by_label(k, sections))  12.4 us
    pallas_call x1, Pallas kernels, attention_grads(): pl.pallas_call(attention_kernel, grid_spec=pltpu.PrefetchScalarGridSpec(n...  8.2 us
    pallas_call x1, Pallas kernels, contract_grads(): pl.pallas_call(contract_kernel, grid_spec=pltpu.PrefetchScalarGridSpec(nu...  7.43 us
  transfers between devices with their start and end apart: 29, of which 14 were waited for; matrix products, arithmetic and copies ran while one was open for 16% of the time, Pallas kernels for 5%

profile of v2, /device:TPU:0, one launch (start us, length us, event | category | flops | bytes accessed | tf_op | source)
XLA Modules:
  0.0 275.6 jit_solution(1893067213756818470)
XLA Ops:
  0.7 0.8 fusion.42
  1.5 5.0 %collective-permute-start.5 = (bf16[16,1536]{1,0:T(8,128)(2,1)S(1)}, bf16[16,1536]{1,0:T(8,128)(2,1)S(1)}, u32[]{:S(2)}, u32[]{:S(2)}) collective-permute-start(bf16[16,1536]{1,0:T(8,128)(2,1)S(1)} %get-tuple-element.153), channel_id=1, source_target_pairs={{0,20},{4,16},{8,28},{12,24},{16,4},{20,0},{24,12},{28,8},{1,21},{... | collective-permute-start | bytes 147464 | tf_op jit(solution)/shard_map/ppermute | solution.py:487
  6.5 1.3 collective-permute-start.4
  7.9 0.9 fusion.28
  8.8 2.5 collective-permute-start.6
  11.3 1.5 collective-permute-start.1
  19.6 2.4 copy.35
  22.0 5.7 %copy.34 = bf16[768,2304]{0,1:T(8,128)(2,1)} copy(bf16[768,2304]{1,0:T(8,128)(2,1)} %wq_ref.1) | data formatting | bytes 7077888 | tf_op args[5]
  27.8 6.7 %copy.36 = bf16[768,3072]{0,1:T(8,128)(2,1)} copy(bf16[768,3072]{1,0:T(8,128)(2,1)} %we_ref.1) | data formatting | bytes 9437184 | tf_op args[11]
  34.4 6.6 %copy.37 = bf16[3072,768]{0,1:T(8,128)(2,1)} copy(bf16[3072,768]{1,0:T(8,128)(2,1)} %wc_ref.1) | data formatting | bytes 9437184 | tf_op args[13]
  41.7 2.0 collective-permute-start.2
  43.8 3.5 %collective-permute-done.2 = bf16[16,1536]{1,0:T(8,128)(2,1)S(1)} collective-permute-done((bf16[16,1536]{1,0:T(8,128)(2,1)S(1)}, bf16[16,1536]{1,0:T(8,128)(2,1)S(1)}, u32[]{:S(2)}, u32[]{:S(2)}) %collective-permute-start.2) | collective-permute-done | bytes 49184 | tf_op jit(solution)/shard_map/ppermute | solution.py:487
  47.2 1.5 collective-permute-done.3
  49.9 42.1 %shard_map.254 = (bf16[8,128,768]{2,1,0:T(8,128)(2,1)}, bf16[8,128,768]{2,1,0:T(8,128)(2,1)}, bf16[8,128,2304]{2,1,0:T(8,128)(2,1)}, bf16[8,1536,128]{2,1,0:T(8,...) custom-call(s32[4]{0:T(128)} %bitcast.175, ...), custom_call_target="tpu_custom_call" | custom-call | tf_op jit(solution)/shard_map/pallas_call | solution.py:227
  92.0 45.8 %shard_map.255 = (bf16[8,128,2304]{2,1,0:T(8,128)(2,1)}, bf16[8,128,768]{2,1,0:T(8,128)(2,1)}, bf16[8,128,3072]{2,1,0:T(8,128)(2,1)}, bf16[8,128,768]{2,1,0:T(8,...) custom-call(bf16[128,768]{1,0:T(8,128)(2,1)} %get-tuple-element.143.cot_ref, f32[8,768]{1,0:T(8,128)} %stack.108.vec_ref, ...), custom_call_target="tpu_custom_call" | custom-call | tf_op jit(solution)/shard_map/pallas_call | solution.py:248
  137.8 7.4 %shard_map.256 = (bf16[2,2,192,768]{3,2,1,0:T(8,128)(2,1)}, bf16[2,2,192,768]{3,2,1,0:T(8,128)(2,1)}) custom-call(s32[4]{0:T(128)} %pad_add_fusion.spot_ref, bf16[1024,3072]{1,0:T(8,128)(2,1)} %bitcast.177, bf16[1024,768]{1,0:T(8,128)(2,1)} %bitcast.179), custom_call_target="tpu_custom_call" | custom-call | flops 2415919104 | bytes 7077888 | tf_op jit(solution)/shard_map/pallas_call | solution.py:341
  145.3 3.1 %collective-permute-done.7 = bf16[2,2,192,768]{3,2,1,0:T(8,128)(2,1)S(1)} collective-permute-done((bf16[2,2,192,768]{3,2,1,0:T(8,128)(2,1)}, bf16[2,2,192,768]{3,2,1,0:T(8,128)(2,1)S(1)}, u32[]{:S(2)}, u32[]{:S(2)}) %collective-permute-start.7) | collective-permute-done | bytes 1179680 | tf_op jit(solution)/shard_map/ppermute | solution.py:446
  148.3 1.5 add.94
  149.9 2.5 collective-permute-start.10
  153.5 6.8 %shard_map.257 = (bf16[2,2,96,1536]{3,2,1,0:T(8,128)(2,1)}, bf16[2,2,96,1536]{3,2,1,0:T(8,128)(2,1)}) custom-call(s32[4]{0:T(128)} %pad_add_fusion.spot_ref, bf16[1024,768]{1,0:T(8,128)(2,1)} %bitcast.178, bf16[1024,3072]{1,0:T(8,128)(2,1)} %bitcast.176), custom_call_target="tpu_custom_call" | custom-call | flops 2415919104 | bytes 7077888 | tf_op jit(solution)/shard_map/pallas_call | solution.py:291
  160.8 5.5 %collective-permute-done.9 = bf16[192,768]{1,0:T(8,128)(2,1)S(1)} collective-permute-done((bf16[192,768]{1,0:T(8,128)(2,1)S(1)}, bf16[192,768]{1,0:T(8,128)(2,1)S(1)}, u32[]{:S(2)}, u32[]{:S(2)}) %collective-permute-start.9) | collective-permute-done | bytes 294944 | tf_op jit(solution)/shard_map/ppermute | solution.py:442
  167.1 2.3 collective-permute-done.11
  169.7 0.8 slice_bitcast_fusion.4
  170.5 1.7 collective-permute-start.14
  172.2 1.3 collective-permute-start.13
  174.0 8.2 %shard_map.258 = (bf16[2,2,112,1536]{3,2,1,0:T(8,128)(2,1)}, bf16[2,2,112,1536]{3,2,1,0:T(8,128)(2,1)}) custom-call(s32[4]{0:T(128)} %pad_add_fusion.spot_ref, bf16[1024,768]{1,0:T(8,128)(2,1)} %bitcast.152, bf16[1024,2304]{1,0:T(8,128)(2,1)} %bitcast.149, bf16[1024,768]{1,0:T(8,128)(2,1)} %bitcast.153, bf16[1024,768]{1,0:T(8,128)(2,1)} %bitcast.154, ...), custom_call_target="tpu_custom_call" | custom-call | flops 2415919104 | bytes 7077888 | tf_op jit(solution)/shard_map/pallas_call | solution.py:400
  182.6 4.4 %collective-permute-done.13 = bf16[96,1536]{1,0:T(8,128)(2,1)} collective-permute-done((bf16[96,1536]{1,0:T(8,128)(2,1)S(1)}, bf16[96,1536]{1,0:T(8,128)(2,1)}, u32[]{:S(2)}, u32[]{:S(2)}) %collective-permute-start.13) | collective-permute-done | bytes 294944 | tf_op jit(solution)/shard_map/ppermute | solution.py:442
  187.1 1.0 pad_maximum_fusion.3
  188.8 1.3 fusion.9
  190.8 1.8 add.99
  192.6 1.6 collective-permute-start.19
  194.2 1.4 collective-permute-start.18
  196.3 1.5 collective-permute-start.21
  197.8 19.7 %collective-permute-done.21 = bf16[192,768]{1,0:T(8,128)(2,1)S(1)} collective-permute-done((bf16[192,768]{1,0:T(8,128)(2,1)S(1)}, bf16[192,768]{1,0:T(8,128)(2,1)S(1)}, u32[]{:S(2)}, u32[]{:S(2)}) %collective-permute-start.21) | collective-permute-done | bytes 294944 | tf_op jit(solution)/shard_map/ppermute | solution.py:442
  218.2 1.5 collective-permute-start.23
  219.7 1.9 collective-permute-start.24
  222.5 19.1 %collective-permute-done.22 = bf16[112,1536]{1,0:T(8,128)(2,1)S(1)} collective-permute-done((bf16[112,1536]{1,0:T(8,128)(2,1)S(1)}, bf16[112,1536]{1,0:T(8,128)(2,1)S(1)}, u32[]{:S(2)}, u32[]{:S(2)}) %collective-permute-start.22) | collective-permute-done | bytes 344096 | tf_op jit(solution)/shard_map/ppermute | solution.py:442
  244.3 2.3 collective-permute-start.27
  246.7 1.4 collective-permute-start.25
  249.5 2.1 collective-permute-start.28
  251.6 0.9 pad_maximum_fusion.6
  252.8 1.6 pad_maximum_fusion
  254.4 1.3 slice_reduce_fusion.2
  256.4 6.6 %collective-permute-done.26 = bf16[112,1536]{1,0:T(8,128)(2,1)S(1)} collective-permute-done((bf16[112,1536]{1,0:T(8,128)(2,1)S(1)}, bf16[112,1536]{1,0:T(8,128)(2,1)S(1)}, u32[]{:S(2)}, u32[]{:S(2)}) %collective-permute-start.26) | collective-permute-done | bytes 344096 | tf_op jit(solution)/shard_map/ppermute | solution.py:442
  263.5 0.9 maximum_maximum_fusion.2
  264.3 1.3 maximum_maximum_fusion.1
  265.7 8.1 %collective-permute-done.28 = bf16[2,96,1536]{2,1,0:T(8,128)(2,1)S(1)} collective-permute-done((bf16[2,96,1536]{2,1,0:T(8,128)(2,1)S(1)}, bf16[2,96,1536]{2,1,0:T(8,128)(2,1)S(1)}, u32[]{:S(2)}, u32[]{:S(2)}) %collective-permute-start.28) | collective-permute-done | bytes 589856 | tf_op jit(solution)/shard_map/ppermute | solution.py:442
  274.0 1.6 maximum_maximum_fusion
  (104 shorter events, 21.8 us)
Async XLA Ops:
  0.6 12.2 %copy-start = (s32[4,1,4]{2,1,0:T(1,128)S(1)}, s32[4,1,4]{2,1,0:T(1,128)}, u32[]{:S(2)}) copy-start(s32[4,1,4]{2,1,0:T(1,128)} %param.16) | copy-start | bytes 196
  1.5 47.3 %collective-permute-start.5 = (bf16[16,1536]{1,0:T(8,128)(2,1)S(1)}, bf16[16,1536]{1,0:T(8,128)(2,1)S(1)}, u32[]{:S(2)}, u32[]{:S(2)}) collective-permute-start(bf16[16,1536]{1,0:T(8,128)(2,1)S(1)} %get-tuple-element.153), channel_id=1, source_target_pairs={{0,20},{4,16},{8,28},{12,24},{16,4},{20,0},{24,12},{28,8},{1,21},{... | collective-permute-start | bytes 147464 | tf_op jit(solution)/shard_map/ppermute | solution.py:487
  6.5 42.3 %collective-permute-start.4 = (bf16[16,1536]{1,0:T(8,128)(2,1)S(1)}, bf16[16,1536]{1,0:T(8,128)(2,1)S(1)}, u32[]{:S(2)}, u32[]{:S(2)}) collective-permute-start(bf16[16,1536]{1,0:T(8,128)(2,1)S(1)} %get-tuple-element.154), channel_id=1, source_target_pairs={{0,24},{4,28},{8,16},{12,20},{16,8},{20,12},{24,0},{28,4},{1,25},{... | collective-permute-start | bytes 147464 | tf_op jit(solution)/shard_map/ppermute | solution.py:487
  8.8 40.0 %collective-permute-start.6 = (bf16[16,1536]{1,0:T(8,128)(2,1)S(1)}, bf16[16,1536]{1,0:T(8,128)(2,1)S(1)}, u32[]{:S(2)}, u32[]{:S(2)}) collective-permute-start(bf16[16,1536]{1,0:T(8,128)(2,1)S(1)} %get-tuple-element.147), channel_id=1, source_target_pairs={{0,28},{4,24},{8,20},{12,16},{16,12},{20,8},{24,4},{28,0},{1,29},{... | collective-permute-start | bytes 147464 | tf_op jit(solution)/shard_map/ppermute | solution.py:487
  11.3 30.4 %collective-permute-start = (bf16[16,1536]{1,0:T(8,128)(2,1)S(1)}, bf16[16,1536]{1,0:T(8,128)(2,1)S(1)}, u32[]{:S(2)}, u32[]{:S(2)}) collective-permute-start(bf16[16,1536]{1,0:T(8,128)(2,1)S(1)} %get-tuple-element.149), channel_id=1, source_target_pairs={{0,8},{4,12},{8,0},{12,4},{16,24},{20,28},{24,16},{28,20},{1,9},{5... | collective-permute-start | bytes 147464 | tf_op jit(solution)/shard_map/ppermute | solution.py:487
  11.3 32.4 %collective-permute-start.1 = (bf16[16,1536]{1,0:T(8,128)(2,1)S(1)}, bf16[16,1536]{1,0:T(8,128)(2,1)S(1)}, u32[]{:S(2)}, u32[]{:S(2)}) collective-permute-start(bf16[16,1536]{1,0:T(8,128)(2,1)S(1)} %get-tuple-element.150), channel_id=1, source_target_pairs={{0,4},{4,0},{8,12},{12,8},{16,20},{20,16},{24,28},{28,24},{1,5},{5... | collective-permute-start | bytes 147464 | tf_op jit(solution)/shard_map/ppermute | solution.py:487
  41.7 5.5 %collective-permute-start.2 = (bf16[16,1536]{1,0:T(8,128)(2,1)S(1)}, bf16[16,1536]{1,0:T(8,128)(2,1)S(1)}, u32[]{:S(2)}, u32[]{:S(2)}) collective-permute-start(bf16[16,1536]{1,0:T(8,128)(2,1)S(1)} %get-tuple-element.151), channel_id=1, source_target_pairs={{0,12},{4,8},{8,4},{12,0},{16,28},{20,24},{24,20},{28,16},{1,13},{... | collective-permute-start | bytes 147464 | tf_op jit(solution)/shard_map/ppermute | solution.py:487
  43.7 5.1 %collective-permute-start.3 = (bf16[16,1536]{1,0:T(8,128)(2,1)S(1)}, bf16[16,1536]{1,0:T(8,128)(2,1)S(1)}, u32[]{:S(2)}, u32[]{:S(2)}) collective-permute-start(bf16[16,1536]{1,0:T(8,128)(2,1)S(1)} %get-tuple-element.152), channel_id=1, source_target_pairs={{0,16},{4,20},{8,24},{12,28},{16,0},{20,4},{24,8},{28,12},{1,17},{... | collective-permute-start | bytes 147464 | tf_op jit(solution)/shard_map/ppermute | solution.py:487
  145.3 3.1 %collective-permute-start.7 = (bf16[2,2,192,768]{3,2,1,0:T(8,128)(2,1)}, bf16[2,2,192,768]{3,2,1,0:T(8,128)(2,1)S(1)}, u32[]{:S(2)}, u32[]{:S(2)}) collective-permute-start(bf16[2,2,192,768]{3,2,1,0:T(8,128)(2,1)} %get-tuple-element.81), channel_id=1, source_target_pairs={{0,1},{1,0},{2,3},{3,2},{4,5},{5,4},{6,7},{7,6},{8,9},{9,8},{10,11... | collective-permute-start | bytes 3538952 | tf_op jit(solution)/shard_map/ppermute | solution.py:446
  149.9 10.9 %collective-permute-start.10 = (bf16[192,768]{1,0:T(8,128)(2,1)S(1)}, bf16[192,768]{1,0:T(8,128)(2,1)S(1)}, u32[]{:S(2)}, u32[]{:S(2)}) collective-permute-start(bf16[192,768]{1,0:T(8,128)(2,1)S(1)} %get-tuple-element.132), channel_id=1, source_target_pairs={{0,6},{1,7},{2,4},{3,5},{4,2},{5,3},{6,0},{7,1},{8,14},{9,15},{10,... | collective-permute-start | bytes 884744 | tf_op jit(solution)/shard_map/ppermute | solution.py:442
  152.4 13.9 %collective-permute-start.9 = (bf16[192,768]{1,0:T(8,128)(2,1)S(1)}, bf16[192,768]{1,0:T(8,128)(2,1)S(1)}, u32[]{:S(2)}, u32[]{:S(2)}) collective-permute-start(bf16[192,768]{1,0:T(8,128)(2,1)S(1)} %get-tuple-element.133), channel_id=1, source_target_pairs={{0,4},{1,5},{2,6},{3,7},{4,0},{5,1},{6,2},{7,3},{8,12},{9,13},{10,... | collective-permute-start | bytes 884744 | tf_op jit(solution)/shard_map/ppermute | solution.py:442
  153.0 13.4 %collective-permute-start.8 = (bf16[192,768]{1,0:T(8,128)(2,1)S(1)}, bf16[192,768]{1,0:T(8,128)(2,1)S(1)}, u32[]{:S(2)}, u32[]{:S(2)}) collective-permute-start(bf16[192,768]{1,0:T(8,128)(2,1)S(1)} %get-tuple-element.134), channel_id=1, source_target_pairs={{0,2},{1,3},{2,0},{3,1},{4,6},{5,7},{6,4},{7,5},{8,10},{9,11},{10,... | collective-permute-start | bytes 884744 | tf_op jit(solution)/shard_map/ppermute | solution.py:442
  160.3 9.1 %copy-start.3 = (bf16[2,2,96,1536]{3,2,1,0:T(8,128)(2,1)S(1)}, bf16[2,2,96,1536]{3,2,1,0:T(8,128)(2,1)}, u32[]{:S(2)}) copy-start(bf16[2,2,96,1536]{3,2,1,0:T(8,128)(2,1)} %get-tuple-element.87) | copy-start | bytes 3538948
  166.3 3.1 %collective-permute-start.11 = (bf16[2,2,96,1536]{3,2,1,0:T(8,128)(2,1)}, bf16[2,2,96,1536]{3,2,1,0:T(8,128)(2,1)S(1)}, u32[]{:S(2)}, u32[]{:S(2)}) collective-permute-start(bf16[2,2,96,1536]{3,2,1,0:T(8,128)(2,1)} %get-tuple-element.88), channel_id=1, source_target_pairs={{0,1},{1,0},{2,3},{3,2},{4,5},{5,4},{6,7},{7,6},{8,9},{9,8},{10,11... | collective-permute-start | bytes 3538952 | tf_op jit(solution)/shard_map/ppermute | solution.py:446
  166.5 16.1 %collective-permute-start.15 = (bf16[192,768]{1,0:T(8,128)(2,1)S(1)}, bf16[192,768]{1,0:T(8,128)(2,1)S(1)}, u32[]{:S(2)}, u32[]{:S(2)}) collective-permute-start(bf16[192,768]{1,0:T(8,128)(2,1)S(1)} %fusion.12), channel_id=1, source_target_pairs={{0,16},{1,17},{2,18},{3,19},{4,20},{5,21},{6,22},{7,23},{8,24},{9,... | collective-permute-start | bytes 884744 | tf_op jit(solution)/shard_map/ppermute | solution.py:442
  170.5 12.2 %collective-permute-start.14 = (bf16[96,1536]{1,0:T(8,128)(2,1)}, bf16[96,1536]{1,0:T(8,128)(2,1)}, u32[]{:S(2)}, u32[]{:S(2)}) collective-permute-start(bf16[96,1536]{1,0:T(8,128)(2,1)} %get-tuple-element.129), channel_id=1, source_target_pairs={{0,6},{1,7},{2,4},{3,5},{4,2},{5,3},{6,0},{7,1},{8,14},{9,15},{10,... | collective-permute-start | bytes 884744 | tf_op jit(solution)/shard_map/ppermute | solution.py:442
  172.2 14.9 %collective-permute-start.13 = (bf16[96,1536]{1,0:T(8,128)(2,1)S(1)}, bf16[96,1536]{1,0:T(8,128)(2,1)}, u32[]{:S(2)}, u32[]{:S(2)}) collective-permute-start(bf16[96,1536]{1,0:T(8,128)(2,1)S(1)} %get-tuple-element.130), channel_id=1, source_target_pairs={{0,4},{1,5},{2,6},{3,7},{4,0},{5,1},{6,2},{7,3},{8,12},{9,13},{10,... | collective-permute-start | bytes 884744 | tf_op jit(solution)/shard_map/ppermute | solution.py:442
  173.4 13.6 %collective-permute-start.12 = (bf16[96,1536]{1,0:T(8,128)(2,1)S(1)}, bf16[96,1536]{1,0:T(8,128)(2,1)}, u32[]{:S(2)}, u32[]{:S(2)}) collective-permute-start(bf16[96,1536]{1,0:T(8,128)(2,1)S(1)} %get-tuple-element.131), channel_id=1, source_target_pairs={{0,2},{1,3},{2,0},{3,1},{4,6},{5,7},{6,4},{7,5},{8,10},{9,11},{10,... | collective-permute-start | bytes 884744 | tf_op jit(solution)/shard_map/ppermute | solution.py:442
  182.2 8.6 %copy-start.2 = (bf16[2,2,112,1536]{3,2,1,0:T(8,128)(2,1)S(1)}, bf16[2,2,112,1536]{3,2,1,0:T(8,128)(2,1)}, u32[]{:S(2)}) copy-start(bf16[2,2,112,1536]{3,2,1,0:T(8,128)(2,1)} %get-tuple-element.100) | copy-start | bytes 4128772
  187.1 3.7 %collective-permute-start.16 = (bf16[2,2,112,1536]{3,2,1,0:T(8,128)(2,1)}, bf16[2,2,112,1536]{3,2,1,0:T(8,128)(2,1)}, u32[]{:S(2)}, u32[]{:S(2)}) collective-permute-start(bf16[2,2,112,1536]{3,2,1,0:T(8,128)(2,1)} %get-tuple-element.101), channel_id=1, source_target_pairs={{0,1},{1,0},{2,3},{3,2},{4,5},{5,4},{6,7},{7,6},{8,9},{9,8},{10,11... | collective-permute-start | bytes 4128776 | tf_op jit(solution)/shard_map/ppermute | solution.py:446
  190.1 27.3 %collective-permute-start.20 = (bf16[128,1536]{1,0:T(8,128)(2,1)S(1)}, bf16[128,1536]{1,0:T(8,128)(2,1)S(1)}, u32[]{:S(2)}, u32[]{:S(2)}) collective-permute-start(bf16[128,1536]{1,0:T(8,128)(2,1)S(1)} %pad_maximum_fusion.4), channel_id=1, source_target_pairs={{0,16},{1,17},{2,18},{3,19},{4,20},{5,21},{6,22},{7,23},{8,24},{9,... | collective-permute-start | bytes 1179656 | tf_op jit(solution)/shard_map/ppermute | solution.py:442
  192.6 24.8 %collective-permute-start.19 = (bf16[112,1536]{1,0:T(8,128)(2,1)S(1)}, bf16[112,1536]{1,0:T(8,128)(2,1)S(1)}, u32[]{:S(2)}, u32[]{:S(2)}) collective-permute-start(bf16[112,1536]{1,0:T(8,128)(2,1)S(1)} %get-tuple-element.118), channel_id=1, source_target_pairs={{0,6},{1,7},{2,4},{3,5},{4,2},{5,3},{6,0},{7,1},{8,14},{9,15},{10,... | collective-permute-start | bytes 1032200 | tf_op jit(solution)/shard_map/ppermute | solution.py:442
  194.2 23.3 %collective-permute-start.18 = (bf16[112,1536]{1,0:T(8,128)(2,1)S(1)}, bf16[112,1536]{1,0:T(8,128)(2,1)S(1)}, u32[]{:S(2)}, u32[]{:S(2)}) collective-permute-start(bf16[112,1536]{1,0:T(8,128)(2,1)S(1)} %get-tuple-element.119), channel_id=1, source_target_pairs={{0,4},{1,5},{2,6},{3,7},{4,0},{5,1},{6,2},{7,3},{8,12},{9,13},{10,... | collective-permute-start | bytes 1032200 | tf_op jit(solution)/shard_map/ppermute | solution.py:442
  195.7 21.8 %collective-permute-start.17 = (bf16[112,1536]{1,0:T(8,128)(2,1)S(1)}, bf16[112,1536]{1,0:T(8,128)(2,1)S(1)}, u32[]{:S(2)}, u32[]{:S(2)}) collective-permute-start(bf16[112,1536]{1,0:T(8,128)(2,1)S(1)} %get-tuple-element.120), channel_id=1, source_target_pairs={{0,2},{1,3},{2,0},{3,1},{4,6},{5,7},{6,4},{7,5},{8,10},{9,11},{10,... | collective-permute-start | bytes 1032200 | tf_op jit(solution)/shard_map/ppermute | solution.py:442
  196.3 21.2 %collective-permute-start.21 = (bf16[192,768]{1,0:T(8,128)(2,1)S(1)}, bf16[192,768]{1,0:T(8,128)(2,1)S(1)}, u32[]{:S(2)}, u32[]{:S(2)}) collective-permute-start(bf16[192,768]{1,0:T(8,128)(2,1)S(1)} %add.105), channel_id=1, source_target_pairs={{0,4},{1,5},{2,6},{3,7},{4,0},{5,1},{6,2},{7,3},{8,12},{9,13},{10,... | collective-permute-start | bytes 884744 | tf_op jit(solution)/shard_map/ppermute | solution.py:442
  218.2 23.4 %collective-permute-start.23 = (bf16[128,1536]{1,0:T(8,128)(2,1)S(1)}, bf16[128,1536]{1,0:T(8,128)(2,1)S(1)}, u32[]{:S(2)}, u32[]{:S(2)}) collective-permute-start(bf16[128,1536]{1,0:T(8,128)(2,1)S(1)} %pad_maximum_fusion.5), channel_id=1, source_target_pairs={{0,4},{1,5},{2,6},{3,7},{4,0},{5,1},{6,2},{7,3},{8,12},{9,13},{10,... | collective-permute-start | bytes 1179656 | tf_op jit(solution)/shard_map/ppermute | solution.py:442
  219.7 22.5 %collective-permute-start.24 = (bf16[2,192,768]{2,1,0:T(8,128)(2,1)S(1)}, bf16[2,192,768]{2,1,0:T(8,128)(2,1)S(1)}, u32[]{:S(2)}, u32[]{:S(2)}) collective-permute-start(bf16[2,192,768]{2,1,0:T(8,128)(2,1)S(1)} %pad_maximum_fusion.1), channel_id=1, source_target_pairs={{0,8},{1,9},{2,10},{3,11},{4,12},{5,13},{6,14},{7,15},{8,0},{9,1},... | collective-permute-start | bytes 1769480 | tf_op jit(solution)/shard_map/ppermute | solution.py:442
  221.9 19.7 %collective-permute-start.22 = (bf16[112,1536]{1,0:T(8,128)(2,1)S(1)}, bf16[112,1536]{1,0:T(8,128)(2,1)S(1)}, u32[]{:S(2)}, u32[]{:S(2)}) collective-permute-start(bf16[112,1536]{1,0:T(8,128)(2,1)S(1)} %fusion.2), channel_id=1, source_target_pairs={{0,16},{1,17},{2,18},{3,19},{4,20},{5,21},{6,22},{7,23},{8,24},{9,... | collective-permute-start | bytes 1032200 | tf_op jit(solution)/shard_map/ppermute | solution.py:442
  242.4 1.2 copy-start.4
  244.3 12.1 %collective-permute-start.27 = (bf16[112,1536]{1,0:T(8,128)(2,1)S(1)}, bf16[112,1536]{1,0:T(8,128)(2,1)S(1)}, u32[]{:S(2)}, u32[]{:S(2)}) collective-permute-start(bf16[112,1536]{1,0:T(8,128)(2,1)S(1)} %add.111), channel_id=1, source_target_pairs={{0,12},{1,13},{2,14},{3,15},{4,8},{5,9},{6,10},{7,11},{8,4},{9,5},... | collective-permute-start | bytes 1032200 | tf_op jit(solution)/shard_map/ppermute | solution.py:442
  246.6 16.4 %collective-permute-start.26 = (bf16[112,1536]{1,0:T(8,128)(2,1)S(1)}, bf16[112,1536]{1,0:T(8,128)(2,1)S(1)}, u32[]{:S(2)}, u32[]{:S(2)}) collective-permute-start(bf16[112,1536]{1,0:T(8,128)(2,1)S(1)} %add.111), channel_id=1, source_target_pairs={{0,8},{1,9},{2,10},{3,11},{4,12},{5,13},{6,14},{7,15},{8,0},{9,1},... | collective-permute-start | bytes 1032200 | tf_op jit(solution)/shard_map/ppermute | solution.py:442
  246.7 16.3 %collective-permute-start.25 = (bf16[112,1536]{1,0:T(8,128)(2,1)S(1)}, bf16[112,1536]{1,0:T(8,128)(2,1)S(1)}, u32[]{:S(2)}, u32[]{:S(2)}) collective-permute-start(bf16[112,1536]{1,0:T(8,128)(2,1)S(1)} %add.111), channel_id=1, source_target_pairs={{0,4},{1,5},{2,6},{3,7},{4,0},{5,1},{6,2},{7,3},{8,12},{9,13},{10,... | collective-permute-start | bytes 1032200 | tf_op jit(solution)/shard_map/ppermute | solution.py:442
  249.5 24.2 %collective-permute-start.28 = (bf16[2,96,1536]{2,1,0:T(8,128)(2,1)S(1)}, bf16[2,96,1536]{2,1,0:T(8,128)(2,1)S(1)}, u32[]{:S(2)}, u32[]{:S(2)}) collective-permute-start(bf16[2,96,1536]{2,1,0:T(8,128)(2,1)S(1)} %pad_maximum_fusion.2), channel_id=1, source_target_pairs={{0,8},{1,9},{2,10},{3,11},{4,12},{5,13},{6,14},{7,15},{8,0},{9,1},... | collective-permute-start | bytes 1769480 | tf_op jit(solution)/shard_map/ppermute | solution.py:442
  274.0 1.6 copy-start.1

commit v3 on v2

--- a/solution.py
+++ b/solution.py
@@ -46,6 +46,10 @@
     )
 
 
+def row_of(ref):
+    return ref[...].reshape(1, -1)
+
+
 def lane_split(pair):
     lane = lax.broadcasted_iota(jnp.int32, pair.shape, 1)
     zero = jnp.zeros_like(pair)
@@ -53,69 +57,97 @@
 
 
 def forward_kernel(
-    ends_ref, x_ref, vec_ref, ebias_ref, qkvb_ref, wq_ref, wo_ref, we_ref, wc_ref,
+    lens_ref, spot_ref, x_ref, g1_ref, b1_ref, qvb_ref, obias_ref, g2_ref, b2_ref, ebias_ref, cbias_ref,
+    wq_hbm, wo_hbm, we_hbm, wc_hbm,
     first_ref, n1_ref, proj_ref, probs_ref, att_ref, n2_ref, second_ref, slope_ref, act_ref,
-    inv_ref, last_ref, h_scr, mask_scr,
+    inv_ref, wqot_ref, wet_ref, wct_ref, last_ref, h_scr, mask_scr, wqo_scr, we_ref, wc_ref, sems,
 ):
     step = pl.program_id(0)
     rows, width = h_scr.shape
     pairs = width // 128
     ff = we_ref.shape[1]
+    loads = [
+        pltpu.make_async_copy(wq_hbm, wqo_scr.at[:, 0 : 3 * width], sems.at[0]),
+        pltpu.make_async_copy(wo_hbm, wqo_scr.at[:, 3 * width : 4 * width], sems.at[1]),
+        pltpu.make_async_copy(we_hbm, we_ref, sems.at[2]),
+        pltpu.make_async_copy(wc_hbm, wc_ref, sems.at[3]),
+    ]
 
     @pl.when(step == 0)
     def _():
+        for load in loads:
+            load.start()
         h_scr[...] = x_ref[...].astype(F32)
         query = lax.broadcasted_iota(jnp.int32, (rows, rows), 0)
         key = lax.broadcasted_iota(jnp.int32, (rows, rows), 1)
         own_q = jnp.zeros((rows, rows), jnp.int32)
         own_k = jnp.zeros((rows, rows), jnp.int32)
-        for slot in range(ends_ref.shape[0]):
-            end = ends_ref[slot]
+        slots = lens_ref.shape[1]
+        end = jnp.int32(0)
+        for slot in range(slots):
+            end = end + lens_ref[spot_ref[4], slot]
             own_q += (query >= end).astype(jnp.int32)
             own_k += (key >= end).astype(jnp.int32)
-        mask_scr[...] = ((own_q == own_k) & (key <= query)).astype(F32)
-
+        mask_scr[...] = jnp.where((own_q == own_k) & (key <= query), 0.0, MASKED)
+        loads[0].wait()
+        loads[1].wait()
+
+    strip = wqot_ref.shape[0]
+    at = pl.multiple_of(jnp.minimum(step, 4 * width // strip - 1) * strip, 128)
+    wqot_ref[...] = wqo_scr[:, pl.ds(at, strip)].T
     h = h_scr[...]
     n1, inv1 = normed_of(h)
-    first_low = (n1 * vec_ref[0:1, :] + vec_ref[1:2, :]).astype(BF)
+    first_low = (n1 * row_of(g1_ref) + row_of(b1_ref)).astype(BF)
     first_ref[0] = first_low
     n1_ref[0] = n1.astype(BF)
-    proj = (nn(first_low, wq_ref[...]) + qkvb_ref[...]).astype(BF)
-    proj_ref[0] = proj
-    allowed = jnp.concatenate([mask_scr[...], mask_scr[...]], axis=0) > 0.5
+    raw = nn(first_low, wqo_scr[:, 0 : 3 * width])
+    queries = ((raw[:, :width] + row_of(qvb_ref)[:, :width]) * SCORE_SCALE).astype(BF)
+    keys = raw[:, width : 2 * width].astype(BF)
+    values = (raw[:, 2 * width :] + row_of(qvb_ref)[:, width:]).astype(BF)
+    proj_ref[0, :, 0:width] = queries
+    proj_ref[0, :, width : 2 * width] = keys
+    proj_ref[0, :, 2 * width : 3 * width] = values
+    mask = mask_scr[...]
+    mask = jnp.concatenate([mask, mask], axis=0)
     outs = []
     for p in range(pairs):
-        q = proj[:, 128 * p : 128 * (p + 1)]
-        k = proj[:, width + 128 * p : width + 128 * (p + 1)]
-        v = proj[:, 2 * width + 128 * p : 2 * width + 128 * (p + 1)]
-        scores = nt(jnp.concatenate(lane_split(q), axis=0), k) * SCORE_SCALE
-        scores = jnp.where(allowed, scores, MASKED)
+        cut = slice(128 * p, 128 * (p + 1))
+        scores = nt(jnp.concatenate(lane_split(queries[:, cut]), axis=0), keys[:, cut]) + mask
         highest = jnp.max(scores, axis=-1, keepdims=True)
         weight = jnp.exp(scores - highest)
-        low = (weight / jnp.sum(weight, axis=-1, keepdims=True)).astype(BF)
+        low = (weight * (1.0 / jnp.sum(weight, axis=-1, keepdims=True))).astype(BF)
         probs_ref[0, 2 * rows * p : 2 * rows * (p + 1), :] = low
         both = jnp.concatenate([low[:rows], low[rows:]], axis=1)
-        outs.append(nn(both, jnp.concatenate(lane_split(v), axis=0)).astype(BF))
+        outs.append(nn(both, jnp.concatenate(lane_split(values[:, cut]), axis=0)).astype(BF))
     attended = jnp.concatenate(outs, axis=1)
     att_ref[0] = attended
-    middle = h + (nn(attended, wo_ref[...]) + vec_ref[2:3, :])
+    middle = h + (nn(attended, wqo_scr[:, 3 * width : 4 * width]) + row_of(obias_ref))
     n2, inv2 = normed_of(middle)
-    second_low = (n2 * vec_ref[3:4, :] + vec_ref[4:5, :]).astype(BF)
+    second_low = (n2 * row_of(g2_ref) + row_of(b2_ref)).astype(BF)
     second_ref[0] = second_low
     n2_ref[0] = n2.astype(BF)
     inv_ref[0] = jnp.concatenate(
         [jnp.broadcast_to(inv1, (rows, 128)), jnp.broadcast_to(inv2, (rows, 128))], axis=1
     )
-    total = middle + vec_ref[5:6, :]
+    total = middle + row_of(cbias_ref)
+
+    @pl.when(step == 0)
+    def _():
+        loads[2].wait()
+        loads[3].wait()
+
+    wet_ref[...] = we_ref[:, pl.ds(at, strip)].T
+    wct_ref[...] = wc_ref[pl.ds(at, strip), :].T
+    ebias = row_of(ebias_ref)
     chunk = 1024
     for j in range(ff // chunk):
         cols = slice(chunk * j, chunk * (j + 1))
-        pre = nn(second_low, we_ref[:, cols]) + ebias_ref[:, cols]
+        pre = nn(second_low, we_ref[:, cols]) + ebias[:, cols]
         square = pre * pre
-        t = jnp.tanh(GELU_A * pre * (1.0 + GELU_B * square))
-        half = 0.5 * (1.0 + t)
-        act = (pre * half).astype(BF)
-        slope = half + 0.5 * GELU_A * pre * (1.0 - t * t) * (1.0 + 3.0 * GELU_B * square)
+        half = 0.5 + 0.5 * jnp.tanh(pre * (GELU_A + GELU_A * GELU_B * square))
+        act = pre * half
+        slope = half + act * (1.0 - half) * (2.0 * GELU_A + 6.0 * GELU_A * GELU_B * square)
+        act = act.astype(BF)
         slope_ref[0, :, cols] = slope.astype(BF)
         act_ref[0, :, cols] = act
         total = total + nn(act, wc_ref[cols, :])
@@ -132,22 +164,32 @@
 
 
 def backward_kernel(
-    cot_ref, vec_ref, wqt_ref, wot_ref, wet_ref, wct_ref,
+    cot_ref, g1_ref, g2_ref, wqot_hbm, wet_hbm, wct_hbm,
     n1_ref, proj_ref, probs_ref, n2_ref, slope_ref, inv_ref,
     gproj_ref, gattn_ref, gpre_ref, gmlp_ref, gtok_ref, sums_ref,
-    g_scr, s768_scr, s2304_scr, s3072_scr,
+    g_scr, s768_scr, s2304_scr, s3072_scr, wqot_ref, wet_ref, wct_ref, sems,
 ):
     step = pl.program_id(0)
     rows, width = g_scr.shape
     pairs = width // 128
     ff = wct_ref.shape[1]
 
+    loads = [
+        pltpu.make_async_copy(wct_hbm, wct_ref, sems.at[0]),
+        pltpu.make_async_copy(wet_hbm, wet_ref, sems.at[1]),
+        pltpu.make_async_copy(wqot_hbm, wqot_ref, sems.at[2]),
+    ]
+
     @pl.when(step == 0)
     def _():
+        for load in loads:
+            load.start()
         g_scr[...] = cot_ref[...].astype(F32)
         s768_scr[...] = jnp.zeros_like(s768_scr)
         s2304_scr[...] = jnp.zeros_like(s2304_scr)
         s3072_scr[...] = jnp.zeros_like(s3072_scr)
+        loads[0].wait()
+        loads[1].wait()
 
     g = g_scr[...]
     gmlp = g.astype(BF)
@@ -161,10 +203,15 @@
         s3072_scr[:, cols] += fold(gpre.astype(F32))
         gsec = gsec + nn(gpre, wet_ref[cols, :])
     n2 = n2_ref[0].astype(F32)
-    gmid = g + norm_back(gsec, n2, inv_ref[0, :, 128:129], vec_ref[3:4, :])
+    gmid = g + norm_back(gsec, n2, inv_ref[0, :, 128:129], row_of(g2_ref))
     gattn = gmid.astype(BF)
     gattn_ref[0] = gattn
-    gatt = nn(gattn, wot_ref[...]).astype(BF)
+
+    @pl.when(step == 0)
+    def _():
+        loads[2].wait()
+
+    gatt = nn(gattn, wqot_ref[3 * width : 4 * width, :]).astype(BF)
     dqs, dks, dvs = [], [], []
     for p in range(pairs):
         q = proj_ref[0, :, 128 * p : 128 * (p + 1)]
@@ -180,13 +227,13 @@
         k2 = jnp.concatenate(lane_split(k), axis=0)
         q2 = jnp.concatenate(lane_split(q), axis=0)
         dqs.append((nn(both, k2) * SCORE_SCALE).astype(BF))
-        dks.append((tn(gscore, q2) * SCORE_SCALE).astype(BF))
+        dks.append(tn(gscore, q2).astype(BF))
         dvs.append(tn(low, out2).astype(BF))
     gproj = jnp.concatenate(dqs + dks + dvs, axis=1)
     gproj_ref[0] = gproj
-    gfirst = nn(gproj, wqt_ref[...])
+    gfirst = nn(gproj, wqot_ref[0 : 3 * width, :])
     n1 = n1_ref[0].astype(F32)
-    gin = gmid + norm_back(gfirst, n1, inv_ref[0, :, 0:1], vec_ref[0:1, :])
+    gin = gmid + norm_back(gfirst, n1, inv_ref[0, :, 0:1], row_of(g1_ref))
     s768_scr[0] += fold(gfirst * n1)
     s768_scr[1] += fold(gfirst)
     s768_scr[2] += fold(gattn.astype(F32))
@@ -213,32 +260,44 @@
     return pl.BlockSpec(shape, lambda i, *_: zeros, pipeline_mode=pl.Buffered(1))
 
 
-def forward_all(ends, x, vec, ebias, qkvb, wq, wo, we, wc, layers):
+def forward_all(lens, spot, x, rows_in, wq, wo, we, wc, layers):
     rows, width = x.shape
     ff = we.shape[1]
     pairs = width // 128
+    strip = ff // 8
     stack = lambda cols, r=rows, t=BF: jax.ShapeDtypeStruct((layers, r, cols), t)
     outs = [
         stack(width), stack(width), stack(3 * width), stack(rows, 2 * rows * pairs), stack(width),
         stack(width), stack(width), stack(ff), stack(ff), stack(256, rows, F32),
     ]
     per_layer = lambda s: pl.BlockSpec((1,) + s.shape[1:], lambda i, *_: (i, 0, 0))
+    turned = [jax.ShapeDtypeStruct(s, BF) for s in ((4 * width, width), (ff, width), (width, ff))]
+    by_rows = pl.BlockSpec((strip, width), lambda i, *_: (jnp.minimum(i, 7), 0))
+    by_cols = pl.BlockSpec((width, strip), lambda i, *_: (0, jnp.minimum(i, 7)))
     last = jax.ShapeDtypeStruct((rows, width), BF)
     return pl.pallas_call(
         forward_kernel,
         grid_spec=pltpu.PrefetchScalarGridSpec(
-            num_scalar_prefetch=1,
+            num_scalar_prefetch=2,
             grid=(layers,),
-            in_specs=[whole_spec(a.shape) for a in (x, vec, ebias, qkvb, wq, wo, we, wc)],
-            out_specs=[per_layer(s) for s in outs] + [whole_spec(last.shape)],
-            scratch_shapes=[pltpu.VMEM((rows, width), F32), pltpu.VMEM((rows, rows), F32)],
+            in_specs=[whole_spec(a.shape) for a in (x, *rows_in)]
+            + [pl.BlockSpec(memory_space=pl.ANY)] * 4,
+            out_specs=[per_layer(s) for s in outs] + [by_rows, by_rows, by_cols, whole_spec(last.shape)],
+            scratch_shapes=[
+                pltpu.VMEM((rows, width), F32),
+                pltpu.VMEM((rows, rows), F32),
+                pltpu.VMEM((width, 4 * width), BF),
+                pltpu.VMEM((width, ff), BF),
+                pltpu.VMEM((ff, width), BF),
+                pltpu.SemaphoreType.DMA((4,)),
+            ],
         ),
-        out_shape=outs + [last],
+        out_shape=outs + turned + [last],
         compiler_params=pltpu.CompilerParams(vmem_limit_bytes=VMEM_LIMIT),
-    )(ends, x, vec, ebias, qkvb, wq, wo, we, wc)
-
-
-def backward_all(cot, vec, wqt, wot, wet, wct, n1, proj, probs, n2, slope, inv):
+    )(lens, spot, x, *rows_in, wq, wo, we, wc)
+
+
+def backward_all(cot, g1, g2, wqot, wet, wct, n1, proj, probs, n2, slope, inv):
     layers, rows, width = n1.shape
     ff = wct.shape[1]
     stack = lambda cols: jax.ShapeDtypeStruct((layers, rows, cols), BF)
@@ -248,7 +307,8 @@
     return pl.pallas_call(
         backward_kernel,
         grid=(layers,),
-        in_specs=[whole_spec(a.shape) for a in (cot, vec, wqt, wot, wet, wct)]
+        in_specs=[whole_spec(a.shape) for a in (cot, g1, g2)]
+        + [pl.BlockSpec(memory_space=pl.ANY)] * 3
         + [per_layer(a) for a in (n1, proj, probs, n2, slope, inv)],
         out_specs=[per_layer(s) for s in outs] + [whole_spec(s.shape) for s in last],
         out_shape=outs + last,
@@ -257,9 +317,13 @@
             pltpu.VMEM((6, 8, width), F32),
             pltpu.VMEM((8, 3 * width), F32),
             pltpu.VMEM((8, ff), F32),
+            pltpu.VMEM((4 * width, width), BF),
+            pltpu.VMEM((ff, width), BF),
+            pltpu.VMEM((width, ff), BF),
+            pltpu.SemaphoreType.DMA((3,)),
         ],
         compiler_params=pltpu.CompilerParams(vmem_limit_bytes=VMEM_LIMIT),
-    )(cot, vec, wqt, wot, wet, wct, n1, proj, probs, n2, slope, inv)
+    )(cot, g1, g2, wqot, wet, wct, n1, proj, probs, n2, slope, inv)
 
 
 def outer_kernel(spot_ref, left_ref, right_ref, give_ref, keep_ref, scr, *, tall):
@@ -447,7 +511,7 @@
 
 
 def plane_parts(both, hop):
-    return hop(both[1, 0], 1, 0, 0), hop(both[0, 1], 0, 1, 0), hop(both[1, 1], 1, 1, 0)
+    return [hop(both[1, 0], 1, 0, 0), hop(both[0, 1], 0, 1, 0), hop(both[1, 1], 1, 1, 0)]
 
 
 def plane_sum(both, parts):
@@ -488,19 +552,14 @@
     shard = xor_order(jnp.stack(got), label)
     shard = shard.reshape(sections // 4, 2, 2, piece_rows, 2 * width).swapaxes(1, 2).reshape(rows, 2 * width)
     x, cot = shard[:, :width], shard[:, width:]
-    ends = jnp.cumsum(lax.dynamic_index_in_dim(lengths, label >> 1, 0, keepdims=False)[0])
-
-    vec = jnp.stack(
-        [first_gain, first_shift, out_bias, second_gain, second_shift, contract_bias, out_bias, out_bias]
-    )
-    qkvb = jnp.concatenate([qv_bias[:width], jnp.zeros((width,), F32), qv_bias[width:]])[None]
-    first, n1, proj, probs, att, n2, second, slope, act, inv, last = forward_all(
-        ends, x, vec, expand_bias[None], qkvb,
+    spot = jnp.stack([(dp >> 1) & 1, dp & 1, section & 1, (section >> 1) & 1, label >> 1]).astype(jnp.int32)
+    first, n1, proj, probs, att, n2, second, slope, act, inv, wqot, wet, wct, last = forward_all(
+        lengths[:, 0], spot, x,
+        [first_gain, first_shift, qv_bias, out_bias, second_gain, second_shift, expand_bias, contract_bias],
         qkv_weight, out_weight, expand_weight, contract_weight, sections,
     )
     gproj, gattn, gpre, gmlp, gtok, sums = backward_all(
-        cot, vec, qkv_weight.T, out_weight.T, expand_weight.T, contract_weight.T,
-        n1, proj, probs, n2, slope, inv,
+        cot, first_gain, second_gain, wqot, wet, wct, n1, proj, probs, n2, slope, inv,
     )
 
     flat = lambda a: a.reshape(-1, a.shape[-1])
@@ -512,7 +571,7 @@
     ]
     if (sections, dps) == (8, 4):
         g_qkv, g_out, g_exp, g_con, v, back = grads_small_slice(
-            section, dp, first, att, second, act, gproj, gattn, gpre, gmlp, sums, blocks
+            section, dp, spot, first, att, second, act, gproj, gattn, gpre, gmlp, sums, blocks
         )
     else:
         half = (label & 1) == 0
@@ -537,10 +596,9 @@
     )
 
 
-def grads_small_slice(section, dp, first, att, second, act, gproj, gattn, gpre, gmlp, sums, blocks):
+def grads_small_slice(section, dp, spot, first, att, second, act, gproj, gattn, gpre, gmlp, sums, blocks):
     sections, dps = 8, 4
-    y, r, x, core = section & 1, (section >> 1) & 1, dp >> 1, dp & 1
-    spot = jnp.stack([x, core, y, r]).astype(jnp.int32)
+    y, r, core = section & 1, (section >> 1) & 1, dp & 1
     width, ff = first.shape[1], act.shape[1]
     hop = partial(move, sections=sections, dps=dps)
     cols = 2 * width
@@ -557,22 +615,25 @@
     from_b, out_c, z_a = tie((from_b, out_c, z_a))
     plane_b, total_a = plane_sum(add_b, from_b), plane_a + z_a
     z_b = hop(jnp.concatenate([plane_b, blocks[2], blocks[3]], axis=0), 0, 0, 2)
-    y_a, add_c = hop(total_a, 0, 1, 0), over_core(*out_c, dps)
+    r_a, add_c = hop(total_a, 0, 0, 1), over_core(*out_c, dps)
     from_c = plane_parts(add_c, hop)
-    from_c, z_b, y_a = tie((from_c, z_b, y_a))
-    pieces = z_b.shape[0] - tall
-    z_b, from_z, through_z = z_b[:tall], z_b[tall : tall + pieces // 2], z_b[tall + pieces // 2 :]
+    from_c, z_b, r_a = tie((from_c, z_b, r_a))
+    pieces = (z_b.shape[0] - tall) // 2
+    z_b, from_z, through_z = z_b[:tall], z_b[tall : tall + pieces], z_b[tall + pieces :]
     plane_c, total_b = plane_sum(add_c, from_c), plane_b + z_b
-    z_c = hop(plane_c, 0, 0, 2)
-    y_b = hop(jnp.concatenate([total_b, blocks[1], through_z], axis=0), 0, 1, 0)
-    far_a = hop(jnp.stack([total_a, y_a]), 0, 0, 1)
-    z_c, y_b, far_a = tie((z_c, y_b, far_a))
-    y_b, from_y, from_both = y_b[:tall], y_b[tall : tall + pieces // 2], y_b[tall + pieces // 2 :]
+    mid = tall // 2
+    top, bottom = total_b[:mid], total_b[mid:]
+    z_c, y_a = hop(plane_c, 0, 0, 2), hop(jnp.stack([total_a, r_a]), 0, 1, 0)
+    r_top, y_bottom = hop(top, 0, 0, 1), hop(jnp.concatenate([bottom, blocks[1], through_z], axis=0), 0, 1, 0)
+    z_c, y_a, r_top, y_bottom = tie((z_c, y_a, r_top, y_bottom))
+    y_bottom, from_y, from_both = y_bottom[:mid], y_bottom[mid : mid + pieces], y_bottom[mid + pieces :]
     back = [blocks[0], from_y, from_z, from_both]
-    total_c = plane_c + z_c
-    rest = all_parts(total_c, hop)
-    far_b = hop(jnp.stack([total_b, y_b]), 0, 0, 1)
-    con, exp = (total_a, y_a, far_a[0], far_a[1]), (total_b, y_b, far_b[0], far_b[1])
+    rest = all_parts(plane_c + z_c, hop)
+    y_top = hop(jnp.stack([top, r_top]), 0, 1, 0)
+    r_bottom = hop(jnp.stack([bottom, y_bottom]), 0, 0, 1)
+    stacked = lambda a, b: jnp.concatenate([a, b], axis=0)
+    con = total_a, y_a[0], r_a, y_a[1]
+    exp = total_b, stacked(y_top[0], y_bottom), stacked(r_top, r_bottom[0]), stacked(y_top[1], r_bottom[1])
     con, exp, att_part = in_order(con, y, r), in_order(exp, y, r), in_order([p[:tall] for p in rest], y, r)
     g_con = jnp.concatenate([con[0][0], con[0][1], con[1][0], con[1][1]], axis=0)
     g_exp = jnp.concatenate([jnp.concatenate([exp[0][j], exp[1][j]], axis=1) for j in (0, 1)], axis=0)

time: 277 us -> 241 us (0.87)
  local copies, waits for them, and re-layouts: 35.3 us -> 8.83 us
  waiting for transfers between devices: 75.5 us -> 66.1 us
    unnamed x20 -> x12, local copies, waits for them, and re-layouts: 21.5 us -> 0.04 us
    ppermute x19 -> x21, waiting for transfers between devices: 65.1 us -> 53.1 us  [move(): return lax.ppermute(array, AXES, pairs)]
    another operation x9 -> x2, local copies, waits for them, and re-layouts: 4.81 us -> 0.64 us  [the longest x1 0.6 us: body(): jnp.stack([dp >> 1 & 1, dp & 1, section & 1, section >> 1 & 1, label >> 1])]
    ppermute x19 -> x21, starting transfers between devices: 23.2 us -> 23.6 us  [move(): return lax.ppermute(array, AXES, pairs)]
  transfers between devices with their start and end apart: 29 -> 31, of which waited for: 14 -> 15; matrix products, arithmetic and copies ran while one was open for 16% -> 7% of each run, Pallas kernels for 5% -> 6%
where the time goes in v3:
time: 241 us; the launch traced here: 240 us
  Pallas kernels  110 us (46%)
  waiting for transfers between devices  66.1 us (27%)
  starting transfers between devices  35.6 us (15%)
  other arithmetic  18.3 us (8%)
  local copies, waits for them, and re-layouts  8.83 us (4%)
    ppermute x21, waiting for transfers between devices, move(): return lax.ppermute(array, AXES, pairs)  53.1 us
    pallas_call x1, Pallas kernels, backward_all(): pl.pallas_call(backward_kernel, grid=(layers,), in_specs=[whole_spec(a.sh...  46.3 us
    pallas_call x1, Pallas kernels, forward_all(): pl.pallas_call(forward_kernel, grid_spec=pltpu.PrefetchScalarGridSpec(num...  41.6 us
    ppermute x21, starting transfers between devices, move(): return lax.ppermute(array, AXES, pairs)  23.6 us
    ppermute x7, starting transfers between devices, body(): lax.ppermute(block, 'section', by_label(k, sections))  12 us
    pallas_call x1, Pallas kernels, attention_grads(): pl.pallas_call(attention_kernel, grid_spec=pltpu.PrefetchScalarGridSpec(n...  8.18 us
    pallas_call x1, Pallas kernels, contract_grads(): pl.pallas_call(contract_kernel, grid_spec=pltpu.PrefetchScalarGridSpec(nu...  7.42 us
    ppermute x7, waiting for transfers between devices, body(): lax.ppermute(block, 'section', by_label(k, sections))  6.98 us
  transfers between devices with their start and end apart: 31, of which 15 were waited for; matrix products, arithmetic and copies ran while one was open for 7% of the time, Pallas kernels for 6%

profile of v3, /device:TPU:0, one launch (start us, length us, event | category | flops | bytes accessed | tf_op | source)
XLA Modules:
  0.0 240.1 jit_solution(12405992765184285097)
XLA Ops:
  0.7 0.9 fusion.24
  1.6 3.1 %collective-permute-start = (bf16[16,1536]{1,0:T(8,128)(2,1)S(1)}, bf16[16,1536]{1,0:T(8,128)(2,1)S(1)}, u32[]{:S(2)}, u32[]{:S(2)}) collective-permute-start(bf16[16,1536]{1,0:T(8,128)(2,1)S(1)} %get-tuple-element.167), channel_id=1, source_target_pairs={{0,8},{4,12},{8,0},{12,4},{16,24},{20,28},{24,16},{28,20},{1,9},{5... | collective-permute-start | bytes 147464 | tf_op jit(solution)/shard_map/ppermute | solution.py:551
  4.7 0.8 fusion.38
  5.5 3.6 %collective-permute-start.5 = (bf16[16,1536]{1,0:T(8,128)(2,1)S(1)}, bf16[16,1536]{1,0:T(8,128)(2,1)S(1)}, u32[]{:S(2)}, u32[]{:S(2)}) collective-permute-start(bf16[16,1536]{1,0:T(8,128)(2,1)S(1)} %get-tuple-element.171), channel_id=1, source_target_pairs={{0,20},{4,16},{8,28},{12,24},{16,4},{20,0},{24,12},{28,8},{1,21},{... | collective-permute-start | bytes 147464 | tf_op jit(solution)/shard_map/ppermute | solution.py:551
  9.3 3.6 %collective-permute-start.6 = (bf16[16,1536]{1,0:T(8,128)(2,1)S(1)}, bf16[16,1536]{1,0:T(8,128)(2,1)S(1)}, u32[]{:S(2)}, u32[]{:S(2)}) collective-permute-start(bf16[16,1536]{1,0:T(8,128)(2,1)S(1)} %get-tuple-element.165), channel_id=1, source_target_pairs={{0,28},{4,24},{8,20},{12,16},{16,12},{20,8},{24,4},{28,0},{1,29},{... | collective-permute-start | bytes 147464 | tf_op jit(solution)/shard_map/ppermute | solution.py:551
  12.9 1.5 collective-permute-start.1
  15.0 2.0 collective-permute-done.1
  17.0 3.5 %collective-permute-done.2 = bf16[16,1536]{1,0:T(8,128)(2,1)S(1)} collective-permute-done((bf16[16,1536]{1,0:T(8,128)(2,1)S(1)}, bf16[16,1536]{1,0:T(8,128)(2,1)S(1)}, u32[]{:S(2)}, u32[]{:S(2)}) %collective-permute-start.2) | collective-permute-done | bytes 49184 | tf_op jit(solution)/shard_map/ppermute | solution.py:551
  20.5 1.5 collective-permute-done.3
  23.1 41.6 %shard_map.254 = (bf16[8,128,768]{2,1,0:T(8,128)(2,1)}, bf16[8,128,768]{2,1,0:T(8,128)(2,1)}, bf16[8,128,2304]{2,1,0:T(8,128)(2,1)}, bf16[8,1536,128]{2,1,0:T(8,...) custom-call(s32[4,4]{1,0:T(4,128)} %bitcast.158, ...), custom_call_target="tpu_custom_call" | custom-call | tf_op jit(solution)/shard_map/pallas_call | solution.py:278
  64.8 46.3 %shard_map.255 = (bf16[8,128,2304]{2,1,0:T(8,128)(2,1)}, bf16[8,128,768]{2,1,0:T(8,128)(2,1)}, bf16[8,128,3072]{2,1,0:T(8,128)(2,1)}, bf16[8,128,768]{2,1,0:T(8,...) custom-call(bf16[128,768]{1,0:T(8,128)(2,1)} %get-tuple-element.149.cot_ref, f32[768]{0:T(1024)} %g1_ref.3, ...), custom_call_target="tpu_custom_call" | custom-call | tf_op jit(solution)/shard_map/pallas_call | solution.py:307
  111.1 7.4 %shard_map.256 = (bf16[2,2,192,768]{3,2,1,0:T(8,128)(2,1)}, bf16[2,2,192,768]{3,2,1,0:T(8,128)(2,1)}) custom-call(s32[5]{0:T(128)} %stack.88.spot_ref, bf16[1024,3072]{1,0:T(8,128)(2,1)} %bitcast.166, bf16[1024,768]{1,0:T(8,128)(2,1)} %bitcast.168), custom_call_target="tpu_custom_call" | custom-call | flops 2415919104 | bytes 7077888 | tf_op jit(solution)/shard_map/pallas_call | solution.py:405
  118.5 3.1 %collective-permute-done.7 = bf16[2,2,192,768]{3,2,1,0:T(8,128)(2,1)S(1)} collective-permute-done((bf16[2,2,192,768]{3,2,1,0:T(8,128)(2,1)}, bf16[2,2,192,768]{3,2,1,0:T(8,128)(2,1)S(1)}, u32[]{:S(2)}, u32[]{:S(2)}) %collective-permute-start.7) | collective-permute-done | bytes 1179680 | tf_op jit(solution)/shard_map/ppermute | solution.py:510
  121.6 1.6 add.92
  123.2 2.6 %collective-permute-start.10 = (bf16[192,768]{1,0:T(8,128)(2,1)S(1)}, bf16[192,768]{1,0:T(8,128)(2,1)S(1)}, u32[]{:S(2)}, u32[]{:S(2)}) collective-permute-start(bf16[192,768]{1,0:T(8,128)(2,1)S(1)} %get-tuple-element.140), channel_id=1, source_target_pairs={{0,6},{1,7},{2,4},{3,5},{4,2},{5,3},{6,0},{7,1},{8,14},{9,15},{10,... | collective-permute-start | bytes 884744 | tf_op jit(solution)/shard_map/ppermute | solution.py:506
  126.8 6.7 %shard_map.257 = (bf16[2,2,96,1536]{3,2,1,0:T(8,128)(2,1)}, bf16[2,2,96,1536]{3,2,1,0:T(8,128)(2,1)}) custom-call(s32[5]{0:T(128)} %stack.88.spot_ref, bf16[1024,768]{1,0:T(8,128)(2,1)} %bitcast.167, bf16[1024,3072]{1,0:T(8,128)(2,1)} %bitcast.165), custom_call_target="tpu_custom_call" | custom-call | flops 2415919104 | bytes 7077888 | tf_op jit(solution)/shard_map/pallas_call | solution.py:355
  134.1 5.5 %collective-permute-done.9 = bf16[192,768]{1,0:T(8,128)(2,1)S(1)} collective-permute-done((bf16[192,768]{1,0:T(8,128)(2,1)S(1)}, bf16[192,768]{1,0:T(8,128)(2,1)S(1)}, u32[]{:S(2)}, u32[]{:S(2)}) %collective-permute-start.9) | collective-permute-done | bytes 294944 | tf_op jit(solution)/shard_map/ppermute | solution.py:506
  140.0 2.7 %collective-permute-done.11 = bf16[2,2,96,1536]{3,2,1,0:T(8,128)(2,1)S(1)} collective-permute-done((bf16[2,2,96,1536]{3,2,1,0:T(8,128)(2,1)}, bf16[2,2,96,1536]{3,2,1,0:T(8,128)(2,1)S(1)}, u32[]{:S(2)}, u32[]{:S(2)}) %collective-permute-start.11) | collective-permute-done | bytes 1179680 | tf_op jit(solution)/shard_map/ppermute | solution.py:510
  143.8 1.6 collective-permute-start.14
  145.4 1.3 collective-permute-start.13
  147.3 8.2 %shard_map.258 = (bf16[2,2,112,1536]{3,2,1,0:T(8,128)(2,1)}, bf16[2,2,112,1536]{3,2,1,0:T(8,128)(2,1)}) custom-call(s32[5]{0:T(128)} %stack.88.spot_ref, bf16[1024,768]{1,0:T(8,128)(2,1)} %bitcast.141, bf16[1024,2304]{1,0:T(8,128)(2,1)} %bitcast.139, bf16[1024,768]{1,0:T(8,128)(2,1)} %bitcast.142, bf16[1024,768]{1,0:T(8,128)(2,1)} %bitcast.143, ...), custom_call_target="tpu_custom_call" | custom-call | flops 2415919104 | bytes 7077888 | tf_op jit(solution)/shard_map/pallas_call | solution.py:464
  156.0 4.5 %collective-permute-done.13 = bf16[96,1536]{1,0:T(8,128)(2,1)} collective-permute-done((bf16[96,1536]{1,0:T(8,128)(2,1)S(1)}, bf16[96,1536]{1,0:T(8,128)(2,1)}, u32[]{:S(2)}, u32[]{:S(2)}) %collective-permute-start.13) | collective-permute-done | bytes 294944 | tf_op jit(solution)/shard_map/ppermute | solution.py:506
  160.4 1.0 pad_maximum_fusion.2
  162.1 1.3 fusion.5
  163.9 1.7 add.97
  165.7 1.6 collective-permute-start.19
  167.3 1.4 collective-permute-start.18
  169.3 1.6 collective-permute-start.21
  170.9 15.1 %collective-permute-done.21 = bf16[192,768]{1,0:T(8,128)(2,1)S(1)} collective-permute-done((bf16[192,768]{1,0:T(8,128)(2,1)S(1)}, bf16[192,768]{1,0:T(8,128)(2,1)S(1)}, u32[]{:S(2)}, u32[]{:S(2)}) %collective-permute-start.21) | collective-permute-done | bytes 294944 | tf_op jit(solution)/shard_map/ppermute | solution.py:506
  186.2 0.9 collective-permute-start.22
  187.2 1.5 collective-permute-start.23
  190.6 2.1 collective-permute-start.24
  192.7 5.1 %collective-permute-done.24 = bf16[48,1536]{1,0:T(8,128)(2,1)S(1)} collective-permute-done((bf16[48,1536]{1,0:T(8,128)(2,1)S(1)}, bf16[48,1536]{1,0:T(8,128)(2,1)S(1)}, u32[]{:S(2)}, u32[]{:S(2)}) %collective-permute-start.24) | collective-permute-done | bytes 147488 | tf_op jit(solution)/shard_map/ppermute | solution.py:506
  197.8 9.8 %collective-permute-done.25 = bf16[80,1536]{1,0:T(8,128)(2,1)} collective-permute-done((bf16[80,1536]{1,0:T(8,128)(2,1)}, bf16[80,1536]{1,0:T(8,128)(2,1)}, u32[]{:S(2)}, u32[]{:S(2)}) %collective-permute-start.25) | collective-permute-done | bytes 245792 | tf_op jit(solution)/shard_map/ppermute | solution.py:506
  208.4 1.5 slice_bitcast_fusion.18
  209.8 0.9 fusion.40
  210.7 1.8 collective-permute-start.28
  212.5 1.2 collective-permute-start.27
  215.0 1.5 collective-permute-start.29
  216.5 0.9 collective-permute-start.30
  217.4 0.9 pad_maximum_fusion.10
  218.7 1.6 pad_maximum_fusion
  220.2 1.3 slice_reduce_fusion.2
  222.3 12.0 %collective-permute-done.29 = bf16[2,48,1536]{2,1,0:T(8,128)(2,1)S(1)} collective-permute-done((bf16[2,48,1536]{2,1,0:T(8,128)(2,1)S(1)}, bf16[2,48,1536]{2,1,0:T(8,128)(2,1)S(1)}, u32[]{:S(2)}, u32[]{:S(2)}) %collective-permute-start.29) | collective-permute-done | bytes 294944 | tf_op jit(solution)/shard_map/ppermute | solution.py:506
  234.7 1.6 maximum_maximum_fusion
  236.3 1.4 fusion.10
  237.9 1.3 maximum_maximum_fusion.1
  239.3 0.9 maximum_maximum_fusion.2
  (92 shorter events, 14.0 us)
Async XLA Ops:
  1.6 13.4 %collective-permute-start = (bf16[16,1536]{1,0:T(8,128)(2,1)S(1)}, bf16[16,1536]{1,0:T(8,128)(2,1)S(1)}, u32[]{:S(2)}, u32[]{:S(2)}) collective-permute-start(bf16[16,1536]{1,0:T(8,128)(2,1)S(1)} %get-tuple-element.167), channel_id=1, source_target_pairs={{0,8},{4,12},{8,0},{12,4},{16,24},{20,28},{24,16},{28,20},{1,9},{5... | collective-permute-start | bytes 147464 | tf_op jit(solution)/shard_map/ppermute | solution.py:551
  5.5 16.5 %collective-permute-start.5 = (bf16[16,1536]{1,0:T(8,128)(2,1)S(1)}, bf16[16,1536]{1,0:T(8,128)(2,1)S(1)}, u32[]{:S(2)}, u32[]{:S(2)}) collective-permute-start(bf16[16,1536]{1,0:T(8,128)(2,1)S(1)} %get-tuple-element.171), channel_id=1, source_target_pairs={{0,20},{4,16},{8,28},{12,24},{16,4},{20,0},{24,12},{28,8},{1,21},{... | collective-permute-start | bytes 147464 | tf_op jit(solution)/shard_map/ppermute | solution.py:551
  9.1 12.9 %collective-permute-start.4 = (bf16[16,1536]{1,0:T(8,128)(2,1)S(1)}, bf16[16,1536]{1,0:T(8,128)(2,1)S(1)}, u32[]{:S(2)}, u32[]{:S(2)}) collective-permute-start(bf16[16,1536]{1,0:T(8,128)(2,1)S(1)} %get-tuple-element.172), channel_id=1, source_target_pairs={{0,24},{4,28},{8,16},{12,20},{16,8},{20,12},{24,0},{28,4},{1,25},{... | collective-permute-start | bytes 147464 | tf_op jit(solution)/shard_map/ppermute | solution.py:551
  9.3 12.7 %collective-permute-start.6 = (bf16[16,1536]{1,0:T(8,128)(2,1)S(1)}, bf16[16,1536]{1,0:T(8,128)(2,1)S(1)}, u32[]{:S(2)}, u32[]{:S(2)}) collective-permute-start(bf16[16,1536]{1,0:T(8,128)(2,1)S(1)} %get-tuple-element.165), channel_id=1, source_target_pairs={{0,28},{4,24},{8,20},{12,16},{16,12},{20,8},{24,4},{28,0},{1,29},{... | collective-permute-start | bytes 147464 | tf_op jit(solution)/shard_map/ppermute | solution.py:551
  12.9 4.1 %collective-permute-start.1 = (bf16[16,1536]{1,0:T(8,128)(2,1)S(1)}, bf16[16,1536]{1,0:T(8,128)(2,1)S(1)}, u32[]{:S(2)}, u32[]{:S(2)}) collective-permute-start(bf16[16,1536]{1,0:T(8,128)(2,1)S(1)} %get-tuple-element.168), channel_id=1, source_target_pairs={{0,4},{4,0},{8,12},{12,8},{16,20},{20,16},{24,28},{28,24},{1,5},{5... | collective-permute-start | bytes 147464 | tf_op jit(solution)/shard_map/ppermute | solution.py:551
  15.0 5.5 %collective-permute-start.2 = (bf16[16,1536]{1,0:T(8,128)(2,1)S(1)}, bf16[16,1536]{1,0:T(8,128)(2,1)S(1)}, u32[]{:S(2)}, u32[]{:S(2)}) collective-permute-start(bf16[16,1536]{1,0:T(8,128)(2,1)S(1)} %get-tuple-element.169), channel_id=1, source_target_pairs={{0,12},{4,8},{8,4},{12,0},{16,28},{20,24},{24,20},{28,16},{1,13},{... | collective-permute-start | bytes 147464 | tf_op jit(solution)/shard_map/ppermute | solution.py:551
  17.0 5.0 %collective-permute-start.3 = (bf16[16,1536]{1,0:T(8,128)(2,1)S(1)}, bf16[16,1536]{1,0:T(8,128)(2,1)S(1)}, u32[]{:S(2)}, u32[]{:S(2)}) collective-permute-start(bf16[16,1536]{1,0:T(8,128)(2,1)S(1)} %get-tuple-element.170), channel_id=1, source_target_pairs={{0,16},{4,20},{8,24},{12,28},{16,0},{20,4},{24,8},{28,12},{1,17},{... | collective-permute-start | bytes 147464 | tf_op jit(solution)/shard_map/ppermute | solution.py:551
  118.5 3.1 %collective-permute-start.7 = (bf16[2,2,192,768]{3,2,1,0:T(8,128)(2,1)}, bf16[2,2,192,768]{3,2,1,0:T(8,128)(2,1)S(1)}, u32[]{:S(2)}, u32[]{:S(2)}) collective-permute-start(bf16[2,2,192,768]{3,2,1,0:T(8,128)(2,1)} %get-tuple-element.88), channel_id=1, source_target_pairs={{0,1},{1,0},{2,3},{3,2},{4,5},{5,4},{6,7},{7,6},{8,9},{9,8},{10,11... | collective-permute-start | bytes 3538952 | tf_op jit(solution)/shard_map/ppermute | solution.py:510
  123.2 10.9 %collective-permute-start.10 = (bf16[192,768]{1,0:T(8,128)(2,1)S(1)}, bf16[192,768]{1,0:T(8,128)(2,1)S(1)}, u32[]{:S(2)}, u32[]{:S(2)}) collective-permute-start(bf16[192,768]{1,0:T(8,128)(2,1)S(1)} %get-tuple-element.140), channel_id=1, source_target_pairs={{0,6},{1,7},{2,4},{3,5},{4,2},{5,3},{6,0},{7,1},{8,14},{9,15},{10,... | collective-permute-start | bytes 884744 | tf_op jit(solution)/shard_map/ppermute | solution.py:506
  125.8 13.8 %collective-permute-start.9 = (bf16[192,768]{1,0:T(8,128)(2,1)S(1)}, bf16[192,768]{1,0:T(8,128)(2,1)S(1)}, u32[]{:S(2)}, u32[]{:S(2)}) collective-permute-start(bf16[192,768]{1,0:T(8,128)(2,1)S(1)} %get-tuple-element.141), channel_id=1, source_target_pairs={{0,4},{1,5},{2,6},{3,7},{4,0},{5,1},{6,2},{7,3},{8,12},{9,13},{10,... | collective-permute-start | bytes 884744 | tf_op jit(solution)/shard_map/ppermute | solution.py:506
  126.2 13.4 %collective-permute-start.8 = (bf16[192,768]{1,0:T(8,128)(2,1)S(1)}, bf16[192,768]{1,0:T(8,128)(2,1)S(1)}, u32[]{:S(2)}, u32[]{:S(2)}) collective-permute-start(bf16[192,768]{1,0:T(8,128)(2,1)S(1)} %get-tuple-element.142), channel_id=1, source_target_pairs={{0,2},{1,3},{2,0},{3,1},{4,6},{5,7},{6,4},{7,5},{8,10},{9,11},{10,... | collective-permute-start | bytes 884744 | tf_op jit(solution)/shard_map/ppermute | solution.py:506
  133.4 9.3 %copy-start.1 = (bf16[2,2,96,1536]{3,2,1,0:T(8,128)(2,1)S(1)}, bf16[2,2,96,1536]{3,2,1,0:T(8,128)(2,1)}, u32[]{:S(2)}) copy-start(bf16[2,2,96,1536]{3,2,1,0:T(8,128)(2,1)} %get-tuple-element.94) | copy-start | bytes 3538948
  139.7 3.1 %collective-permute-start.11 = (bf16[2,2,96,1536]{3,2,1,0:T(8,128)(2,1)}, bf16[2,2,96,1536]{3,2,1,0:T(8,128)(2,1)S(1)}, u32[]{:S(2)}, u32[]{:S(2)}) collective-permute-start(bf16[2,2,96,1536]{3,2,1,0:T(8,128)(2,1)} %get-tuple-element.95), channel_id=1, source_target_pairs={{0,1},{1,0},{2,3},{3,2},{4,5},{5,4},{6,7},{7,6},{8,9},{9,8},{10,11... | collective-permute-start | bytes 3538952 | tf_op jit(solution)/shard_map/ppermute | solution.py:510
  139.8 16.1 %collective-permute-start.15 = (bf16[192,768]{1,0:T(8,128)(2,1)S(1)}, bf16[192,768]{1,0:T(8,128)(2,1)S(1)}, u32[]{:S(2)}, u32[]{:S(2)}) collective-permute-start(bf16[192,768]{1,0:T(8,128)(2,1)S(1)} %fusion.8), channel_id=1, source_target_pairs={{0,16},{1,17},{2,18},{3,19},{4,20},{5,21},{6,22},{7,23},{8,24},{9,... | collective-permute-start | bytes 884744 | tf_op jit(solution)/shard_map/ppermute | solution.py:506
  143.8 12.1 %collective-permute-start.14 = (bf16[96,1536]{1,0:T(8,128)(2,1)}, bf16[96,1536]{1,0:T(8,128)(2,1)}, u32[]{:S(2)}, u32[]{:S(2)}) collective-permute-start(bf16[96,1536]{1,0:T(8,128)(2,1)} %get-tuple-element.137), channel_id=1, source_target_pairs={{0,6},{1,7},{2,4},{3,5},{4,2},{5,3},{6,0},{7,1},{8,14},{9,15},{10,... | collective-permute-start | bytes 884744 | tf_op jit(solution)/shard_map/ppermute | solution.py:506
  145.4 15.0 %collective-permute-start.13 = (bf16[96,1536]{1,0:T(8,128)(2,1)S(1)}, bf16[96,1536]{1,0:T(8,128)(2,1)}, u32[]{:S(2)}, u32[]{:S(2)}) collective-permute-start(bf16[96,1536]{1,0:T(8,128)(2,1)S(1)} %get-tuple-element.138), channel_id=1, source_target_pairs={{0,4},{1,5},{2,6},{3,7},{4,0},{5,1},{6,2},{7,3},{8,12},{9,13},{10,... | collective-permute-start | bytes 884744 | tf_op jit(solution)/shard_map/ppermute | solution.py:506
  146.8 13.6 %collective-permute-start.12 = (bf16[96,1536]{1,0:T(8,128)(2,1)S(1)}, bf16[96,1536]{1,0:T(8,128)(2,1)}, u32[]{:S(2)}, u32[]{:S(2)}) collective-permute-start(bf16[96,1536]{1,0:T(8,128)(2,1)S(1)} %get-tuple-element.139), channel_id=1, source_target_pairs={{0,2},{1,3},{2,0},{3,1},{4,6},{5,7},{6,4},{7,5},{8,10},{9,11},{10,... | collective-permute-start | bytes 884744 | tf_op jit(solution)/shard_map/ppermute | solution.py:506
  155.5 8.4 %copy-start = (bf16[2,2,112,1536]{3,2,1,0:T(8,128)(2,1)S(1)}, bf16[2,2,112,1536]{3,2,1,0:T(8,128)(2,1)}, u32[]{:S(2)}) copy-start(bf16[2,2,112,1536]{3,2,1,0:T(8,128)(2,1)} %get-tuple-element.107) | copy-start | bytes 4128772
  160.4 3.5 %collective-permute-start.16 = (bf16[2,2,112,1536]{3,2,1,0:T(8,128)(2,1)}, bf16[2,2,112,1536]{3,2,1,0:T(8,128)(2,1)}, u32[]{:S(2)}, u32[]{:S(2)}) collective-permute-start(bf16[2,2,112,1536]{3,2,1,0:T(8,128)(2,1)} %get-tuple-element.108), channel_id=1, source_target_pairs={{0,1},{1,0},{2,3},{3,2},{4,5},{5,4},{6,7},{7,6},{8,9},{9,8},{10,11... | collective-permute-start | bytes 4128776 | tf_op jit(solution)/shard_map/ppermute | solution.py:510
  163.5 22.5 %collective-permute-start.20 = (bf16[128,1536]{1,0:T(8,128)(2,1)S(1)}, bf16[128,1536]{1,0:T(8,128)(2,1)S(1)}, u32[]{:S(2)}, u32[]{:S(2)}) collective-permute-start(bf16[128,1536]{1,0:T(8,128)(2,1)S(1)} %pad_maximum_fusion.3), channel_id=1, source_target_pairs={{0,16},{1,17},{2,18},{3,19},{4,20},{5,21},{6,22},{7,23},{8,24},{9,... | collective-permute-start | bytes 1179656 | tf_op jit(solution)/shard_map/ppermute | solution.py:506
  165.7 20.3 %collective-permute-start.19 = (bf16[112,1536]{1,0:T(8,128)(2,1)S(1)}, bf16[112,1536]{1,0:T(8,128)(2,1)S(1)}, u32[]{:S(2)}, u32[]{:S(2)}) collective-permute-start(bf16[112,1536]{1,0:T(8,128)(2,1)S(1)} %get-tuple-element.126), channel_id=1, source_target_pairs={{0,6},{1,7},{2,4},{3,5},{4,2},{5,3},{6,0},{7,1},{8,14},{9,15},{10,... | collective-permute-start | bytes 1032200 | tf_op jit(solution)/shard_map/ppermute | solution.py:506
  167.3 18.7 %collective-permute-start.18 = (bf16[112,1536]{1,0:T(8,128)(2,1)S(1)}, bf16[112,1536]{1,0:T(8,128)(2,1)S(1)}, u32[]{:S(2)}, u32[]{:S(2)}) collective-permute-start(bf16[112,1536]{1,0:T(8,128)(2,1)S(1)} %get-tuple-element.127), channel_id=1, source_target_pairs={{0,4},{1,5},{2,6},{3,7},{4,0},{5,1},{6,2},{7,3},{8,12},{9,13},{10,... | collective-permute-start | bytes 1032200 | tf_op jit(solution)/shard_map/ppermute | solution.py:506
  168.7 17.2 %collective-permute-start.17 = (bf16[112,1536]{1,0:T(8,128)(2,1)S(1)}, bf16[112,1536]{1,0:T(8,128)(2,1)S(1)}, u32[]{:S(2)}, u32[]{:S(2)}) collective-permute-start(bf16[112,1536]{1,0:T(8,128)(2,1)S(1)} %get-tuple-element.128), channel_id=1, source_target_pairs={{0,2},{1,3},{2,0},{3,1},{4,6},{5,7},{6,4},{7,5},{8,10},{9,11},{10,... | collective-permute-start | bytes 1032200 | tf_op jit(solution)/shard_map/ppermute | solution.py:506
  169.3 16.6 %collective-permute-start.21 = (bf16[192,768]{1,0:T(8,128)(2,1)S(1)}, bf16[192,768]{1,0:T(8,128)(2,1)S(1)}, u32[]{:S(2)}, u32[]{:S(2)}) collective-permute-start(bf16[192,768]{1,0:T(8,128)(2,1)S(1)} %add.103), channel_id=1, source_target_pairs={{0,8},{1,9},{2,10},{3,11},{4,12},{5,13},{6,14},{7,15},{8,0},{9,1},... | collective-permute-start | bytes 884744 | tf_op jit(solution)/shard_map/ppermute | solution.py:506
  186.2 21.4 %collective-permute-start.22 = (bf16[112,1536]{1,0:T(8,128)(2,1)S(1)}, bf16[112,1536]{1,0:T(8,128)(2,1)S(1)}, u32[]{:S(2)}, u32[]{:S(2)}) collective-permute-start(bf16[112,1536]{1,0:T(8,128)(2,1)S(1)} %fusion.2), channel_id=1, source_target_pairs={{0,16},{1,17},{2,18},{3,19},{4,20},{5,21},{6,22},{7,23},{8,24},{9,... | collective-permute-start | bytes 1032200 | tf_op jit(solution)/shard_map/ppermute | solution.py:506
  187.2 20.4 %collective-permute-start.23 = (bf16[2,192,768]{2,1,0:T(8,128)(2,1)S(1)}, bf16[2,192,768]{2,1,0:T(8,128)(2,1)S(1)}, u32[]{:S(2)}, u32[]{:S(2)}) collective-permute-start(bf16[2,192,768]{2,1,0:T(8,128)(2,1)S(1)} %pad_maximum_fusion.1), channel_id=1, source_target_pairs={{0,4},{1,5},{2,6},{3,7},{4,0},{5,1},{6,2},{7,3},{8,12},{9,13},{10,... | collective-permute-start | bytes 1769480 | tf_op jit(solution)/shard_map/ppermute | solution.py:506
  190.0 17.6 %collective-permute-start.25 = (bf16[80,1536]{1,0:T(8,128)(2,1)}, bf16[80,1536]{1,0:T(8,128)(2,1)}, u32[]{:S(2)}, u32[]{:S(2)}) collective-permute-start(bf16[80,1536]{1,0:T(8,128)(2,1)} %pad_maximum_fusion.9), channel_id=1, source_target_pairs={{0,4},{1,5},{2,6},{3,7},{4,0},{5,1},{6,2},{7,3},{8,12},{9,13},{10,... | collective-permute-start | bytes 737288 | tf_op jit(solution)/shard_map/ppermute | solution.py:506
  190.6 7.2 %collective-permute-start.24 = (bf16[48,1536]{1,0:T(8,128)(2,1)S(1)}, bf16[48,1536]{1,0:T(8,128)(2,1)S(1)}, u32[]{:S(2)}, u32[]{:S(2)}) collective-permute-start(bf16[48,1536]{1,0:T(8,128)(2,1)S(1)} %get-tuple-element.158), channel_id=1, source_target_pairs={{0,8},{1,9},{2,10},{3,11},{4,12},{5,13},{6,14},{7,15},{8,0},{9,1},... | collective-permute-start | bytes 442376 | tf_op jit(solution)/shard_map/ppermute | solution.py:506
  207.7 0.7 copy-start.2
  210.7 25.5 %collective-permute-start.28 = (bf16[112,1536]{1,0:T(8,128)(2,1)S(1)}, bf16[112,1536]{1,0:T(8,128)(2,1)S(1)}, u32[]{:S(2)}, u32[]{:S(2)}) collective-permute-start(bf16[112,1536]{1,0:T(8,128)(2,1)S(1)} %add.109), channel_id=1, source_target_pairs={{0,12},{1,13},{2,14},{3,15},{4,8},{5,9},{6,10},{7,11},{8,4},{9,5},... | collective-permute-start | bytes 1032200 | tf_op jit(solution)/shard_map/ppermute | solution.py:506
  212.5 23.8 %collective-permute-start.27 = (bf16[112,1536]{1,0:T(8,128)(2,1)S(1)}, bf16[112,1536]{1,0:T(8,128)(2,1)}, u32[]{:S(2)}, u32[]{:S(2)}) collective-permute-start(bf16[112,1536]{1,0:T(8,128)(2,1)S(1)} %add.109), channel_id=1, source_target_pairs={{0,8},{1,9},{2,10},{3,11},{4,12},{5,13},{6,14},{7,15},{8,0},{9,1},... | collective-permute-start | bytes 1032200 | tf_op jit(solution)/shard_map/ppermute | solution.py:506
  213.7 22.6 %collective-permute-start.26 = (bf16[112,1536]{1,0:T(8,128)(2,1)S(1)}, bf16[112,1536]{1,0:T(8,128)(2,1)}, u32[]{:S(2)}, u32[]{:S(2)}) collective-permute-start(bf16[112,1536]{1,0:T(8,128)(2,1)S(1)} %add.109), channel_id=1, source_target_pairs={{0,4},{1,5},{2,6},{3,7},{4,0},{5,1},{6,2},{7,3},{8,12},{9,13},{10,... | collective-permute-start | bytes 1032200 | tf_op jit(solution)/shard_map/ppermute | solution.py:506
  215.0 19.2 %collective-permute-start.29 = (bf16[2,48,1536]{2,1,0:T(8,128)(2,1)S(1)}, bf16[2,48,1536]{2,1,0:T(8,128)(2,1)S(1)}, u32[]{:S(2)}, u32[]{:S(2)}) collective-permute-start(bf16[2,48,1536]{2,1,0:T(8,128)(2,1)S(1)} %pad_maximum_fusion.4), channel_id=1, source_target_pairs={{0,4},{1,5},{2,6},{3,7},{4,0},{5,1},{6,2},{7,3},{8,12},{9,13},{10,... | collective-permute-start | bytes 884744 | tf_op jit(solution)/shard_map/ppermute | solution.py:506
  216.5 17.7 %collective-permute-start.30 = (bf16[2,48,1536]{2,1,0:T(8,128)(2,1)S(1)}, bf16[2,48,1536]{2,1,0:T(8,128)(2,1)S(1)}, u32[]{:S(2)}, u32[]{:S(2)}) collective-permute-start(bf16[2,48,1536]{2,1,0:T(8,128)(2,1)S(1)} %pad_maximum_fusion.6), channel_id=1, source_target_pairs={{0,8},{1,9},{2,10},{3,11},{4,12},{5,13},{6,14},{7,15},{8,0},{9,1},... | collective-permute-start | bytes 884744 | tf_op jit(solution)/shard_map/ppermute | solution.py:506

commit v4 on v3

--- a/solution.py
+++ b/solution.py
@@ -109,13 +109,14 @@
     proj_ref[0, :, 2 * width : 3 * width] = values
     mask = mask_scr[...]
     mask = jnp.concatenate([mask, mask], axis=0)
+    cuts = [slice(128 * p, 128 * (p + 1)) for p in range(pairs)]
+    scores = [nt(jnp.concatenate(lane_split(queries[:, cut]), axis=0), keys[:, cut]) + mask for cut in cuts]
+    tops = [jnp.max(s, axis=-1, keepdims=True) for s in scores]
+    weights = [jnp.exp(s - t) for s, t in zip(scores, tops)]
+    sums = [1.0 / jnp.sum(w, axis=-1, keepdims=True) for w in weights]
+    lows = [(w * t).astype(BF) for w, t in zip(weights, sums)]
     outs = []
-    for p in range(pairs):
-        cut = slice(128 * p, 128 * (p + 1))
-        scores = nt(jnp.concatenate(lane_split(queries[:, cut]), axis=0), keys[:, cut]) + mask
-        highest = jnp.max(scores, axis=-1, keepdims=True)
-        weight = jnp.exp(scores - highest)
-        low = (weight * (1.0 / jnp.sum(weight, axis=-1, keepdims=True))).astype(BF)
+    for p, (low, cut) in enumerate(zip(lows, cuts)):
         probs_ref[0, 2 * rows * p : 2 * rows * (p + 1), :] = low
         both = jnp.concatenate([low[:rows], low[rows:]], axis=1)
         outs.append(nn(both, jnp.concatenate(lane_split(values[:, cut]), axis=0)).astype(BF))
@@ -139,10 +140,14 @@
     wet_ref[...] = we_ref[:, pl.ds(at, strip)].T
     wct_ref[...] = wc_ref[pl.ds(at, strip), :].T
     ebias = row_of(ebias_ref)
-    chunk = 1024
-    for j in range(ff // chunk):
-        cols = slice(chunk * j, chunk * (j + 1))
-        pre = nn(second_low, we_ref[:, cols]) + ebias[:, cols]
+    chunk = 768
+    cuts = [slice(chunk * j, chunk * (j + 1)) for j in range(ff // chunk)]
+    expand = lambda cut: nn(second_low, we_ref[:, cut]) + ebias[:, cut]
+    pres = [expand(cuts[0])]
+    for j, cols in enumerate(cuts):
+        if j + 1 < len(cuts):
+            pres.append(expand(cuts[j + 1]))
+        pre = pres[j]
         square = pre * pre
         half = 0.5 + 0.5 * jnp.tanh(pre * (GELU_A + GELU_A * GELU_B * square))
         act = pre * half
@@ -164,11 +169,19 @@
 
 
 def backward_kernel(
-    cot_ref, g1_ref, g2_ref, wqot_hbm, wet_hbm, wct_hbm,
-    n1_ref, proj_ref, probs_ref, n2_ref, slope_ref, inv_ref,
-    gproj_ref, gattn_ref, gpre_ref, gmlp_ref, gtok_ref, sums_ref,
-    g_scr, s768_scr, s2304_scr, s3072_scr, wqot_ref, wet_ref, wct_ref, sems,
+    spot_ref, cot_ref, g1_ref, g2_ref, wqot_hbm, wet_hbm, wct_hbm,
+    n1_ref, proj_ref, probs_ref, n2_ref, slope_ref, inv_ref, *refs, fused,
 ):
+    if fused:
+        act_hbm, refs = refs[0], refs[1:]
+    gproj_ref, gattn_ref, gpre_ref, gtok_ref, sums_ref, *refs = refs
+    if fused:
+        give_ref, keep_ref, *refs = refs
+    else:
+        gmlp_ref, *refs = refs
+    g_scr, s768_scr, s2304_scr, s3072_scr, wqot_ref, wet_ref, wct_ref, sems, *refs = refs
+    if fused:
+        act_scr, gmlp_scr, tile_scr = refs
     step = pl.program_id(0)
     rows, width = g_scr.shape
     pairs = width // 128
@@ -179,6 +192,14 @@
         pltpu.make_async_copy(wet_hbm, wet_ref, sems.at[1]),
         pltpu.make_async_copy(wqot_hbm, wqot_ref, sems.at[2]),
     ]
+
+    if fused:
+        x, c, r = spot_ref[0], spot_ref[1], spot_ref[3]
+        tall = act_scr.shape[1] // 4
+        for i in range(4):
+            block = (((i & 1) ^ x) * 2 + ((1 - (i >> 1)) ^ c)) * 2 + r
+            source = act_hbm.at[:, pl.ds(pl.multiple_of(block * tall, 128), tall)]
+            loads.append(pltpu.make_async_copy(source, act_scr.at[:, tall * i : tall * (i + 1)], sems.at[3 + i]))
 
     @pl.when(step == 0)
     def _():
@@ -193,7 +214,11 @@
 
     g = g_scr[...]
     gmlp = g.astype(BF)
-    gmlp_ref[0] = gmlp
+    if fused:
+        layer = pl.num_programs(0) - 1 - step
+        gmlp_scr[pl.ds(pl.multiple_of(layer * rows, rows), rows), :] = gmlp
+    else:
+        gmlp_ref[0] = gmlp
     gsec = jnp.zeros((rows, width), F32)
     chunk = 1024
     for j in range(ff // chunk):
@@ -213,22 +238,29 @@
 
     gatt = nn(gattn, wqot_ref[3 * width : 4 * width, :]).astype(BF)
     dqs, dks, dvs = [], [], []
+    outs2, gprobs = [], []
+    for p in range(pairs):
+        v = proj_ref[0, :, 2 * width + 128 * p : 2 * width + 128 * (p + 1)]
+        out2 = jnp.concatenate(lane_split(gatt[:, 128 * p : 128 * (p + 1)]), axis=0)
+        outs2.append(out2)
+        gprobs.append(nt(out2, v))
+    gscores = []
+    for p in range(pairs):
+        prob = probs_ref[0, 2 * rows * p : 2 * rows * (p + 1), :].astype(F32)
+        gs = prob * (gprobs[p] - jnp.sum(prob * gprobs[p], axis=-1, keepdims=True))
+        gscores.append(gs.astype(BF))
     for p in range(pairs):
         q = proj_ref[0, :, 128 * p : 128 * (p + 1)]
         k = proj_ref[0, :, width + 128 * p : width + 128 * (p + 1)]
-        v = proj_ref[0, :, 2 * width + 128 * p : 2 * width + 128 * (p + 1)]
-        out2 = jnp.concatenate(lane_split(gatt[:, 128 * p : 128 * (p + 1)]), axis=0)
+        gscore = gscores[p]
         low = probs_ref[0, 2 * rows * p : 2 * rows * (p + 1), :]
-        prob = low.astype(F32)
-        gprob = nt(out2, v)
-        gscore = prob * (gprob - jnp.sum(prob * gprob, axis=-1, keepdims=True))
-        gscore = gscore.astype(BF)
         both = jnp.concatenate([gscore[:rows], gscore[rows:]], axis=1)
         k2 = jnp.concatenate(lane_split(k), axis=0)
         q2 = jnp.concatenate(lane_split(q), axis=0)
         dqs.append((nn(both, k2) * SCORE_SCALE).astype(BF))
-        dks.append(tn(gscore, q2).astype(BF))
-        dvs.append(tn(low, out2).astype(BF))
+        kv = tn(jnp.concatenate([gscore, low], axis=1), jnp.concatenate([q2, outs2[p]], axis=1))
+        dks.append(kv[:rows, :128].astype(BF))
+        dvs.append(kv[rows:, 128:].astype(BF))
     gproj = jnp.concatenate(dqs + dks + dvs, axis=1)
     gproj_ref[0] = gproj
     gfirst = nn(gproj, wqot_ref[0 : 3 * width, :])
@@ -253,6 +285,16 @@
         sums_ref[6:7, 0:width] = row(s2304_scr[:, 0:width])
         sums_ref[6:7, width : 2 * width] = row(s2304_scr[:, 2 * width : 3 * width])
         sums_ref[7:8, :] = row(s3072_scr[...])
+        if fused:
+            y = spot_ref[2]
+            for load in loads[3:]:
+                load.wait()
+            for out, at in ((give_ref, 0), (keep_ref, 2 * tall)):
+                tile_scr[...] = tn(act_scr[:, at : at + 2 * tall], gmlp_scr[...]).astype(BF)
+                for xrel in (0, 1):
+                    for yrel in (0, 1):
+                        start = pl.multiple_of(xrel * tall + (y ^ yrel) * (tall // 2), 16)
+                        out[xrel, yrel] = tile_scr[pl.ds(start, tall // 2), :]
 
 
 def whole_spec(shape):
@@ -297,33 +339,53 @@
     )(lens, spot, x, *rows_in, wq, wo, we, wc)
 
 
-def backward_all(cot, g1, g2, wqot, wet, wct, n1, proj, probs, n2, slope, inv):
+def backward_all(spot, cot, g1, g2, wqot, wet, wct, n1, proj, probs, n2, slope, inv, act=None):
     layers, rows, width = n1.shape
     ff = wct.shape[1]
+    fused = act is not None
     stack = lambda cols: jax.ShapeDtypeStruct((layers, rows, cols), BF)
-    outs = [stack(3 * width), stack(width), stack(ff), stack(width)]
-    per_layer = lambda s: pl.BlockSpec((1,) + s.shape[1:], lambda i: (layers - 1 - i, 0, 0))
+    outs = [stack(3 * width), stack(width), stack(ff)]
+    per_layer = lambda s: pl.BlockSpec((1,) + s.shape[1:], lambda i, *_: (layers - 1 - i, 0, 0))
     last = [jax.ShapeDtypeStruct((rows, width), BF), jax.ShapeDtypeStruct((8, ff), F32)]
+    out_specs = [per_layer(s) for s in outs] + [whole_spec(s.shape) for s in last]
+    more_in, more_scratch = [], []
+    if fused:
+        more_in = [act]
+        last += [parts_of(ff // 16, width)] * 2
+        out_specs += [whole_spec(last[-1].shape)] * 2
+        more_scratch = [
+            pltpu.VMEM((layers * rows, ff // 2), BF),
+            pltpu.VMEM((layers * rows, width), BF),
+            pltpu.VMEM((ff // 4, width), BF),
+        ]
+    else:
+        last.append(stack(width))
+        out_specs.append(per_layer(last[-1]))
     return pl.pallas_call(
-        backward_kernel,
-        grid=(layers,),
-        in_specs=[whole_spec(a.shape) for a in (cot, g1, g2)]
-        + [pl.BlockSpec(memory_space=pl.ANY)] * 3
-        + [per_layer(a) for a in (n1, proj, probs, n2, slope, inv)],
-        out_specs=[per_layer(s) for s in outs] + [whole_spec(s.shape) for s in last],
+        partial(backward_kernel, fused=fused),
+        grid_spec=pltpu.PrefetchScalarGridSpec(
+            num_scalar_prefetch=1,
+            grid=(layers,),
+            in_specs=[whole_spec(a.shape) for a in (cot, g1, g2)]
+            + [pl.BlockSpec(memory_space=pl.ANY)] * 3
+            + [per_layer(a) for a in (n1, proj, probs, n2, slope, inv)]
+            + [pl.BlockSpec(memory_space=pl.ANY)] * len(more_in),
+            out_specs=out_specs,
+            scratch_shapes=[
+                pltpu.VMEM((rows, width), F32),
+                pltpu.VMEM((6, 8, width), F32),
+                pltpu.VMEM((8, 3 * width), F32),
+                pltpu.VMEM((8, ff), F32),
+                pltpu.VMEM((4 * width, width), BF),
+                pltpu.VMEM((ff, width), BF),
+                pltpu.VMEM((width, ff), BF),
+                pltpu.SemaphoreType.DMA((7,)),
+            ]
+            + more_scratch,
+        ),
         out_shape=outs + last,
-        scratch_shapes=[
-            pltpu.VMEM((rows, width), F32),
-            pltpu.VMEM((6, 8, width), F32),
-            pltpu.VMEM((8, 3 * width), F32),
-            pltpu.VMEM((8, ff), F32),
-            pltpu.VMEM((4 * width, width), BF),
-            pltpu.VMEM((ff, width), BF),
-            pltpu.VMEM((width, ff), BF),
-            pltpu.SemaphoreType.DMA((3,)),
-        ],
         compiler_params=pltpu.CompilerParams(vmem_limit_bytes=VMEM_LIMIT),
-    )(cot, g1, g2, wqot, wet, wct, n1, proj, probs, n2, slope, inv)
+    )(spot, cot, g1, g2, wqot, wet, wct, n1, proj, probs, n2, slope, inv, *more_in)
 
 
 def outer_kernel(spot_ref, left_ref, right_ref, give_ref, keep_ref, scr, *, tall):
@@ -374,53 +436,6 @@
     return pl.CostEstimate(
         flops=2 * depth * rows * cols, transcendentals=0, bytes_accessed=2 * depth * (rows + cols) + 2 * rows * cols
     )
-
-
-def contract_kernel(spot_ref, left_ref, right_ref, give_ref, keep_ref, scr):
-    step = pl.program_id(0)
-    y = spot_ref[2]
-    tall = scr.shape[0] // 2
-    scr[...] = tn(left_ref[...], right_ref[...]).astype(BF)
-    for yrel in (0, 1):
-        start = pl.multiple_of((y ^ yrel) * tall, tall)
-
-        @pl.when(step < 2)
-        def _():
-            give_ref[0, yrel] = scr[pl.ds(start, tall), :]
-
-        @pl.when(step >= 2)
-        def _():
-            keep_ref[0, yrel] = scr[pl.ds(start, tall), :]
-
-
-def contract_grads(spot, left, right):
-    depth, ff = left.shape
-    width = right.shape[1]
-    tall = ff // 8
-
-    def column(i, s):
-        return (0, (((i & 1) ^ s[0]) * 2 + ((1 - (i >> 1)) ^ s[1])) * 2 + s[3])
-
-    out = parts_of(tall // 2, width)
-    return pl.pallas_call(
-        contract_kernel,
-        grid_spec=pltpu.PrefetchScalarGridSpec(
-            num_scalar_prefetch=1,
-            grid=(4,),
-            in_specs=[
-                pl.BlockSpec((depth, tall), column),
-                pl.BlockSpec((depth, width), lambda i, s: (0, 0)),
-            ],
-            out_specs=[
-                pl.BlockSpec((1, 2, tall // 2, width), lambda i, s: (jnp.minimum(i, 1), 0, 0, 0)),
-                pl.BlockSpec((1, 2, tall // 2, width), lambda i, s: (jnp.maximum(i - 2, 0), 0, 0, 0)),
-            ],
-            scratch_shapes=[pltpu.VMEM((tall, width), BF)],
-        ),
-        out_shape=[out, out],
-        cost_estimate=cost_of(depth, ff // 2, width),
-        compiler_params=pltpu.CompilerParams(vmem_limit_bytes=VMEM_LIMIT),
-    )(spot, left, right)
 
 
 def attention_kernel(
@@ -558,20 +573,21 @@
         [first_gain, first_shift, qv_bias, out_bias, second_gain, second_shift, expand_bias, contract_bias],
         qkv_weight, out_weight, expand_weight, contract_weight, sections,
     )
-    gproj, gattn, gpre, gmlp, gtok, sums = backward_all(
-        cot, first_gain, second_gain, wqot, wet, wct, n1, proj, probs, n2, slope, inv,
-    )
-
     flat = lambda a: a.reshape(-1, a.shape[-1])
     first, att, second, act = flat(first), flat(att), flat(second), flat(act)
-    gproj, gattn, gpre, gmlp = flat(gproj), flat(gattn), flat(gpre), flat(gmlp)
+    known = (sections, dps) == (8, 4)
+    gproj, gattn, gpre, gtok, sums, *contract = backward_all(
+        spot, cot, first_gain, second_gain, wqot, wet, wct, n1, proj, probs, n2, slope, inv,
+        act if known else None,
+    )
+    gproj, gattn, gpre = flat(gproj), flat(gattn), flat(gpre)
     both = jnp.concatenate([last, gtok], axis=1).reshape(sections, piece_rows, 2 * width)
     blocks = [
         lax.dynamic_index_in_dim(both, label_of(label ^ k), 0, keepdims=False) for k in range(0, sections, 2)
     ]
-    if (sections, dps) == (8, 4):
+    if known:
         g_qkv, g_out, g_exp, g_con, v, back = grads_small_slice(
-            section, dp, spot, first, att, second, act, gproj, gattn, gpre, gmlp, sums, blocks
+            section, dp, spot, first, att, second, gproj, gattn, gpre, contract, sums, blocks
         )
     else:
         half = (label & 1) == 0
@@ -582,7 +598,7 @@
             return lax.psum(own, "section").astype(F32)
 
         g_qkv, g_out = everywhere(tn(first, gproj)), everywhere(tn(att, gattn))
-        g_exp, g_con = everywhere(tn(second, gpre)), everywhere(tn(act, gmlp))
+        g_exp, g_con = everywhere(tn(second, gpre)), everywhere(tn(act, flat(contract[0])))
         v = [everywhere(sums[i, :n]) for i, n in enumerate([width] * 6 + [2 * width, ff])]
         back = blocks[:1] + [
             lax.ppermute(block, "section", by_label(2 * i + 2, sections)) for i, block in enumerate(blocks[1:])
@@ -596,18 +612,18 @@
     )
 
 
-def grads_small_slice(section, dp, spot, first, att, second, act, gproj, gattn, gpre, gmlp, sums, blocks):
+def grads_small_slice(section, dp, spot, first, att, second, gproj, gattn, gpre, contract, sums, blocks):
     sections, dps = 8, 4
     y, r, core = section & 1, (section >> 1) & 1, dp & 1
-    width, ff = first.shape[1], act.shape[1]
+    width, ff = first.shape[1], gpre.shape[1]
     hop = partial(move, sections=sections, dps=dps)
     cols = 2 * width
     tall = width // 8
     tie = lax.optimization_barrier
-    add_a = over_core(*contract_grads(spot, act, gmlp), dps)
+    add_a = over_core(*contract, dps)
     second, gpre, add_a = tie((second, gpre, add_a))
     from_a, out_b = plane_parts(add_a, hop), expand_grads(spot, second, gpre)
-    from_a, out_b = tie((from_a, out_b))
+    from_a, out_b, blocks = tie((from_a, out_b, blocks))
     plane_a = plane_sum(add_a, from_a)
     z_a, add_b = hop(plane_a, 0, 0, 2), over_core(*out_b, dps)
     first, gproj, att, gattn, add_b = tie((first, gproj, att, gattn, add_b))
@@ -615,7 +631,7 @@
     from_b, out_c, z_a = tie((from_b, out_c, z_a))
     plane_b, total_a = plane_sum(add_b, from_b), plane_a + z_a
     z_b = hop(jnp.concatenate([plane_b, blocks[2], blocks[3]], axis=0), 0, 0, 2)
-    r_a, add_c = hop(total_a, 0, 0, 1), over_core(*out_c, dps)
+    r_a, add_c = hop(total_a, 0, 0, 1), over_core(*out_c, dps)[:, :, : tall + 2]
     from_c = plane_parts(add_c, hop)
     from_c, z_b, r_a = tie((from_c, z_b, r_a))
     pieces = (z_b.shape[0] - tall) // 2
@@ -634,19 +650,22 @@
     stacked = lambda a, b: jnp.concatenate([a, b], axis=0)
     con = total_a, y_a[0], r_a, y_a[1]
     exp = total_b, stacked(y_top[0], y_bottom), stacked(r_top, r_bottom[0]), stacked(y_top[1], r_bottom[1])
-    con, exp, att_part = in_order(con, y, r), in_order(exp, y, r), in_order([p[:tall] for p in rest], y, r)
+    con, att_part = in_order(con, y, r), in_order([p[:tall] for p in rest], y, r)
     g_con = jnp.concatenate([con[0][0], con[0][1], con[1][0], con[1][1]], axis=0)
-    g_exp = jnp.concatenate([jnp.concatenate([exp[0][j], exp[1][j]], axis=1) for j in (0, 1)], axis=0)
     wide = gproj.shape[1] // 2
     side = lambda a, b: jnp.concatenate(
         [jnp.concatenate([att_part[0][j][:, a:b], att_part[1][j][:, a:b]], axis=1) for j in (0, 1)], axis=0
     )
-    vectors = rest[0][tall:].astype(F32)
+    g_qkv, g_out, last_b = tie((side(0, wide), side(wide, cols), exp[0]))
+    exp = in_order((last_b,) + exp[1:], y, r)
+    g_exp = jnp.concatenate([jnp.concatenate([exp[0][j], exp[1][j]], axis=1) for j in (0, 1)], axis=0)
+    g_con, vectors = tie((g_con, rest[0][tall:]))
+    vectors = vectors.astype(F32)
     windows = vectors[0].reshape(6, -1)
     quarter = width // 4
     windows = jnp.where(core == 0, windows[:, :quarter], windows[:, 64 : 64 + quarter])
     v = [windows[i] for i in range(6)] + [vectors[1, : 2 * quarter], vectors[1, 2 * quarter : 2 * quarter + ff // 4]]
-    return side(0, wide), side(wide, cols), g_exp, g_con, v, back
+    return g_qkv, g_out, g_exp, g_con, v, back
 
 
 def solution(mesh):

time: 241 us -> 217 us (0.900)
  Pallas kernels: 110 us -> 94 us
  other arithmetic: 18.3 us -> 15.8 us
    pallas_call x2 -> x1, Pallas kernels: 53.7 us -> 40.9 us  [backward_all(): pl.pallas_call(partial(backward_kernel, fused=fused), grid_spec=pltpu.Pre...]
    pallas_call x1, Pallas kernels: 41.6 us -> 38.2 us  [forward_all(): pl.pallas_call(forward_kernel, grid_spec=pltpu.PrefetchScalarGridSpec(num...]
    ppermute x21, waiting for transfers between devices: 53.1 us -> 50 us  [move(): return lax.ppermute(array, AXES, pairs)]
  transfers between devices with their start and end apart: 31 -> 31, of which waited for: 15 -> 14; matrix products, arithmetic and copies ran while one was open for 7% -> 5% of each run, Pallas kernels for 6% -> 7%
where the time goes in v4:
time: 217 us; the launch traced here: 216 us
  Pallas kernels  94 us (43%)
  waiting for transfers between devices  64.6 us (30%)
  starting transfers between devices  33.9 us (16%)
  other arithmetic  15.8 us (7%)
  local copies, waits for them, and re-layouts  6.45 us (3%)
    ppermute x21, waiting for transfers between devices, move(): return lax.ppermute(array, AXES, pairs)  50 us
    pallas_call x1, Pallas kernels, backward_all(): pl.pallas_call(partial(backward_kernel, fused=fused), grid_spec=pltpu.Pre...  40.9 us
    pallas_call x1, Pallas kernels, forward_all(): pl.pallas_call(forward_kernel, grid_spec=pltpu.PrefetchScalarGridSpec(num...  38.2 us
    ppermute x21, starting transfers between devices, move(): return lax.ppermute(array, AXES, pairs)  21.8 us
    ppermute x7, starting transfers between devices, body(): lax.ppermute(block, 'section', by_label(k, sections))  12 us
    pallas_call x1, Pallas kernels, attention_grads(): pl.pallas_call(attention_kernel, grid_spec=pltpu.PrefetchScalarGridSpec(n...  8.21 us
    ppermute x3, waiting for transfers between devices, over_core(): return keep + lax.ppermute(give, 'dp', [(d, d ^ 1) for d in range(dps)])  7.63 us
    ppermute x7, waiting for transfers between devices, body(): lax.ppermute(block, 'section', by_label(k, sections))  6.98 us
  transfers between devices with their start and end apart: 31, of which 14 were waited for; matrix products, arithmetic and copies ran while one was open for 5% of the time, Pallas kernels for 7%

profile of v4, /device:TPU:0, one launch (start us, length us, event | category | flops | bytes accessed | tf_op | source)
XLA Modules:
  0.0 216.1 jit_solution(6712070770461459293)
XLA Ops:
  0.7 0.9 fusion.24
  1.6 3.1 %collective-permute-start = (bf16[16,1536]{1,0:T(8,128)(2,1)S(1)}, bf16[16,1536]{1,0:T(8,128)(2,1)S(1)}, u32[]{:S(2)}, u32[]{:S(2)}) collective-permute-start(bf16[16,1536]{1,0:T(8,128)(2,1)S(1)} %get-tuple-element.183), channel_id=1, source_target_pairs={{0,8},{4,12},{8,0},{12,4},{16,24},{20,28},{24,16},{28,20},{1,9},{5... | collective-permute-start | bytes 147464 | tf_op jit(solution)/shard_map/ppermute | solution.py:566
  4.7 0.8 fusion.38
  5.5 3.6 %collective-permute-start.5 = (bf16[16,1536]{1,0:T(8,128)(2,1)S(1)}, bf16[16,1536]{1,0:T(8,128)(2,1)S(1)}, u32[]{:S(2)}, u32[]{:S(2)}) collective-permute-start(bf16[16,1536]{1,0:T(8,128)(2,1)S(1)} %get-tuple-element.187), channel_id=1, source_target_pairs={{0,20},{4,16},{8,28},{12,24},{16,4},{20,0},{24,12},{28,8},{1,21},{... | collective-permute-start | bytes 147464 | tf_op jit(solution)/shard_map/ppermute | solution.py:566
  9.3 3.6 %collective-permute-start.6 = (bf16[16,1536]{1,0:T(8,128)(2,1)S(1)}, bf16[16,1536]{1,0:T(8,128)(2,1)S(1)}, u32[]{:S(2)}, u32[]{:S(2)}) collective-permute-start(bf16[16,1536]{1,0:T(8,128)(2,1)S(1)} %get-tuple-element.181), channel_id=1, source_target_pairs={{0,28},{4,24},{8,20},{12,16},{16,12},{20,8},{24,4},{28,0},{1,29},{... | collective-permute-start | bytes 147464 | tf_op jit(solution)/shard_map/ppermute | solution.py:566
  12.9 1.5 collective-permute-start.1
  15.0 2.0 collective-permute-done.1
  17.0 3.5 %collective-permute-done.2 = bf16[16,1536]{1,0:T(8,128)(2,1)S(1)} collective-permute-done((bf16[16,1536]{1,0:T(8,128)(2,1)S(1)}, bf16[16,1536]{1,0:T(8,128)(2,1)S(1)}, u32[]{:S(2)}, u32[]{:S(2)}) %collective-permute-start.2) | collective-permute-done | bytes 49184 | tf_op jit(solution)/shard_map/ppermute | solution.py:566
  20.5 1.5 collective-permute-done.3
  22.4 0.8 fusion.39
  23.1 38.2 %shard_map.254 = (bf16[8,128,768]{2,1,0:T(8,128)(2,1)}, bf16[8,128,768]{2,1,0:T(8,128)(2,1)}, bf16[8,128,2304]{2,1,0:T(8,128)(2,1)}, bf16[8,1536,128]{2,1,0:T(8,...) custom-call(s32[4,4]{1,0:T(4,128)} %bitcast.162, ...), custom_call_target="tpu_custom_call" | custom-call | tf_op jit(solution)/shard_map/pallas_call | solution.py:320
  61.4 40.9 %shard_map.255 = (bf16[8,128,2304]{2,1,0:T(8,128)(2,1)}, bf16[8,128,768]{2,1,0:T(8,128)(2,1)}, bf16[8,128,3072]{2,1,0:T(8,128)(2,1)}, bf16[128,768]{1,0:T(8,128)...) custom-call(s32[5]{0:T(128)} %stack.90.spot_ref, ...), custom_call_target="tpu_custom_call" | custom-call | tf_op jit(solution)/shard_map/pallas_call | solution.py:364
  102.4 1.0 pad_maximum_fusion.2
  103.4 2.0 collective-permute-done.7
  105.4 1.5 add.91
  107.0 2.6 %collective-permute-start.10 = (bf16[192,768]{1,0:T(8,128)(2,1)S(1)}, bf16[192,768]{1,0:T(8,128)(2,1)S(1)}, u32[]{:S(2)}, u32[]{:S(2)}) collective-permute-start(bf16[192,768]{1,0:T(8,128)(2,1)S(1)} %get-tuple-element.156), channel_id=1, source_target_pairs={{0,6},{1,7},{2,4},{3,5},{4,2},{5,3},{6,0},{7,1},{8,14},{9,15},{10,... | collective-permute-start | bytes 884744 | tf_op jit(solution)/shard_map/ppermute | solution.py:521
  110.6 0.6 dynamic-slice_bitcast_fusion
  111.2 6.7 %shard_map.256 = (bf16[2,2,96,1536]{3,2,1,0:T(8,128)(2,1)}, bf16[2,2,96,1536]{3,2,1,0:T(8,128)(2,1)}) custom-call(s32[5]{0:T(128)} %stack.90.spot_ref, bf16[1024,768]{1,0:T(8,128)(2,1)} %bitcast.170, bf16[1024,3072]{1,0:T(8,128)(2,1)} %bitcast.169), custom_call_target="tpu_custom_call" | custom-call | flops 2415919104 | bytes 7077888 | tf_op jit(solution)/shard_map/pallas_call | solution.py:417
  117.9 5.5 %collective-permute-done.9 = bf16[192,768]{1,0:T(8,128)(2,1)S(1)} collective-permute-done((bf16[192,768]{1,0:T(8,128)(2,1)S(1)}, bf16[192,768]{1,0:T(8,128)(2,1)S(1)}, u32[]{:S(2)}, u32[]{:S(2)}) %collective-permute-start.9) | collective-permute-done | bytes 294944 | tf_op jit(solution)/shard_map/ppermute | solution.py:521
  123.8 2.7 %collective-permute-done.11 = bf16[2,2,96,1536]{3,2,1,0:T(8,128)(2,1)S(1)} collective-permute-done((bf16[2,2,96,1536]{3,2,1,0:T(8,128)(2,1)}, bf16[2,2,96,1536]{3,2,1,0:T(8,128)(2,1)S(1)}, u32[]{:S(2)}, u32[]{:S(2)}) %collective-permute-start.11) | collective-permute-done | bytes 1179680 | tf_op jit(solution)/shard_map/ppermute | solution.py:525
  127.0 1.7 collective-permute-start.14
  128.6 1.4 collective-permute-start.13
  130.5 8.2 %shard_map.257 = (bf16[2,2,112,1536]{3,2,1,0:T(8,128)(2,1)}, bf16[2,2,112,1536]{3,2,1,0:T(8,128)(2,1)}) custom-call(s32[5]{0:T(128)} %stack.90.spot_ref, bf16[1024,768]{1,0:T(8,128)(2,1)} %bitcast.144, bf16[1024,2304]{1,0:T(8,128)(2,1)} %bitcast.142, bf16[1024,768]{1,0:T(8,128)(2,1)} %bitcast.145, bf16[1024,768]{1,0:T(8,128)(2,1)} %bitcast.146, ...), custom_call_target="tpu_custom_call" | custom-call | flops 2415919104 | bytes 7077888 | tf_op jit(solution)/shard_map/pallas_call | solution.py:479
  138.7 1.1 collective-permute-done.15
  139.8 3.5 %collective-permute-done.13 = bf16[96,1536]{1,0:T(8,128)(2,1)S(1)} collective-permute-done((bf16[96,1536]{1,0:T(8,128)(2,1)S(1)}, bf16[96,1536]{1,0:T(8,128)(2,1)S(1)}, u32[]{:S(2)}, u32[]{:S(2)}) %collective-permute-start.13) | collective-permute-done | bytes 294944 | tf_op jit(solution)/shard_map/ppermute | solution.py:521
  143.8 2.9 %collective-permute-done.16 = bf16[2,2,112,1536]{3,2,1,0:T(8,128)(2,1)S(1)} collective-permute-done((bf16[2,2,112,1536]{3,2,1,0:T(8,128)(2,1)}, bf16[2,2,112,1536]{3,2,1,0:T(8,128)(2,1)S(1)}, u32[]{:S(2)}, u32[]{:S(2)}) %collective-permute-start.16) | collective-permute-done | bytes 1376288 | tf_op jit(solution)/shard_map/ppermute | solution.py:525
  147.1 1.7 collective-permute-start.19
  148.7 1.4 collective-permute-start.18
  150.8 16.5 %collective-permute-done.21 = bf16[192,768]{1,0:T(8,128)(2,1)S(1)} collective-permute-done((bf16[192,768]{1,0:T(8,128)(2,1)S(1)}, bf16[192,768]{1,0:T(8,128)(2,1)S(1)}, u32[]{:S(2)}, u32[]{:S(2)}) %collective-permute-start.21) | collective-permute-done | bytes 294944 | tf_op jit(solution)/shard_map/ppermute | solution.py:521
  167.6 0.7 slice_bitcast_fusion.20
  168.4 1.5 collective-permute-start.23
  169.9 0.6 slice_bitcast_fusion.17
  170.5 0.7 pad_maximum_fusion.9
  171.8 1.9 collective-permute-start.24
  173.7 9.8 %collective-permute-done.24 = bf16[48,1536]{1,0:T(8,128)(2,1)S(1)} collective-permute-done((bf16[48,1536]{1,0:T(8,128)(2,1)}, bf16[48,1536]{1,0:T(8,128)(2,1)S(1)}, u32[]{:S(2)}, u32[]{:S(2)}) %collective-permute-start.24) | collective-permute-done | bytes 147488 | tf_op jit(solution)/shard_map/ppermute | solution.py:521
  183.5 3.9 %collective-permute-done.25 = bf16[80,1536]{1,0:T(8,128)(2,1)S(1)} collective-permute-done((bf16[80,1536]{1,0:T(8,128)(2,1)}, bf16[80,1536]{1,0:T(8,128)(2,1)S(1)}, u32[]{:S(2)}, u32[]{:S(2)}) %collective-permute-start.25) | collective-permute-done | bytes 245792 | tf_op jit(solution)/shard_map/ppermute | solution.py:521
  187.4 0.7 slice_bitcast_fusion.18
  188.1 1.1 add.109
  189.2 2.5 %collective-permute-start.28 = (bf16[98,1536]{1,0:T(8,128)(2,1)S(1)}, bf16[98,1536]{1,0:T(8,128)(2,1)S(1)}, u32[]{:S(2)}, u32[]{:S(2)}) collective-permute-start(bf16[98,1536]{1,0:T(8,128)(2,1)S(1)} %add.109), channel_id=1, source_target_pairs={{0,12},{1,13},{2,14},{3,15},{4,8},{5,9},{6,10},{7,11},{8,4},{9,5},... | collective-permute-start | bytes 903176 | tf_op jit(solution)/shard_map/ppermute | solution.py:521
  193.0 1.6 pad_maximum_fusion
  195.3 1.5 collective-permute-start.29
  196.8 1.6 collective-permute-start.30
  199.9 0.7 fusion.22
  200.6 9.6 %collective-permute-done.29 = bf16[2,48,1536]{2,1,0:T(8,128)(2,1)S(1)} collective-permute-done((bf16[2,48,1536]{2,1,0:T(8,128)(2,1)S(1)}, bf16[2,48,1536]{2,1,0:T(8,128)(2,1)S(1)}, u32[]{:S(2)}, u32[]{:S(2)}) %collective-permute-start.29) | collective-permute-done | bytes 294944 | tf_op jit(solution)/shard_map/ppermute | solution.py:521
  210.3 1.3 fusion.10
  211.9 1.3 maximum_maximum_fusion.1
  213.2 0.9 maximum_maximum_fusion.2
  214.5 1.6 maximum_maximum_fusion
  (102 shorter events, 10.2 us)
Async XLA Ops:
  1.6 13.4 %collective-permute-start = (bf16[16,1536]{1,0:T(8,128)(2,1)S(1)}, bf16[16,1536]{1,0:T(8,128)(2,1)S(1)}, u32[]{:S(2)}, u32[]{:S(2)}) collective-permute-start(bf16[16,1536]{1,0:T(8,128)(2,1)S(1)} %get-tuple-element.183), channel_id=1, source_target_pairs={{0,8},{4,12},{8,0},{12,4},{16,24},{20,28},{24,16},{28,20},{1,9},{5... | collective-permute-start | bytes 147464 | tf_op jit(solution)/shard_map/ppermute | solution.py:566
  5.5 16.5 %collective-permute-start.5 = (bf16[16,1536]{1,0:T(8,128)(2,1)S(1)}, bf16[16,1536]{1,0:T(8,128)(2,1)S(1)}, u32[]{:S(2)}, u32[]{:S(2)}) collective-permute-start(bf16[16,1536]{1,0:T(8,128)(2,1)S(1)} %get-tuple-element.187), channel_id=1, source_target_pairs={{0,20},{4,16},{8,28},{12,24},{16,4},{20,0},{24,12},{28,8},{1,21},{... | collective-permute-start | bytes 147464 | tf_op jit(solution)/shard_map/ppermute | solution.py:566
  9.1 12.9 %collective-permute-start.4 = (bf16[16,1536]{1,0:T(8,128)(2,1)S(1)}, bf16[16,1536]{1,0:T(8,128)(2,1)S(1)}, u32[]{:S(2)}, u32[]{:S(2)}) collective-permute-start(bf16[16,1536]{1,0:T(8,128)(2,1)S(1)} %get-tuple-element.188), channel_id=1, source_target_pairs={{0,24},{4,28},{8,16},{12,20},{16,8},{20,12},{24,0},{28,4},{1,25},{... | collective-permute-start | bytes 147464 | tf_op jit(solution)/shard_map/ppermute | solution.py:566
  9.3 12.7 %collective-permute-start.6 = (bf16[16,1536]{1,0:T(8,128)(2,1)S(1)}, bf16[16,1536]{1,0:T(8,128)(2,1)S(1)}, u32[]{:S(2)}, u32[]{:S(2)}) collective-permute-start(bf16[16,1536]{1,0:T(8,128)(2,1)S(1)} %get-tuple-element.181), channel_id=1, source_target_pairs={{0,28},{4,24},{8,20},{12,16},{16,12},{20,8},{24,4},{28,0},{1,29},{... | collective-permute-start | bytes 147464 | tf_op jit(solution)/shard_map/ppermute | solution.py:566
  12.9 4.1 %collective-permute-start.1 = (bf16[16,1536]{1,0:T(8,128)(2,1)S(1)}, bf16[16,1536]{1,0:T(8,128)(2,1)S(1)}, u32[]{:S(2)}, u32[]{:S(2)}) collective-permute-start(bf16[16,1536]{1,0:T(8,128)(2,1)S(1)} %get-tuple-element.184), channel_id=1, source_target_pairs={{0,4},{4,0},{8,12},{12,8},{16,20},{20,16},{24,28},{28,24},{1,5},{5... | collective-permute-start | bytes 147464 | tf_op jit(solution)/shard_map/ppermute | solution.py:566
  15.0 5.5 %collective-permute-start.2 = (bf16[16,1536]{1,0:T(8,128)(2,1)S(1)}, bf16[16,1536]{1,0:T(8,128)(2,1)S(1)}, u32[]{:S(2)}, u32[]{:S(2)}) collective-permute-start(bf16[16,1536]{1,0:T(8,128)(2,1)S(1)} %get-tuple-element.185), channel_id=1, source_target_pairs={{0,12},{4,8},{8,4},{12,0},{16,28},{20,24},{24,20},{28,16},{1,13},{... | collective-permute-start | bytes 147464 | tf_op jit(solution)/shard_map/ppermute | solution.py:566
  17.0 5.0 %collective-permute-start.3 = (bf16[16,1536]{1,0:T(8,128)(2,1)S(1)}, bf16[16,1536]{1,0:T(8,128)(2,1)S(1)}, u32[]{:S(2)}, u32[]{:S(2)}) collective-permute-start(bf16[16,1536]{1,0:T(8,128)(2,1)S(1)} %get-tuple-element.186), channel_id=1, source_target_pairs={{0,16},{4,20},{8,24},{12,28},{16,0},{20,4},{24,8},{28,12},{1,17},{... | collective-permute-start | bytes 147464 | tf_op jit(solution)/shard_map/ppermute | solution.py:566
  61.4 41.1 %copy-start.7 = (bf16[128,768]{1,0:T(8,128)(2,1)S(1)}, bf16[128,768]{1,0:T(8,128)(2,1)}, u32[]{:S(2)}) copy-start(bf16[128,768]{1,0:T(8,128)(2,1)} %get-tuple-element.95) | copy-start | bytes 589828
  102.3 3.1 %collective-permute-start.7 = (bf16[2,2,192,768]{3,2,1,0:T(8,128)(2,1)}, bf16[2,2,192,768]{3,2,1,0:T(8,128)(2,1)S(1)}, u32[]{:S(2)}, u32[]{:S(2)}) collective-permute-start(bf16[2,2,192,768]{3,2,1,0:T(8,128)(2,1)} %get-tuple-element.89), channel_id=1, source_target_pairs={{0,1},{1,0},{2,3},{3,2},{4,5},{5,4},{6,7},{7,6},{8,9},{9,8},{10,11... | collective-permute-start | bytes 3538952 | tf_op jit(solution)/shard_map/ppermute | solution.py:525
  107.0 10.9 %collective-permute-start.10 = (bf16[192,768]{1,0:T(8,128)(2,1)S(1)}, bf16[192,768]{1,0:T(8,128)(2,1)S(1)}, u32[]{:S(2)}, u32[]{:S(2)}) collective-permute-start(bf16[192,768]{1,0:T(8,128)(2,1)S(1)} %get-tuple-element.156), channel_id=1, source_target_pairs={{0,6},{1,7},{2,4},{3,5},{4,2},{5,3},{6,0},{7,1},{8,14},{9,15},{10,... | collective-permute-start | bytes 884744 | tf_op jit(solution)/shard_map/ppermute | solution.py:521
  109.6 13.8 %collective-permute-start.9 = (bf16[192,768]{1,0:T(8,128)(2,1)S(1)}, bf16[192,768]{1,0:T(8,128)(2,1)S(1)}, u32[]{:S(2)}, u32[]{:S(2)}) collective-permute-start(bf16[192,768]{1,0:T(8,128)(2,1)S(1)} %get-tuple-element.157), channel_id=1, source_target_pairs={{0,4},{1,5},{2,6},{3,7},{4,0},{5,1},{6,2},{7,3},{8,12},{9,13},{10,... | collective-permute-start | bytes 884744 | tf_op jit(solution)/shard_map/ppermute | solution.py:521
  110.1 13.4 %collective-permute-start.8 = (bf16[192,768]{1,0:T(8,128)(2,1)S(1)}, bf16[192,768]{1,0:T(8,128)(2,1)S(1)}, u32[]{:S(2)}, u32[]{:S(2)}) collective-permute-start(bf16[192,768]{1,0:T(8,128)(2,1)S(1)} %get-tuple-element.158), channel_id=1, source_target_pairs={{0,2},{1,3},{2,0},{3,1},{4,6},{5,7},{6,4},{7,5},{8,10},{9,11},{10,... | collective-permute-start | bytes 884744 | tf_op jit(solution)/shard_map/ppermute | solution.py:521
  117.9 8.7 %copy-start.1 = (bf16[2,2,96,1536]{3,2,1,0:T(8,128)(2,1)S(1)}, bf16[2,2,96,1536]{3,2,1,0:T(8,128)(2,1)}, u32[]{:S(2)}) copy-start(bf16[2,2,96,1536]{3,2,1,0:T(8,128)(2,1)} %get-tuple-element.102) | copy-start | bytes 3538948
  123.5 3.1 %collective-permute-start.11 = (bf16[2,2,96,1536]{3,2,1,0:T(8,128)(2,1)}, bf16[2,2,96,1536]{3,2,1,0:T(8,128)(2,1)S(1)}, u32[]{:S(2)}, u32[]{:S(2)}) collective-permute-start(bf16[2,2,96,1536]{3,2,1,0:T(8,128)(2,1)} %get-tuple-element.103), channel_id=1, source_target_pairs={{0,1},{1,0},{2,3},{3,2},{4,5},{5,4},{6,7},{7,6},{8,9},{9,8},{10,11... | collective-permute-start | bytes 3538952 | tf_op jit(solution)/shard_map/ppermute | solution.py:525
  123.7 16.1 %collective-permute-start.15 = (bf16[192,768]{1,0:T(8,128)(2,1)S(1)}, bf16[192,768]{1,0:T(8,128)(2,1)S(1)}, u32[]{:S(2)}, u32[]{:S(2)}) collective-permute-start(bf16[192,768]{1,0:T(8,128)(2,1)S(1)} %fusion.8), channel_id=1, source_target_pairs={{0,16},{1,17},{2,18},{3,19},{4,20},{5,21},{6,22},{7,23},{8,24},{9,... | collective-permute-start | bytes 884744 | tf_op jit(solution)/shard_map/ppermute | solution.py:521
  127.0 12.8 %collective-permute-start.14 = (bf16[96,1536]{1,0:T(8,128)(2,1)S(1)}, bf16[96,1536]{1,0:T(8,128)(2,1)S(1)}, u32[]{:S(2)}, u32[]{:S(2)}) collective-permute-start(bf16[96,1536]{1,0:T(8,128)(2,1)S(1)} %get-tuple-element.153), channel_id=1, source_target_pairs={{0,6},{1,7},{2,4},{3,5},{4,2},{5,3},{6,0},{7,1},{8,14},{9,15},{10,... | collective-permute-start | bytes 884744 | tf_op jit(solution)/shard_map/ppermute | solution.py:521
  128.6 14.7 %collective-permute-start.13 = (bf16[96,1536]{1,0:T(8,128)(2,1)S(1)}, bf16[96,1536]{1,0:T(8,128)(2,1)S(1)}, u32[]{:S(2)}, u32[]{:S(2)}) collective-permute-start(bf16[96,1536]{1,0:T(8,128)(2,1)S(1)} %get-tuple-element.154), channel_id=1, source_target_pairs={{0,4},{1,5},{2,6},{3,7},{4,0},{5,1},{6,2},{7,3},{8,12},{9,13},{10,... | collective-permute-start | bytes 884744 | tf_op jit(solution)/shard_map/ppermute | solution.py:521
  130.0 13.3 %collective-permute-start.12 = (bf16[96,1536]{1,0:T(8,128)(2,1)S(1)}, bf16[96,1536]{1,0:T(8,128)(2,1)S(1)}, u32[]{:S(2)}, u32[]{:S(2)}) collective-permute-start(bf16[96,1536]{1,0:T(8,128)(2,1)S(1)} %get-tuple-element.155), channel_id=1, source_target_pairs={{0,2},{1,3},{2,0},{3,1},{4,6},{5,7},{6,4},{7,5},{8,10},{9,11},{10,... | collective-permute-start | bytes 884744 | tf_op jit(solution)/shard_map/ppermute | solution.py:521
  138.7 7.9 %copy-start = (bf16[2,2,112,1536]{3,2,1,0:T(8,128)(2,1)S(1)}, bf16[2,2,112,1536]{3,2,1,0:T(8,128)(2,1)}, u32[]{:S(2)}) copy-start(bf16[2,2,112,1536]{3,2,1,0:T(8,128)(2,1)} %get-tuple-element.115) | copy-start | bytes 4128772
  143.3 3.3 %collective-permute-start.16 = (bf16[2,2,112,1536]{3,2,1,0:T(8,128)(2,1)}, bf16[2,2,112,1536]{3,2,1,0:T(8,128)(2,1)S(1)}, u32[]{:S(2)}, u32[]{:S(2)}) collective-permute-start(bf16[2,2,112,1536]{3,2,1,0:T(8,128)(2,1)} %get-tuple-element.116), channel_id=1, source_target_pairs={{0,1},{1,0},{2,3},{3,2},{4,5},{5,4},{6,7},{7,6},{8,9},{9,8},{10,11... | collective-permute-start | bytes 4128776 | tf_op jit(solution)/shard_map/ppermute | solution.py:525
  143.5 23.8 %collective-permute-start.20 = (bf16[128,1536]{1,0:T(8,128)(2,1)S(1)}, bf16[128,1536]{1,0:T(8,128)(2,1)S(1)}, u32[]{:S(2)}, u32[]{:S(2)}) collective-permute-start(bf16[128,1536]{1,0:T(8,128)(2,1)S(1)} %pad_maximum_fusion.3), channel_id=1, source_target_pairs={{0,16},{1,17},{2,18},{3,19},{4,20},{5,21},{6,22},{7,23},{8,24},{9,... | collective-permute-start | bytes 1179656 | tf_op jit(solution)/shard_map/ppermute | solution.py:521
  147.1 20.2 %collective-permute-start.19 = (bf16[98,1536]{1,0:T(8,128)(2,1)S(1)}, bf16[98,1536]{1,0:T(8,128)(2,1)S(1)}, u32[]{:S(2)}, u32[]{:S(2)}) collective-permute-start(bf16[98,1536]{1,0:T(8,128)(2,1)S(1)} %get-tuple-element.138), channel_id=1, source_target_pairs={{0,6},{1,7},{2,4},{3,5},{4,2},{5,3},{6,0},{7,1},{8,14},{9,15},{10,... | collective-permute-start | bytes 903176 | tf_op jit(solution)/shard_map/ppermute | solution.py:521
  148.7 18.6 %collective-permute-start.18 = (bf16[98,1536]{1,0:T(8,128)(2,1)S(1)}, bf16[98,1536]{1,0:T(8,128)(2,1)S(1)}, u32[]{:S(2)}, u32[]{:S(2)}) collective-permute-start(bf16[98,1536]{1,0:T(8,128)(2,1)S(1)} %get-tuple-element.139), channel_id=1, source_target_pairs={{0,4},{1,5},{2,6},{3,7},{4,0},{5,1},{6,2},{7,3},{8,12},{9,13},{10,... | collective-permute-start | bytes 903176 | tf_op jit(solution)/shard_map/ppermute | solution.py:521
  150.1 17.2 %collective-permute-start.17 = (bf16[98,1536]{1,0:T(8,128)(2,1)S(1)}, bf16[98,1536]{1,0:T(8,128)(2,1)S(1)}, u32[]{:S(2)}, u32[]{:S(2)}) collective-permute-start(bf16[98,1536]{1,0:T(8,128)(2,1)S(1)} %get-tuple-element.140), channel_id=1, source_target_pairs={{0,2},{1,3},{2,0},{3,1},{4,6},{5,7},{6,4},{7,5},{8,10},{9,11},{10,... | collective-permute-start | bytes 903176 | tf_op jit(solution)/shard_map/ppermute | solution.py:521
  150.7 16.6 %collective-permute-start.21 = (bf16[192,768]{1,0:T(8,128)(2,1)S(1)}, bf16[192,768]{1,0:T(8,128)(2,1)S(1)}, u32[]{:S(2)}, u32[]{:S(2)}) collective-permute-start(bf16[192,768]{1,0:T(8,128)(2,1)S(1)} %add.104), channel_id=1, source_target_pairs={{0,8},{1,9},{2,10},{3,11},{4,12},{5,13},{6,14},{7,15},{8,0},{9,1},... | collective-permute-start | bytes 884744 | tf_op jit(solution)/shard_map/ppermute | solution.py:521
  167.6 19.8 %collective-permute-start.22 = (bf16[98,1536]{1,0:T(8,128)(2,1)S(1)}, bf16[98,1536]{1,0:T(8,128)(2,1)S(1)}, u32[]{:S(2)}, u32[]{:S(2)}) collective-permute-start(bf16[98,1536]{1,0:T(8,128)(2,1)S(1)} %fusion.2), channel_id=1, source_target_pairs={{0,16},{1,17},{2,18},{3,19},{4,20},{5,21},{6,22},{7,23},{8,24},{9,... | collective-permute-start | bytes 903176 | tf_op jit(solution)/shard_map/ppermute | solution.py:521
  168.4 18.9 %collective-permute-start.23 = (bf16[2,192,768]{2,1,0:T(8,128)(2,1)S(1)}, bf16[2,192,768]{2,1,0:T(8,128)(2,1)S(1)}, u32[]{:S(2)}, u32[]{:S(2)}) collective-permute-start(bf16[2,192,768]{2,1,0:T(8,128)(2,1)S(1)} %pad_maximum_fusion.1), channel_id=1, source_target_pairs={{0,4},{1,5},{2,6},{3,7},{4,0},{5,1},{6,2},{7,3},{8,12},{9,13},{10,... | collective-permute-start | bytes 1769480 | tf_op jit(solution)/shard_map/ppermute | solution.py:521
  171.2 16.1 %collective-permute-start.25 = (bf16[80,1536]{1,0:T(8,128)(2,1)}, bf16[80,1536]{1,0:T(8,128)(2,1)S(1)}, u32[]{:S(2)}, u32[]{:S(2)}) collective-permute-start(bf16[80,1536]{1,0:T(8,128)(2,1)} %pad_maximum_fusion.9), channel_id=1, source_target_pairs={{0,4},{1,5},{2,6},{3,7},{4,0},{5,1},{6,2},{7,3},{8,12},{9,13},{10,... | collective-permute-start | bytes 737288 | tf_op jit(solution)/shard_map/ppermute | solution.py:521
  171.8 11.6 %collective-permute-start.24 = (bf16[48,1536]{1,0:T(8,128)(2,1)}, bf16[48,1536]{1,0:T(8,128)(2,1)S(1)}, u32[]{:S(2)}, u32[]{:S(2)}) collective-permute-start(bf16[48,1536]{1,0:T(8,128)(2,1)} %get-tuple-element.174), channel_id=1, source_target_pairs={{0,8},{1,9},{2,10},{3,11},{4,12},{5,13},{6,14},{7,15},{8,0},{9,1},... | collective-permute-start | bytes 442376 | tf_op jit(solution)/shard_map/ppermute | solution.py:521
  187.3 0.8 copy-start.2
  189.2 21.1 %collective-permute-start.28 = (bf16[98,1536]{1,0:T(8,128)(2,1)S(1)}, bf16[98,1536]{1,0:T(8,128)(2,1)S(1)}, u32[]{:S(2)}, u32[]{:S(2)}) collective-permute-start(bf16[98,1536]{1,0:T(8,128)(2,1)S(1)} %add.109), channel_id=1, source_target_pairs={{0,12},{1,13},{2,14},{3,15},{4,8},{5,9},{6,10},{7,11},{8,4},{9,5},... | collective-permute-start | bytes 903176 | tf_op jit(solution)/shard_map/ppermute | solution.py:521
  191.7 18.6 %collective-permute-start.27 = (bf16[98,1536]{1,0:T(8,128)(2,1)S(1)}, bf16[98,1536]{1,0:T(8,128)(2,1)S(1)}, u32[]{:S(2)}, u32[]{:S(2)}) collective-permute-start(bf16[98,1536]{1,0:T(8,128)(2,1)S(1)} %add.109), channel_id=1, source_target_pairs={{0,8},{1,9},{2,10},{3,11},{4,12},{5,13},{6,14},{7,15},{8,0},{9,1},... | collective-permute-start | bytes 903176 | tf_op jit(solution)/shard_map/ppermute | solution.py:521
  192.2 18.2 %collective-permute-start.26 = (bf16[98,1536]{1,0:T(8,128)(2,1)S(1)}, bf16[98,1536]{1,0:T(8,128)(2,1)}, u32[]{:S(2)}, u32[]{:S(2)}) collective-permute-start(bf16[98,1536]{1,0:T(8,128)(2,1)S(1)} %add.109), channel_id=1, source_target_pairs={{0,4},{1,5},{2,6},{3,7},{4,0},{5,1},{6,2},{7,3},{8,12},{9,13},{10,... | collective-permute-start | bytes 903176 | tf_op jit(solution)/shard_map/ppermute | solution.py:521
  193.0 6.1 %copy-start.3 = (bf16[16,1536]{1,0:T(8,128)(2,1)S(1)}, bf16[16,1536]{1,0:T(8,128)(2,1)}, u32[]{:S(2)}) copy-start(bf16[16,1536]{1,0:T(8,128)(2,1)} %get-tuple-element.97) | copy-start | bytes 147460
  193.0 6.1 %copy-start.4 = (bf16[1,16,1536]{2,1,0:T(8,128)(2,1)S(1)}, bf16[1,16,1536]{2,1,0:T(8,128)(2,1)}, u32[]{:S(2)}) copy-start(bf16[1,16,1536]{2,1,0:T(8,128)(2,1)} %get-tuple-element.159) | copy-start | bytes 147460
  193.0 6.1 %copy-start.5 = (bf16[1,16,1536]{2,1,0:T(8,128)(2,1)S(1)}, bf16[1,16,1536]{2,1,0:T(8,128)(2,1)}, u32[]{:S(2)}) copy-start(bf16[1,16,1536]{2,1,0:T(8,128)(2,1)} %get-tuple-element.177) | copy-start | bytes 147460
  193.0 6.1 %copy-start.6 = (bf16[1,16,1536]{2,1,0:T(8,128)(2,1)S(1)}, bf16[1,16,1536]{2,1,0:T(8,128)(2,1)}, u32[]{:S(2)}) copy-start(bf16[1,16,1536]{2,1,0:T(8,128)(2,1)} %get-tuple-element.178) | copy-start | bytes 147460
  195.3 14.9 %collective-permute-start.29 = (bf16[2,48,1536]{2,1,0:T(8,128)(2,1)S(1)}, bf16[2,48,1536]{2,1,0:T(8,128)(2,1)S(1)}, u32[]{:S(2)}, u32[]{:S(2)}) collective-permute-start(bf16[2,48,1536]{2,1,0:T(8,128)(2,1)S(1)} %pad_maximum_fusion.4), channel_id=1, source_target_pairs={{0,4},{1,5},{2,6},{3,7},{4,0},{5,1},{6,2},{7,3},{8,12},{9,13},{10,... | collective-permute-start | bytes 884744 | tf_op jit(solution)/shard_map/ppermute | solution.py:521
  196.8 13.5 %collective-permute-start.30 = (bf16[2,48,1536]{2,1,0:T(8,128)(2,1)S(1)}, bf16[2,48,1536]{2,1,0:T(8,128)(2,1)S(1)}, u32[]{:S(2)}, u32[]{:S(2)}) collective-permute-start(bf16[2,48,1536]{2,1,0:T(8,128)(2,1)S(1)} %pad_maximum_fusion.6), channel_id=1, source_target_pairs={{0,8},{1,9},{2,10},{3,11},{4,12},{5,13},{6,14},{7,15},{8,0},{9,1},... | collective-permute-start | bytes 884744 | tf_op jit(solution)/shard_map/ppermute | solution.py:521

commit v5 on v4

--- a/solution.py
+++ b/solution.py
@@ -631,7 +631,7 @@
     from_b, out_c, z_a = tie((from_b, out_c, z_a))
     plane_b, total_a = plane_sum(add_b, from_b), plane_a + z_a
     z_b = hop(jnp.concatenate([plane_b, blocks[2], blocks[3]], axis=0), 0, 0, 2)
-    r_a, add_c = hop(total_a, 0, 0, 1), over_core(*out_c, dps)[:, :, : tall + 2]
+    r_a, add_c = hop(total_a, 0, 0, 1), over_core(*out_c, dps)[:, :, : tall + 8]
     from_c = plane_parts(add_c, hop)
     from_c, z_b, r_a = tie((from_c, z_b, r_a))
     pieces = (z_b.shape[0] - tall) // 2
@@ -647,17 +647,17 @@
     rest = all_parts(plane_c + z_c, hop)
     y_top = hop(jnp.stack([top, r_top]), 0, 1, 0)
     r_bottom = hop(jnp.stack([bottom, y_bottom]), 0, 0, 1)
-    stacked = lambda a, b: jnp.concatenate([a, b], axis=0)
     con = total_a, y_a[0], r_a, y_a[1]
-    exp = total_b, stacked(y_top[0], y_bottom), stacked(r_top, r_bottom[0]), stacked(y_top[1], r_bottom[1])
     con, att_part = in_order(con, y, r), in_order([p[:tall] for p in rest], y, r)
     g_con = jnp.concatenate([con[0][0], con[0][1], con[1][0], con[1][1]], axis=0)
     wide = gproj.shape[1] // 2
     side = lambda a, b: jnp.concatenate(
         [jnp.concatenate([att_part[0][j][:, a:b], att_part[1][j][:, a:b]], axis=1) for j in (0, 1)], axis=0
     )
-    g_qkv, g_out, last_b = tie((side(0, wide), side(wide, cols), exp[0]))
-    exp = in_order((last_b,) + exp[1:], y, r)
+    g_qkv, g_out, y_top, r_bottom = tie((side(0, wide), side(wide, cols), y_top, r_bottom))
+    stacked = lambda a, b: jnp.concatenate([a, b], axis=0)
+    exp = total_b, stacked(y_top[0], y_bottom), stacked(r_top, r_bottom[0]), stacked(y_top[1], r_bottom[1])
+    exp = in_order(exp, y, r)
     g_exp = jnp.concatenate([jnp.concatenate([exp[0][j], exp[1][j]], axis=1) for j in (0, 1)], axis=0)
     g_con, vectors = tie((g_con, rest[0][tall:]))
     vectors = vectors.astype(F32)

time: 217 us -> 213 us (0.982)
  waiting for transfers between devices: 64.6 us -> 61.5 us
    ppermute x21, waiting for transfers between devices: 50 us -> 46.9 us  [move(): return lax.ppermute(array, AXES, pairs)]
  transfers between devices with their start and end apart: 31 -> 31, of which waited for: 14 -> 15; matrix products, arithmetic and copies ran while one was open for 5% -> 7% of each run, Pallas kernels for 7% -> 7%
where the time goes in v5:
time: 213 us
  Pallas kernels  94 us (44%)
  waiting for transfers between devices  61.5 us (29%)
  starting transfers between devices  33.9 us (16%)
  other arithmetic  15.8 us (7%)
  local copies, waits for them, and re-layouts  6.44 us (3%)
    ppermute x21, waiting for transfers between devices, move(): return lax.ppermute(array, AXES, pairs)  46.9 us
    pallas_call x1, Pallas kernels, backward_all(): pl.pallas_call(partial(backward_kernel, fused=fused), grid_spec=pltpu.Pre...  40.9 us
    pallas_call x1, Pallas kernels, forward_all(): pl.pallas_call(forward_kernel, grid_spec=pltpu.PrefetchScalarGridSpec(num...  38.2 us
    ppermute x21, starting transfers between devices, move(): return lax.ppermute(array, AXES, pairs)  21.8 us
    ppermute x7, starting transfers between devices, body(): lax.ppermute(block, 'section', by_label(k, sections))  12 us
    pallas_call x1, Pallas kernels, attention_grads(): pl.pallas_call(attention_kernel, grid_spec=pltpu.PrefetchScalarGridSpec(n...  8.23 us
    ppermute x3, waiting for transfers between devices, over_core(): return keep + lax.ppermute(give, 'dp', [(d, d ^ 1) for d in range(dps)])  7.63 us
    ppermute x7, waiting for transfers between devices, body(): lax.ppermute(block, 'section', by_label(k, sections))  6.98 us
  transfers between devices with their start and end apart: 31, of which 15 were waited for; matrix products, arithmetic and copies ran while one was open for 7% of the time, Pallas kernels for 7%

profile of v5, /device:TPU:0, one launch (start us, length us, event | category | flops | bytes accessed | tf_op | source)
XLA Modules:
  0.0 212.8 jit_solution(6301366963481361519)
XLA Ops:
  0.7 0.9 fusion.24
  1.6 3.1 %collective-permute-start = (bf16[16,1536]{1,0:T(8,128)(2,1)S(1)}, bf16[16,1536]{1,0:T(8,128)(2,1)S(1)}, u32[]{:S(2)}, u32[]{:S(2)}) collective-permute-start(bf16[16,1536]{1,0:T(8,128)(2,1)S(1)} %get-tuple-element.185), channel_id=1, source_target_pairs={{0,8},{4,12},{8,0},{12,4},{16,24},{20,28},{24,16},{28,20},{1,9},{5... | collective-permute-start | bytes 147464 | tf_op jit(solution)/shard_map/ppermute | solution.py:566
  4.7 0.8 fusion.38
  5.5 3.6 %collective-permute-start.5 = (bf16[16,1536]{1,0:T(8,128)(2,1)S(1)}, bf16[16,1536]{1,0:T(8,128)(2,1)S(1)}, u32[]{:S(2)}, u32[]{:S(2)}) collective-permute-start(bf16[16,1536]{1,0:T(8,128)(2,1)S(1)} %get-tuple-element.189), channel_id=1, source_target_pairs={{0,20},{4,16},{8,28},{12,24},{16,4},{20,0},{24,12},{28,8},{1,21},{... | collective-permute-start | bytes 147464 | tf_op jit(solution)/shard_map/ppermute | solution.py:566
  9.3 3.6 %collective-permute-start.6 = (bf16[16,1536]{1,0:T(8,128)(2,1)S(1)}, bf16[16,1536]{1,0:T(8,128)(2,1)S(1)}, u32[]{:S(2)}, u32[]{:S(2)}) collective-permute-start(bf16[16,1536]{1,0:T(8,128)(2,1)S(1)} %get-tuple-element.183), channel_id=1, source_target_pairs={{0,28},{4,24},{8,20},{12,16},{16,12},{20,8},{24,4},{28,0},{1,29},{... | collective-permute-start | bytes 147464 | tf_op jit(solution)/shard_map/ppermute | solution.py:566
  12.9 1.5 collective-permute-start.1
  15.0 2.0 collective-permute-done.1
  17.0 3.5 %collective-permute-done.2 = bf16[16,1536]{1,0:T(8,128)(2,1)S(1)} collective-permute-done((bf16[16,1536]{1,0:T(8,128)(2,1)S(1)}, bf16[16,1536]{1,0:T(8,128)(2,1)S(1)}, u32[]{:S(2)}, u32[]{:S(2)}) %collective-permute-start.2) | collective-permute-done | bytes 49184 | tf_op jit(solution)/shard_map/ppermute | solution.py:566
  20.5 1.5 collective-permute-done.3
  22.4 0.8 fusion.39
  23.1 38.2 %shard_map.254 = (bf16[8,128,768]{2,1,0:T(8,128)(2,1)}, bf16[8,128,768]{2,1,0:T(8,128)(2,1)}, bf16[8,128,2304]{2,1,0:T(8,128)(2,1)}, bf16[8,1536,128]{2,1,0:T(8,...) custom-call(s32[4,4]{1,0:T(4,128)} %bitcast.162, ...), custom_call_target="tpu_custom_call" | custom-call | tf_op jit(solution)/shard_map/pallas_call | solution.py:320
  61.4 40.9 %shard_map.255 = (bf16[8,128,2304]{2,1,0:T(8,128)(2,1)}, bf16[8,128,768]{2,1,0:T(8,128)(2,1)}, bf16[8,128,3072]{2,1,0:T(8,128)(2,1)}, bf16[128,768]{1,0:T(8,128)...) custom-call(s32[5]{0:T(128)} %stack.90.spot_ref, ...), custom_call_target="tpu_custom_call" | custom-call | tf_op jit(solution)/shard_map/pallas_call | solution.py:364
  102.5 1.0 pad_maximum_fusion.2
  103.4 2.0 collective-permute-done.7
  105.4 1.5 add.91
  107.0 2.6 %collective-permute-start.10 = (bf16[192,768]{1,0:T(8,128)(2,1)S(1)}, bf16[192,768]{1,0:T(8,128)(2,1)S(1)}, u32[]{:S(2)}, u32[]{:S(2)}) collective-permute-start(bf16[192,768]{1,0:T(8,128)(2,1)S(1)} %get-tuple-element.158), channel_id=1, source_target_pairs={{0,6},{1,7},{2,4},{3,5},{4,2},{5,3},{6,0},{7,1},{8,14},{9,15},{10,... | collective-permute-start | bytes 884744 | tf_op jit(solution)/shard_map/ppermute | solution.py:521
  110.6 0.6 dynamic-slice_bitcast_fusion
  111.2 6.7 %shard_map.256 = (bf16[2,2,96,1536]{3,2,1,0:T(8,128)(2,1)}, bf16[2,2,96,1536]{3,2,1,0:T(8,128)(2,1)}) custom-call(s32[5]{0:T(128)} %stack.90.spot_ref, bf16[1024,768]{1,0:T(8,128)(2,1)} %bitcast.170, bf16[1024,3072]{1,0:T(8,128)(2,1)} %bitcast.169), custom_call_target="tpu_custom_call" | custom-call | flops 2415919104 | bytes 7077888 | tf_op jit(solution)/shard_map/pallas_call | solution.py:417
  117.9 5.5 %collective-permute-done.9 = bf16[192,768]{1,0:T(8,128)(2,1)S(1)} collective-permute-done((bf16[192,768]{1,0:T(8,128)(2,1)S(1)}, bf16[192,768]{1,0:T(8,128)(2,1)S(1)}, u32[]{:S(2)}, u32[]{:S(2)}) %collective-permute-start.9) | collective-permute-done | bytes 294944 | tf_op jit(solution)/shard_map/ppermute | solution.py:521
  123.8 2.7 %collective-permute-done.11 = bf16[2,2,96,1536]{3,2,1,0:T(8,128)(2,1)S(1)} collective-permute-done((bf16[2,2,96,1536]{3,2,1,0:T(8,128)(2,1)}, bf16[2,2,96,1536]{3,2,1,0:T(8,128)(2,1)S(1)}, u32[]{:S(2)}, u32[]{:S(2)}) %collective-permute-start.11) | collective-permute-done | bytes 1179680 | tf_op jit(solution)/shard_map/ppermute | solution.py:525
  127.0 1.7 collective-permute-start.14
  128.6 1.4 collective-permute-start.13
  130.5 8.2 %shard_map.257 = (bf16[2,2,112,1536]{3,2,1,0:T(8,128)(2,1)}, bf16[2,2,112,1536]{3,2,1,0:T(8,128)(2,1)}) custom-call(s32[5]{0:T(128)} %stack.90.spot_ref, bf16[1024,768]{1,0:T(8,128)(2,1)} %bitcast.144, bf16[1024,2304]{1,0:T(8,128)(2,1)} %bitcast.142, bf16[1024,768]{1,0:T(8,128)(2,1)} %bitcast.145, bf16[1024,768]{1,0:T(8,128)(2,1)} %bitcast.146, ...), custom_call_target="tpu_custom_call" | custom-call | flops 2415919104 | bytes 7077888 | tf_op jit(solution)/shard_map/pallas_call | solution.py:479
  138.8 1.1 collective-permute-done.15
  139.8 3.5 %collective-permute-done.13 = bf16[96,1536]{1,0:T(8,128)(2,1)S(1)} collective-permute-done((bf16[96,1536]{1,0:T(8,128)(2,1)S(1)}, bf16[96,1536]{1,0:T(8,128)(2,1)S(1)}, u32[]{:S(2)}, u32[]{:S(2)}) %collective-permute-start.13) | collective-permute-done | bytes 294944 | tf_op jit(solution)/shard_map/ppermute | solution.py:521
  143.8 2.9 %collective-permute-done.16 = bf16[2,2,112,1536]{3,2,1,0:T(8,128)(2,1)S(1)} collective-permute-done((bf16[2,2,112,1536]{3,2,1,0:T(8,128)(2,1)}, bf16[2,2,112,1536]{3,2,1,0:T(8,128)(2,1)S(1)}, u32[]{:S(2)}, u32[]{:S(2)}) %collective-permute-start.16) | collective-permute-done | bytes 1376288 | tf_op jit(solution)/shard_map/ppermute | solution.py:525
  147.1 1.7 collective-permute-start.19
  148.7 1.4 collective-permute-start.18
  150.8 16.5 %collective-permute-done.21 = bf16[192,768]{1,0:T(8,128)(2,1)S(1)} collective-permute-done((bf16[192,768]{1,0:T(8,128)(2,1)S(1)}, bf16[192,768]{1,0:T(8,128)(2,1)S(1)}, u32[]{:S(2)}, u32[]{:S(2)}) %collective-permute-start.21) | collective-permute-done | bytes 294944 | tf_op jit(solution)/shard_map/ppermute | solution.py:521
  167.6 0.7 slice_bitcast_fusion.19
  168.4 1.5 collective-permute-start.23
  169.9 0.6 slice_bitcast_fusion.17
  170.5 0.7 pad_maximum_fusion.9
  171.8 1.9 collective-permute-start.24
  173.7 9.8 %collective-permute-done.24 = bf16[48,1536]{1,0:T(8,128)(2,1)S(1)} collective-permute-done((bf16[48,1536]{1,0:T(8,128)(2,1)}, bf16[48,1536]{1,0:T(8,128)(2,1)S(1)}, u32[]{:S(2)}, u32[]{:S(2)}) %collective-permute-start.24) | collective-permute-done | bytes 147488 | tf_op jit(solution)/shard_map/ppermute | solution.py:521
  183.5 3.9 %collective-permute-done.25 = bf16[80,1536]{1,0:T(8,128)(2,1)S(1)} collective-permute-done((bf16[80,1536]{1,0:T(8,128)(2,1)}, bf16[80,1536]{1,0:T(8,128)(2,1)S(1)}, u32[]{:S(2)}, u32[]{:S(2)}) %collective-permute-start.25) | collective-permute-done | bytes 245792 | tf_op jit(solution)/shard_map/ppermute | solution.py:521
  187.4 0.7 slice_bitcast_fusion.18
  188.1 1.1 add.109
  189.2 2.5 %collective-permute-start.28 = (bf16[104,1536]{1,0:T(8,128)(2,1)S(1)}, bf16[104,1536]{1,0:T(8,128)(2,1)S(1)}, u32[]{:S(2)}, u32[]{:S(2)}) collective-permute-start(bf16[104,1536]{1,0:T(8,128)(2,1)S(1)} %add.109), channel_id=1, source_target_pairs={{0,12},{1,13},{2,14},{3,15},{4,8},{5,9},{6,10},{7,11},{8,4},{9,5},... | collective-permute-start | bytes 958472 | tf_op jit(solution)/shard_map/ppermute | solution.py:521
  193.0 1.6 pad_maximum_fusion
  195.3 1.5 collective-permute-start.29
  196.8 1.6 collective-permute-start.30
  199.9 0.7 fusion.22
  200.6 6.4 %collective-permute-done.27 = bf16[104,1536]{1,0:T(8,128)(2,1)S(1)} collective-permute-done((bf16[104,1536]{1,0:T(8,128)(2,1)S(1)}, bf16[104,1536]{1,0:T(8,128)(2,1)S(1)}, u32[]{:S(2)}, u32[]{:S(2)}) %collective-permute-start.27) | collective-permute-done | bytes 319520 | tf_op jit(solution)/shard_map/ppermute | solution.py:521
  207.1 1.3 fusion.10
  208.6 0.9 maximum_maximum_fusion.2
  209.5 1.3 maximum_maximum_fusion.1
  211.3 1.6 maximum_maximum_fusion
  (101 shorter events, 10.3 us)
Async XLA Ops:
  1.6 13.4 %collective-permute-start = (bf16[16,1536]{1,0:T(8,128)(2,1)S(1)}, bf16[16,1536]{1,0:T(8,128)(2,1)S(1)}, u32[]{:S(2)}, u32[]{:S(2)}) collective-permute-start(bf16[16,1536]{1,0:T(8,128)(2,1)S(1)} %get-tuple-element.185), channel_id=1, source_target_pairs={{0,8},{4,12},{8,0},{12,4},{16,24},{20,28},{24,16},{28,20},{1,9},{5... | collective-permute-start | bytes 147464 | tf_op jit(solution)/shard_map/ppermute | solution.py:566
  5.5 16.5 %collective-permute-start.5 = (bf16[16,1536]{1,0:T(8,128)(2,1)S(1)}, bf16[16,1536]{1,0:T(8,128)(2,1)S(1)}, u32[]{:S(2)}, u32[]{:S(2)}) collective-permute-start(bf16[16,1536]{1,0:T(8,128)(2,1)S(1)} %get-tuple-element.189), channel_id=1, source_target_pairs={{0,20},{4,16},{8,28},{12,24},{16,4},{20,0},{24,12},{28,8},{1,21},{... | collective-permute-start | bytes 147464 | tf_op jit(solution)/shard_map/ppermute | solution.py:566
  9.1 12.9 %collective-permute-start.4 = (bf16[16,1536]{1,0:T(8,128)(2,1)S(1)}, bf16[16,1536]{1,0:T(8,128)(2,1)S(1)}, u32[]{:S(2)}, u32[]{:S(2)}) collective-permute-start(bf16[16,1536]{1,0:T(8,128)(2,1)S(1)} %get-tuple-element.190), channel_id=1, source_target_pairs={{0,24},{4,28},{8,16},{12,20},{16,8},{20,12},{24,0},{28,4},{1,25},{... | collective-permute-start | bytes 147464 | tf_op jit(solution)/shard_map/ppermute | solution.py:566
  9.3 12.7 %collective-permute-start.6 = (bf16[16,1536]{1,0:T(8,128)(2,1)S(1)}, bf16[16,1536]{1,0:T(8,128)(2,1)S(1)}, u32[]{:S(2)}, u32[]{:S(2)}) collective-permute-start(bf16[16,1536]{1,0:T(8,128)(2,1)S(1)} %get-tuple-element.183), channel_id=1, source_target_pairs={{0,28},{4,24},{8,20},{12,16},{16,12},{20,8},{24,4},{28,0},{1,29},{... | collective-permute-start | bytes 147464 | tf_op jit(solution)/shard_map/ppermute | solution.py:566
  12.9 4.1 %collective-permute-start.1 = (bf16[16,1536]{1,0:T(8,128)(2,1)S(1)}, bf16[16,1536]{1,0:T(8,128)(2,1)S(1)}, u32[]{:S(2)}, u32[]{:S(2)}) collective-permute-start(bf16[16,1536]{1,0:T(8,128)(2,1)S(1)} %get-tuple-element.186), channel_id=1, source_target_pairs={{0,4},{4,0},{8,12},{12,8},{16,20},{20,16},{24,28},{28,24},{1,5},{5... | collective-permute-start | bytes 147464 | tf_op jit(solution)/shard_map/ppermute | solution.py:566
  15.0 5.5 %collective-permute-start.2 = (bf16[16,1536]{1,0:T(8,128)(2,1)S(1)}, bf16[16,1536]{1,0:T(8,128)(2,1)S(1)}, u32[]{:S(2)}, u32[]{:S(2)}) collective-permute-start(bf16[16,1536]{1,0:T(8,128)(2,1)S(1)} %get-tuple-element.187), channel_id=1, source_target_pairs={{0,12},{4,8},{8,4},{12,0},{16,28},{20,24},{24,20},{28,16},{1,13},{... | collective-permute-start | bytes 147464 | tf_op jit(solution)/shard_map/ppermute | solution.py:566
  17.0 5.0 %collective-permute-start.3 = (bf16[16,1536]{1,0:T(8,128)(2,1)S(1)}, bf16[16,1536]{1,0:T(8,128)(2,1)S(1)}, u32[]{:S(2)}, u32[]{:S(2)}) collective-permute-start(bf16[16,1536]{1,0:T(8,128)(2,1)S(1)} %get-tuple-element.188), channel_id=1, source_target_pairs={{0,16},{4,20},{8,24},{12,28},{16,0},{20,4},{24,8},{28,12},{1,17},{... | collective-permute-start | bytes 147464 | tf_op jit(solution)/shard_map/ppermute | solution.py:566
  61.4 41.1 %copy-start.7 = (bf16[128,768]{1,0:T(8,128)(2,1)S(1)}, bf16[128,768]{1,0:T(8,128)(2,1)}, u32[]{:S(2)}) copy-start(bf16[128,768]{1,0:T(8,128)(2,1)} %get-tuple-element.96) | copy-start | bytes 589828
  102.3 3.1 %collective-permute-start.7 = (bf16[2,2,192,768]{3,2,1,0:T(8,128)(2,1)}, bf16[2,2,192,768]{3,2,1,0:T(8,128)(2,1)S(1)}, u32[]{:S(2)}, u32[]{:S(2)}) collective-permute-start(bf16[2,2,192,768]{3,2,1,0:T(8,128)(2,1)} %get-tuple-element.90), channel_id=1, source_target_pairs={{0,1},{1,0},{2,3},{3,2},{4,5},{5,4},{6,7},{7,6},{8,9},{9,8},{10,11... | collective-permute-start | bytes 3538952 | tf_op jit(solution)/shard_map/ppermute | solution.py:525
  107.0 10.9 %collective-permute-start.10 = (bf16[192,768]{1,0:T(8,128)(2,1)S(1)}, bf16[192,768]{1,0:T(8,128)(2,1)S(1)}, u32[]{:S(2)}, u32[]{:S(2)}) collective-permute-start(bf16[192,768]{1,0:T(8,128)(2,1)S(1)} %get-tuple-element.158), channel_id=1, source_target_pairs={{0,6},{1,7},{2,4},{3,5},{4,2},{5,3},{6,0},{7,1},{8,14},{9,15},{10,... | collective-permute-start | bytes 884744 | tf_op jit(solution)/shard_map/ppermute | solution.py:521
  109.6 13.8 %collective-permute-start.9 = (bf16[192,768]{1,0:T(8,128)(2,1)S(1)}, bf16[192,768]{1,0:T(8,128)(2,1)S(1)}, u32[]{:S(2)}, u32[]{:S(2)}) collective-permute-start(bf16[192,768]{1,0:T(8,128)(2,1)S(1)} %get-tuple-element.159), channel_id=1, source_target_pairs={{0,4},{1,5},{2,6},{3,7},{4,0},{5,1},{6,2},{7,3},{8,12},{9,13},{10,... | collective-permute-start | bytes 884744 | tf_op jit(solution)/shard_map/ppermute | solution.py:521
  110.1 13.4 %collective-permute-start.8 = (bf16[192,768]{1,0:T(8,128)(2,1)S(1)}, bf16[192,768]{1,0:T(8,128)(2,1)S(1)}, u32[]{:S(2)}, u32[]{:S(2)}) collective-permute-start(bf16[192,768]{1,0:T(8,128)(2,1)S(1)} %get-tuple-element.160), channel_id=1, source_target_pairs={{0,2},{1,3},{2,0},{3,1},{4,6},{5,7},{6,4},{7,5},{8,10},{9,11},{10,... | collective-permute-start | bytes 884744 | tf_op jit(solution)/shard_map/ppermute | solution.py:521
  117.9 8.7 %copy-start.1 = (bf16[2,2,96,1536]{3,2,1,0:T(8,128)(2,1)S(1)}, bf16[2,2,96,1536]{3,2,1,0:T(8,128)(2,1)}, u32[]{:S(2)}) copy-start(bf16[2,2,96,1536]{3,2,1,0:T(8,128)(2,1)} %get-tuple-element.103) | copy-start | bytes 3538948
  123.5 3.1 %collective-permute-start.11 = (bf16[2,2,96,1536]{3,2,1,0:T(8,128)(2,1)}, bf16[2,2,96,1536]{3,2,1,0:T(8,128)(2,1)S(1)}, u32[]{:S(2)}, u32[]{:S(2)}) collective-permute-start(bf16[2,2,96,1536]{3,2,1,0:T(8,128)(2,1)} %get-tuple-element.104), channel_id=1, source_target_pairs={{0,1},{1,0},{2,3},{3,2},{4,5},{5,4},{6,7},{7,6},{8,9},{9,8},{10,11... | collective-permute-start | bytes 3538952 | tf_op jit(solution)/shard_map/ppermute | solution.py:525
  123.7 16.1 %collective-permute-start.15 = (bf16[192,768]{1,0:T(8,128)(2,1)S(1)}, bf16[192,768]{1,0:T(8,128)(2,1)S(1)}, u32[]{:S(2)}, u32[]{:S(2)}) collective-permute-start(bf16[192,768]{1,0:T(8,128)(2,1)S(1)} %fusion.8), channel_id=1, source_target_pairs={{0,16},{1,17},{2,18},{3,19},{4,20},{5,21},{6,22},{7,23},{8,24},{9,... | collective-permute-start | bytes 884744 | tf_op jit(solution)/shard_map/ppermute | solution.py:521
  127.0 12.8 %collective-permute-start.14 = (bf16[96,1536]{1,0:T(8,128)(2,1)S(1)}, bf16[96,1536]{1,0:T(8,128)(2,1)S(1)}, u32[]{:S(2)}, u32[]{:S(2)}) collective-permute-start(bf16[96,1536]{1,0:T(8,128)(2,1)S(1)} %get-tuple-element.155), channel_id=1, source_target_pairs={{0,6},{1,7},{2,4},{3,5},{4,2},{5,3},{6,0},{7,1},{8,14},{9,15},{10,... | collective-permute-start | bytes 884744 | tf_op jit(solution)/shard_map/ppermute | solution.py:521
  128.6 14.7 %collective-permute-start.13 = (bf16[96,1536]{1,0:T(8,128)(2,1)S(1)}, bf16[96,1536]{1,0:T(8,128)(2,1)S(1)}, u32[]{:S(2)}, u32[]{:S(2)}) collective-permute-start(bf16[96,1536]{1,0:T(8,128)(2,1)S(1)} %get-tuple-element.156), channel_id=1, source_target_pairs={{0,4},{1,5},{2,6},{3,7},{4,0},{5,1},{6,2},{7,3},{8,12},{9,13},{10,... | collective-permute-start | bytes 884744 | tf_op jit(solution)/shard_map/ppermute | solution.py:521
  130.0 13.3 %collective-permute-start.12 = (bf16[96,1536]{1,0:T(8,128)(2,1)S(1)}, bf16[96,1536]{1,0:T(8,128)(2,1)S(1)}, u32[]{:S(2)}, u32[]{:S(2)}) collective-permute-start(bf16[96,1536]{1,0:T(8,128)(2,1)S(1)} %get-tuple-element.157), channel_id=1, source_target_pairs={{0,2},{1,3},{2,0},{3,1},{4,6},{5,7},{6,4},{7,5},{8,10},{9,11},{10,... | collective-permute-start | bytes 884744 | tf_op jit(solution)/shard_map/ppermute | solution.py:521
  138.7 7.9 %copy-start = (bf16[2,2,112,1536]{3,2,1,0:T(8,128)(2,1)S(1)}, bf16[2,2,112,1536]{3,2,1,0:T(8,128)(2,1)}, u32[]{:S(2)}) copy-start(bf16[2,2,112,1536]{3,2,1,0:T(8,128)(2,1)} %get-tuple-element.116) | copy-start | bytes 4128772
  143.3 3.3 %collective-permute-start.16 = (bf16[2,2,112,1536]{3,2,1,0:T(8,128)(2,1)}, bf16[2,2,112,1536]{3,2,1,0:T(8,128)(2,1)S(1)}, u32[]{:S(2)}, u32[]{:S(2)}) collective-permute-start(bf16[2,2,112,1536]{3,2,1,0:T(8,128)(2,1)} %get-tuple-element.117), channel_id=1, source_target_pairs={{0,1},{1,0},{2,3},{3,2},{4,5},{5,4},{6,7},{7,6},{8,9},{9,8},{10,11... | collective-permute-start | bytes 4128776 | tf_op jit(solution)/shard_map/ppermute | solution.py:525
  143.5 23.8 %collective-permute-start.20 = (bf16[128,1536]{1,0:T(8,128)(2,1)S(1)}, bf16[128,1536]{1,0:T(8,128)(2,1)S(1)}, u32[]{:S(2)}, u32[]{:S(2)}) collective-permute-start(bf16[128,1536]{1,0:T(8,128)(2,1)S(1)} %pad_maximum_fusion.3), channel_id=1, source_target_pairs={{0,16},{1,17},{2,18},{3,19},{4,20},{5,21},{6,22},{7,23},{8,24},{9,... | collective-permute-start | bytes 1179656 | tf_op jit(solution)/shard_map/ppermute | solution.py:521
  147.1 20.2 %collective-permute-start.19 = (bf16[104,1536]{1,0:T(8,128)(2,1)S(1)}, bf16[104,1536]{1,0:T(8,128)(2,1)S(1)}, u32[]{:S(2)}, u32[]{:S(2)}) collective-permute-start(bf16[104,1536]{1,0:T(8,128)(2,1)S(1)} %get-tuple-element.140), channel_id=1, source_target_pairs={{0,6},{1,7},{2,4},{3,5},{4,2},{5,3},{6,0},{7,1},{8,14},{9,15},{10,... | collective-permute-start | bytes 958472 | tf_op jit(solution)/shard_map/ppermute | solution.py:521
  148.7 18.6 %collective-permute-start.18 = (bf16[104,1536]{1,0:T(8,128)(2,1)S(1)}, bf16[104,1536]{1,0:T(8,128)(2,1)S(1)}, u32[]{:S(2)}, u32[]{:S(2)}) collective-permute-start(bf16[104,1536]{1,0:T(8,128)(2,1)S(1)} %get-tuple-element.141), channel_id=1, source_target_pairs={{0,4},{1,5},{2,6},{3,7},{4,0},{5,1},{6,2},{7,3},{8,12},{9,13},{10,... | collective-permute-start | bytes 958472 | tf_op jit(solution)/shard_map/ppermute | solution.py:521
  150.1 17.2 %collective-permute-start.17 = (bf16[104,1536]{1,0:T(8,128)(2,1)S(1)}, bf16[104,1536]{1,0:T(8,128)(2,1)S(1)}, u32[]{:S(2)}, u32[]{:S(2)}) collective-permute-start(bf16[104,1536]{1,0:T(8,128)(2,1)S(1)} %get-tuple-element.142), channel_id=1, source_target_pairs={{0,2},{1,3},{2,0},{3,1},{4,6},{5,7},{6,4},{7,5},{8,10},{9,11},{10,... | collective-permute-start | bytes 958472 | tf_op jit(solution)/shard_map/ppermute | solution.py:521
  150.7 16.6 %collective-permute-start.21 = (bf16[192,768]{1,0:T(8,128)(2,1)S(1)}, bf16[192,768]{1,0:T(8,128)(2,1)S(1)}, u32[]{:S(2)}, u32[]{:S(2)}) collective-permute-start(bf16[192,768]{1,0:T(8,128)(2,1)S(1)} %add.104), channel_id=1, source_target_pairs={{0,8},{1,9},{2,10},{3,11},{4,12},{5,13},{6,14},{7,15},{8,0},{9,1},... | collective-permute-start | bytes 884744 | tf_op jit(solution)/shard_map/ppermute | solution.py:521
  167.6 19.8 %collective-permute-start.22 = (bf16[104,1536]{1,0:T(8,128)(2,1)S(1)}, bf16[104,1536]{1,0:T(8,128)(2,1)S(1)}, u32[]{:S(2)}, u32[]{:S(2)}) collective-permute-start(bf16[104,1536]{1,0:T(8,128)(2,1)S(1)} %fusion.2), channel_id=1, source_target_pairs={{0,16},{1,17},{2,18},{3,19},{4,20},{5,21},{6,22},{7,23},{8,24},{9,... | collective-permute-start | bytes 958472 | tf_op jit(solution)/shard_map/ppermute | solution.py:521
  168.4 18.9 %collective-permute-start.23 = (bf16[2,192,768]{2,1,0:T(8,128)(2,1)S(1)}, bf16[2,192,768]{2,1,0:T(8,128)(2,1)S(1)}, u32[]{:S(2)}, u32[]{:S(2)}) collective-permute-start(bf16[2,192,768]{2,1,0:T(8,128)(2,1)S(1)} %pad_maximum_fusion.1), channel_id=1, source_target_pairs={{0,4},{1,5},{2,6},{3,7},{4,0},{5,1},{6,2},{7,3},{8,12},{9,13},{10,... | collective-permute-start | bytes 1769480 | tf_op jit(solution)/shard_map/ppermute | solution.py:521
  171.2 16.1 %collective-permute-start.25 = (bf16[80,1536]{1,0:T(8,128)(2,1)}, bf16[80,1536]{1,0:T(8,128)(2,1)S(1)}, u32[]{:S(2)}, u32[]{:S(2)}) collective-permute-start(bf16[80,1536]{1,0:T(8,128)(2,1)} %pad_maximum_fusion.9), channel_id=1, source_target_pairs={{0,4},{1,5},{2,6},{3,7},{4,0},{5,1},{6,2},{7,3},{8,12},{9,13},{10,... | collective-permute-start | bytes 737288 | tf_op jit(solution)/shard_map/ppermute | solution.py:521
  171.8 11.6 %collective-permute-start.24 = (bf16[48,1536]{1,0:T(8,128)(2,1)}, bf16[48,1536]{1,0:T(8,128)(2,1)S(1)}, u32[]{:S(2)}, u32[]{:S(2)}) collective-permute-start(bf16[48,1536]{1,0:T(8,128)(2,1)} %get-tuple-element.176), channel_id=1, source_target_pairs={{0,8},{1,9},{2,10},{3,11},{4,12},{5,13},{6,14},{7,15},{8,0},{9,1},... | collective-permute-start | bytes 442376 | tf_op jit(solution)/shard_map/ppermute | solution.py:521
  187.3 0.8 copy-start.2
  189.2 11.4 %collective-permute-start.28 = (bf16[104,1536]{1,0:T(8,128)(2,1)S(1)}, bf16[104,1536]{1,0:T(8,128)(2,1)S(1)}, u32[]{:S(2)}, u32[]{:S(2)}) collective-permute-start(bf16[104,1536]{1,0:T(8,128)(2,1)S(1)} %add.109), channel_id=1, source_target_pairs={{0,12},{1,13},{2,14},{3,15},{4,8},{5,9},{6,10},{7,11},{8,4},{9,5},... | collective-permute-start | bytes 958472 | tf_op jit(solution)/shard_map/ppermute | solution.py:521
  191.7 15.4 %collective-permute-start.27 = (bf16[104,1536]{1,0:T(8,128)(2,1)S(1)}, bf16[104,1536]{1,0:T(8,128)(2,1)S(1)}, u32[]{:S(2)}, u32[]{:S(2)}) collective-permute-start(bf16[104,1536]{1,0:T(8,128)(2,1)S(1)} %add.109), channel_id=1, source_target_pairs={{0,8},{1,9},{2,10},{3,11},{4,12},{5,13},{6,14},{7,15},{8,0},{9,1},... | collective-permute-start | bytes 958472 | tf_op jit(solution)/shard_map/ppermute | solution.py:521
  192.2 14.9 %collective-permute-start.26 = (bf16[104,1536]{1,0:T(8,128)(2,1)S(1)}, bf16[104,1536]{1,0:T(8,128)(2,1)}, u32[]{:S(2)}, u32[]{:S(2)}) collective-permute-start(bf16[104,1536]{1,0:T(8,128)(2,1)S(1)} %add.109), channel_id=1, source_target_pairs={{0,4},{1,5},{2,6},{3,7},{4,0},{5,1},{6,2},{7,3},{8,12},{9,13},{10,... | collective-permute-start | bytes 958472 | tf_op jit(solution)/shard_map/ppermute | solution.py:521
  193.0 6.1 %copy-start.3 = (bf16[16,1536]{1,0:T(8,128)(2,1)S(1)}, bf16[16,1536]{1,0:T(8,128)(2,1)}, u32[]{:S(2)}) copy-start(bf16[16,1536]{1,0:T(8,128)(2,1)} %get-tuple-element.98) | copy-start | bytes 147460
  193.0 6.1 %copy-start.4 = (bf16[1,16,1536]{2,1,0:T(8,128)(2,1)S(1)}, bf16[1,16,1536]{2,1,0:T(8,128)(2,1)}, u32[]{:S(2)}) copy-start(bf16[1,16,1536]{2,1,0:T(8,128)(2,1)} %get-tuple-element.161) | copy-start | bytes 147460
  193.0 6.1 %copy-start.5 = (bf16[1,16,1536]{2,1,0:T(8,128)(2,1)S(1)}, bf16[1,16,1536]{2,1,0:T(8,128)(2,1)}, u32[]{:S(2)}) copy-start(bf16[1,16,1536]{2,1,0:T(8,128)(2,1)} %get-tuple-element.179) | copy-start | bytes 147460
  193.0 6.1 %copy-start.6 = (bf16[1,16,1536]{2,1,0:T(8,128)(2,1)S(1)}, bf16[1,16,1536]{2,1,0:T(8,128)(2,1)}, u32[]{:S(2)}) copy-start(bf16[1,16,1536]{2,1,0:T(8,128)(2,1)} %get-tuple-element.180) | copy-start | bytes 147460
  195.3 15.5 %collective-permute-start.29 = (bf16[2,48,1536]{2,1,0:T(8,128)(2,1)S(1)}, bf16[2,48,1536]{2,1,0:T(8,128)(2,1)S(1)}, u32[]{:S(2)}, u32[]{:S(2)}) collective-permute-start(bf16[2,48,1536]{2,1,0:T(8,128)(2,1)S(1)} %pad_maximum_fusion.4), channel_id=1, source_target_pairs={{0,4},{1,5},{2,6},{3,7},{4,0},{5,1},{6,2},{7,3},{8,12},{9,13},{10,... | collective-permute-start | bytes 884744 | tf_op jit(solution)/shard_map/ppermute | solution.py:521
  196.8 14.0 %collective-permute-start.30 = (bf16[2,48,1536]{2,1,0:T(8,128)(2,1)S(1)}, bf16[2,48,1536]{2,1,0:T(8,128)(2,1)S(1)}, u32[]{:S(2)}, u32[]{:S(2)}) collective-permute-start(bf16[2,48,1536]{2,1,0:T(8,128)(2,1)S(1)} %pad_maximum_fusion.5), channel_id=1, source_target_pairs={{0,8},{1,9},{2,10},{3,11},{4,12},{5,13},{6,14},{7,15},{8,0},{9,1},... | collective-permute-start | bytes 884744 | tf_op jit(solution)/shard_map/ppermute | solution.py:521

commit v6 on v5

--- a/solution.py
+++ b/solution.py
@@ -560,12 +560,10 @@
     label = label_of(section)
 
     sent = jnp.concatenate([tokens[:, 0], cotangent[:, 0]], axis=-1)
-    got = []
-    for k in range(sections):
-        block = lax.dynamic_index_in_dim(sent, (label ^ k) >> 1, 0, keepdims=False)
-        got.append(block if k == 0 else lax.ppermute(block, "section", by_label(k, sections)))
-    shard = xor_order(jnp.stack(got), label)
-    shard = shard.reshape(sections // 4, 2, 2, piece_rows, 2 * width).swapaxes(1, 2).reshape(rows, 2 * width)
+    outgoing = sent.reshape(sections // 4, 1, 2, piece_rows, 2 * width)
+    outgoing = jnp.broadcast_to(outgoing, (sections // 4, 2, 2, piece_rows, 2 * width))
+    outgoing = outgoing.reshape(sections, piece_rows, 2 * width)
+    shard = lax.all_to_all(outgoing, "section", 0, 0, tiled=True).reshape(rows, 2 * width)
     x, cot = shard[:, :width], shard[:, width:]
     spot = jnp.stack([(dp >> 1) & 1, dp & 1, section & 1, (section >> 1) & 1, label >> 1]).astype(jnp.int32)
     first, n1, proj, probs, att, n2, second, slope, act, inv, wqot, wet, wct, last = forward_all(

time: 213 us -> 212 us (level)
  starting transfers between devices: 33.9 us -> 28 us
  waiting for transfers between devices: 61.5 us -> 67.3 us
    ppermute x7 -> x0, starting transfers between devices: 12 us -> none  [body(): lax.ppermute(block, 'section', by_label(k, sections))]
    all_to_all x0 -> x1, waiting for transfers between devices: none -> 11.1 us  [body(): lax.all_to_all(outgoing, 'section', 0, 0, tiled=True)]
    all_to_all x0 -> x1, starting transfers between devices: none -> 7.28 us  [body(): lax.all_to_all(outgoing, 'section', 0, 0, tiled=True)]
    ppermute x7 -> x0, waiting for transfers between devices: 6.98 us -> none  [body(): lax.ppermute(block, 'section', by_label(k, sections))]
    ppermute x21, waiting for transfers between devices: 46.9 us -> 49.2 us  [move(): return lax.ppermute(array, AXES, pairs)]
  transfers between devices with their start and end apart: 31 -> 25, of which waited for: 15 -> 12; matrix products, arithmetic and copies ran while one was open for 7% -> 6% of each run, Pallas kernels for 7% -> 7%
where the time goes in v6:
time: 212 us; the launch traced here: 211 us
  Pallas kernels  94 us (44%)
  waiting for transfers between devices  67.3 us (32%)
  starting transfers between devices  28 us (13%)
  other arithmetic  13.9 us (7%)
  local copies, waits for them, and re-layouts  7.09 us (3%)
    ppermute x21, waiting for transfers between devices, move(): return lax.ppermute(array, AXES, pairs)  49.2 us
    pallas_call x1, Pallas kernels, backward_all(): pl.pallas_call(partial(backward_kernel, fused=fused), grid_spec=pltpu.Pre...  40.9 us
    pallas_call x1, Pallas kernels, forward_all(): pl.pallas_call(forward_kernel, grid_spec=pltpu.PrefetchScalarGridSpec(num...  38.3 us
    ppermute x21, starting transfers between devices, move(): return lax.ppermute(array, AXES, pairs)  20.6 us
    all_to_all x1, waiting for transfers between devices, body(): lax.all_to_all(outgoing, 'section', 0, 0, tiled=True)  11.1 us
    pallas_call x1, Pallas kernels, attention_grads(): pl.pallas_call(attention_kernel, grid_spec=pltpu.PrefetchScalarGridSpec(n...  8.2 us
    all_to_all x1, starting transfers between devices, body(): lax.all_to_all(outgoing, 'section', 0, 0, tiled=True)  7.28 us
    ppermute x3, waiting for transfers between devices, over_core(): return keep + lax.ppermute(give, 'dp', [(d, d ^ 1) for d in range(dps)])  6.97 us
  transfers between devices with their start and end apart: 25, of which 12 were waited for; matrix products, arithmetic and copies ran while one was open for 6% of the time, Pallas kernels for 7%

profile of v6, /device:TPU:0, one launch (start us, length us, event | category | flops | bytes accessed | tf_op | source)
XLA Modules:
  0.0 211.2 jit_solution(11532199522929708670)
XLA Ops:
  0.6 1.0 maximum_bitcast_fusion
  1.6 0.8 broadcast_in_dim.12
  2.4 7.3 %all-to-all-start = ((bf16[8,16,1536]{2,1,0:T(8,128)(2,1)}), bf16[8,16,1536]{2,1,0:T(8,128)(2,1)S(1)}, u32[]{:S(2)}, u32[]{:S(2)}) async-start(bf16[8,16,1536]{2,1,0:T(8,128)(2,1)} %bitcast.9), calls=%async_computation | async-start | bytes 786432 | tf_op jit(solution)/shard_map/all_to_all | solution.py:566
  10.3 11.1 %all-to-all-done = bf16[8,16,1536]{2,1,0:T(8,128)(2,1)S(1)} async-done(((bf16[8,16,1536]{2,1,0:T(8,128)(2,1)}), bf16[8,16,1536]{2,1,0:T(8,128)(2,1)S(1)}, u32[]{:S(2)}, u32[]{:S(2)}) %all-to-all-start) | async-done | bytes 393248 | tf_op jit(solution)/shard_map/all_to_all | solution.py:566
  21.4 0.8 fusion.23
  22.1 38.3 %shard_map.254 = (bf16[8,128,768]{2,1,0:T(8,128)(2,1)}, bf16[8,128,768]{2,1,0:T(8,128)(2,1)}, bf16[8,128,2304]{2,1,0:T(8,128)(2,1)}, bf16[8,1536,128]{2,1,0:T(8,...) custom-call(s32[4,4]{1,0:T(4,128)} %bitcast.125, ...), custom_call_target="tpu_custom_call" | custom-call | tf_op jit(solution)/shard_map/pallas_call | solution.py:320
  60.4 40.9 %shard_map.255 = (bf16[8,128,2304]{2,1,0:T(8,128)(2,1)}, bf16[8,128,768]{2,1,0:T(8,128)(2,1)}, bf16[8,128,3072]{2,1,0:T(8,128)(2,1)}, bf16[128,768]{1,0:T(8,128)...) custom-call(s32[5]{0:T(128)} %stack.65.spot_ref, ...), custom_call_target="tpu_custom_call" | custom-call | tf_op jit(solution)/shard_map/pallas_call | solution.py:364
  101.4 1.0 pad_maximum_fusion.2
  102.4 2.0 collective-permute-done
  104.4 1.5 add.58
  106.0 1.6 collective-permute-start.1
  107.6 1.5 collective-permute-start.2
  109.6 0.6 dynamic-slice_bitcast_fusion
  110.2 6.7 %shard_map.256 = (bf16[2,2,96,1536]{3,2,1,0:T(8,128)(2,1)}, bf16[2,2,96,1536]{3,2,1,0:T(8,128)(2,1)}) custom-call(s32[5]{0:T(128)} %stack.65.spot_ref, bf16[1024,768]{1,0:T(8,128)(2,1)} %bitcast.133, bf16[1024,3072]{1,0:T(8,128)(2,1)} %bitcast.132), custom_call_target="tpu_custom_call" | custom-call | flops 2415919104 | bytes 7077888 | tf_op jit(solution)/shard_map/pallas_call | solution.py:417
  116.9 5.8 %collective-permute-done.2 = bf16[192,768]{1,0:T(8,128)(2,1)S(1)} collective-permute-done((bf16[192,768]{1,0:T(8,128)(2,1)S(1)}, bf16[192,768]{1,0:T(8,128)(2,1)S(1)}, u32[]{:S(2)}, u32[]{:S(2)}) %collective-permute-start.2) | collective-permute-done | bytes 294944 | tf_op jit(solution)/shard_map/ppermute | solution.py:521
  122.8 0.9 collective-permute-start.8
  123.7 2.0 collective-permute-done.4
  126.1 1.2 collective-permute-start.5
  127.4 0.8 collective-permute-start.6
  128.2 1.5 collective-permute-start.7
  129.7 8.2 %shard_map.257 = (bf16[2,2,112,1536]{3,2,1,0:T(8,128)(2,1)}, bf16[2,2,112,1536]{3,2,1,0:T(8,128)(2,1)}) custom-call(s32[5]{0:T(128)} %stack.65.spot_ref, bf16[1024,768]{1,0:T(8,128)(2,1)} %bitcast.113, bf16[1024,2304]{1,0:T(8,128)(2,1)} %bitcast.111, bf16[1024,768]{1,0:T(8,128)(2,1)} %bitcast.114, bf16[1024,768]{1,0:T(8,128)(2,1)} %bitcast.115, ...), custom_call_target="tpu_custom_call" | custom-call | flops 2415919104 | bytes 7077888 | tf_op jit(solution)/shard_map/pallas_call | solution.py:479
  137.9 1.7 collective-permute-done.8
  139.6 2.9 %collective-permute-done.7 = bf16[96,1536]{1,0:T(8,128)(2,1)S(1)} collective-permute-done((bf16[96,1536]{1,0:T(8,128)(2,1)S(1)}, bf16[96,1536]{1,0:T(8,128)(2,1)S(1)}, u32[]{:S(2)}, u32[]{:S(2)}) %collective-permute-start.7) | collective-permute-done | bytes 294944 | tf_op jit(solution)/shard_map/ppermute | solution.py:521
  142.9 2.9 %collective-permute-done.9 = bf16[2,2,112,1536]{3,2,1,0:T(8,128)(2,1)S(1)} collective-permute-done((bf16[2,2,112,1536]{3,2,1,0:T(8,128)(2,1)}, bf16[2,2,112,1536]{3,2,1,0:T(8,128)(2,1)S(1)}, u32[]{:S(2)}, u32[]{:S(2)}) %collective-permute-start.9) | collective-permute-done | bytes 1376288 | tf_op jit(solution)/shard_map/ppermute | solution.py:525
  146.2 0.9 collective-permute-start.10
  147.1 1.5 collective-permute-start.11
  148.6 1.2 collective-permute-start.12
  150.2 16.2 %collective-permute-done.14 = bf16[192,768]{1,0:T(8,128)(2,1)S(1)} collective-permute-done((bf16[192,768]{1,0:T(8,128)(2,1)S(1)}, bf16[192,768]{1,0:T(8,128)(2,1)S(1)}, u32[]{:S(2)}, u32[]{:S(2)}) %collective-permute-start.14) | collective-permute-done | bytes 294944 | tf_op jit(solution)/shard_map/ppermute | solution.py:521
  166.5 0.7 slice_bitcast_fusion.19
  167.3 0.8 collective-permute-start.16
  168.2 0.6 slice_bitcast_fusion.17
  168.9 0.7 pad_maximum_fusion.9
  169.6 1.3 collective-permute-start.18
  170.9 2.0 collective-permute-start.17
  172.9 4.6 %collective-permute-done.17 = bf16[48,1536]{1,0:T(8,128)(2,1)S(1)} collective-permute-done((bf16[48,1536]{1,0:T(8,128)(2,1)}, bf16[48,1536]{1,0:T(8,128)(2,1)S(1)}, u32[]{:S(2)}, u32[]{:S(2)}) %collective-permute-start.17) | collective-permute-done | bytes 147488 | tf_op jit(solution)/shard_map/ppermute | solution.py:521
  177.5 8.7 %collective-permute-done.18 = bf16[80,1536]{1,0:T(8,128)(2,1)S(1)} collective-permute-done((bf16[80,1536]{1,0:T(8,128)(2,1)}, bf16[80,1536]{1,0:T(8,128)(2,1)S(1)}, u32[]{:S(2)}, u32[]{:S(2)}) %collective-permute-start.18) | collective-permute-done | bytes 245792 | tf_op jit(solution)/shard_map/ppermute | solution.py:521
  186.2 0.7 copy-done.2
  187.0 0.8 collective-permute-start.19
  187.8 2.8 %collective-permute-start.21 = (bf16[104,1536]{1,0:T(8,128)(2,1)S(1)}, bf16[104,1536]{1,0:T(8,128)(2,1)}, u32[]{:S(2)}, u32[]{:S(2)}) collective-permute-start(bf16[104,1536]{1,0:T(8,128)(2,1)S(1)} %add.76), channel_id=1, source_target_pairs={{0,12},{1,13},{2,14},{3,15},{4,8},{5,9},{6,10},{7,11},{8,4},{9,5},... | collective-permute-start | bytes 958472 | tf_op jit(solution)/shard_map/ppermute | solution.py:521
  190.8 1.6 pad_maximum_fusion
  193.2 0.8 collective-permute-start.22
  195.4 0.7 fusion.22
  196.1 4.1 %collective-permute-done.19 = bf16[104,1536]{1,0:T(8,128)(2,1)S(1)} collective-permute-done((bf16[104,1536]{1,0:T(8,128)(2,1)S(1)}, bf16[104,1536]{1,0:T(8,128)(2,1)S(1)}, u32[]{:S(2)}, u32[]{:S(2)}) %collective-permute-start.19) | collective-permute-done | bytes 319520 | tf_op jit(solution)/shard_map/ppermute | solution.py:521
  200.2 5.2 %collective-permute-done.21 = bf16[104,1536]{1,0:T(8,128)(2,1)} collective-permute-done((bf16[104,1536]{1,0:T(8,128)(2,1)S(1)}, bf16[104,1536]{1,0:T(8,128)(2,1)}, u32[]{:S(2)}, u32[]{:S(2)}) %collective-permute-start.21) | collective-permute-done | bytes 319520 | tf_op jit(solution)/shard_map/ppermute | solution.py:521
  205.4 1.4 fusion.10
  207.0 0.9 maximum_maximum_fusion.2
  207.9 1.3 maximum_maximum_fusion.1
  209.6 1.6 maximum_maximum_fusion
  (76 shorter events, 6.5 us)
Async XLA Ops:
  2.4 19.0 %all-to-all-start = ((bf16[8,16,1536]{2,1,0:T(8,128)(2,1)}), bf16[8,16,1536]{2,1,0:T(8,128)(2,1)S(1)}, u32[]{:S(2)}, u32[]{:S(2)}) async-start(bf16[8,16,1536]{2,1,0:T(8,128)(2,1)} %bitcast.9), calls=%async_computation | async-start | bytes 786432 | tf_op jit(solution)/shard_map/all_to_all | solution.py:566
  60.4 41.0 %copy-start.5 = (bf16[128,768]{1,0:T(8,128)(2,1)S(1)}, bf16[128,768]{1,0:T(8,128)(2,1)}, u32[]{:S(2)}) copy-start(bf16[128,768]{1,0:T(8,128)(2,1)} %get-tuple-element.96) | copy-start | bytes 589828
  101.3 3.1 %collective-permute-start = (bf16[2,2,192,768]{3,2,1,0:T(8,128)(2,1)}, bf16[2,2,192,768]{3,2,1,0:T(8,128)(2,1)S(1)}, u32[]{:S(2)}, u32[]{:S(2)}) collective-permute-start(bf16[2,2,192,768]{3,2,1,0:T(8,128)(2,1)} %get-tuple-element.90), channel_id=1, source_target_pairs={{0,1},{1,0},{2,3},{3,2},{4,5},{5,4},{6,7},{7,6},{8,9},{9,8},{10,11... | collective-permute-start | bytes 3538952 | tf_op jit(solution)/shard_map/ppermute | solution.py:525
  106.0 10.9 %collective-permute-start.1 = (bf16[192,768]{1,0:T(8,128)(2,1)S(1)}, bf16[192,768]{1,0:T(8,128)(2,1)S(1)}, u32[]{:S(2)}, u32[]{:S(2)}) collective-permute-start(bf16[192,768]{1,0:T(8,128)(2,1)S(1)} %get-tuple-element.160), channel_id=1, source_target_pairs={{0,2},{1,3},{2,0},{3,1},{4,6},{5,7},{6,4},{7,5},{8,10},{9,11},{10,... | collective-permute-start | bytes 884744 | tf_op jit(solution)/shard_map/ppermute | solution.py:521
  107.6 15.1 %collective-permute-start.2 = (bf16[192,768]{1,0:T(8,128)(2,1)S(1)}, bf16[192,768]{1,0:T(8,128)(2,1)S(1)}, u32[]{:S(2)}, u32[]{:S(2)}) collective-permute-start(bf16[192,768]{1,0:T(8,128)(2,1)S(1)} %get-tuple-element.159), channel_id=1, source_target_pairs={{0,4},{1,5},{2,6},{3,7},{4,0},{5,1},{6,2},{7,3},{8,12},{9,13},{10,... | collective-permute-start | bytes 884744 | tf_op jit(solution)/shard_map/ppermute | solution.py:521
  109.1 13.6 %collective-permute-start.3 = (bf16[192,768]{1,0:T(8,128)(2,1)S(1)}, bf16[192,768]{1,0:T(8,128)(2,1)S(1)}, u32[]{:S(2)}, u32[]{:S(2)}) collective-permute-start(bf16[192,768]{1,0:T(8,128)(2,1)S(1)} %get-tuple-element.158), channel_id=1, source_target_pairs={{0,6},{1,7},{2,4},{3,5},{4,2},{5,3},{6,0},{7,1},{8,14},{9,15},{10,... | collective-permute-start | bytes 884744 | tf_op jit(solution)/shard_map/ppermute | solution.py:521
  116.9 8.9 %copy-start.1 = (bf16[2,2,96,1536]{3,2,1,0:T(8,128)(2,1)S(1)}, bf16[2,2,96,1536]{3,2,1,0:T(8,128)(2,1)}, u32[]{:S(2)}) copy-start(bf16[2,2,96,1536]{3,2,1,0:T(8,128)(2,1)} %get-tuple-element.103) | copy-start | bytes 3538948
  122.7 3.1 %collective-permute-start.4 = (bf16[2,2,96,1536]{3,2,1,0:T(8,128)(2,1)}, bf16[2,2,96,1536]{3,2,1,0:T(8,128)(2,1)S(1)}, u32[]{:S(2)}, u32[]{:S(2)}) collective-permute-start(bf16[2,2,96,1536]{3,2,1,0:T(8,128)(2,1)} %get-tuple-element.104), channel_id=1, source_target_pairs={{0,1},{1,0},{2,3},{3,2},{4,5},{5,4},{6,7},{7,6},{8,9},{9,8},{10,11... | collective-permute-start | bytes 3538952 | tf_op jit(solution)/shard_map/ppermute | solution.py:525
  122.8 16.7 %collective-permute-start.8 = (bf16[192,768]{1,0:T(8,128)(2,1)S(1)}, bf16[192,768]{1,0:T(8,128)(2,1)S(1)}, u32[]{:S(2)}, u32[]{:S(2)}) collective-permute-start(bf16[192,768]{1,0:T(8,128)(2,1)S(1)} %fusion.8), channel_id=1, source_target_pairs={{0,16},{1,17},{2,18},{3,19},{4,20},{5,21},{6,22},{7,23},{8,24},{9,... | collective-permute-start | bytes 884744 | tf_op jit(solution)/shard_map/ppermute | solution.py:521
  126.1 13.4 %collective-permute-start.5 = (bf16[96,1536]{1,0:T(8,128)(2,1)S(1)}, bf16[96,1536]{1,0:T(8,128)(2,1)S(1)}, u32[]{:S(2)}, u32[]{:S(2)}) collective-permute-start(bf16[96,1536]{1,0:T(8,128)(2,1)S(1)} %get-tuple-element.157), channel_id=1, source_target_pairs={{0,2},{1,3},{2,0},{3,1},{4,6},{5,7},{6,4},{7,5},{8,10},{9,11},{10,... | collective-permute-start | bytes 884744 | tf_op jit(solution)/shard_map/ppermute | solution.py:521
  127.4 12.2 %collective-permute-start.6 = (bf16[96,1536]{1,0:T(8,128)(2,1)S(1)}, bf16[96,1536]{1,0:T(8,128)(2,1)S(1)}, u32[]{:S(2)}, u32[]{:S(2)}) collective-permute-start(bf16[96,1536]{1,0:T(8,128)(2,1)S(1)} %get-tuple-element.156), channel_id=1, source_target_pairs={{0,4},{1,5},{2,6},{3,7},{4,0},{5,1},{6,2},{7,3},{8,12},{9,13},{10,... | collective-permute-start | bytes 884744 | tf_op jit(solution)/shard_map/ppermute | solution.py:521
  128.2 14.3 %collective-permute-start.7 = (bf16[96,1536]{1,0:T(8,128)(2,1)S(1)}, bf16[96,1536]{1,0:T(8,128)(2,1)S(1)}, u32[]{:S(2)}, u32[]{:S(2)}) collective-permute-start(bf16[96,1536]{1,0:T(8,128)(2,1)S(1)} %get-tuple-element.155), channel_id=1, source_target_pairs={{0,6},{1,7},{2,4},{3,5},{4,2},{5,3},{6,0},{7,1},{8,14},{9,15},{10,... | collective-permute-start | bytes 884744 | tf_op jit(solution)/shard_map/ppermute | solution.py:521
  137.9 7.9 %copy-start = (bf16[2,2,112,1536]{3,2,1,0:T(8,128)(2,1)S(1)}, bf16[2,2,112,1536]{3,2,1,0:T(8,128)(2,1)}, u32[]{:S(2)}) copy-start(bf16[2,2,112,1536]{3,2,1,0:T(8,128)(2,1)} %get-tuple-element.116) | copy-start | bytes 4128772
  142.5 3.3 %collective-permute-start.9 = (bf16[2,2,112,1536]{3,2,1,0:T(8,128)(2,1)}, bf16[2,2,112,1536]{3,2,1,0:T(8,128)(2,1)S(1)}, u32[]{:S(2)}, u32[]{:S(2)}) collective-permute-start(bf16[2,2,112,1536]{3,2,1,0:T(8,128)(2,1)} %get-tuple-element.117), channel_id=1, source_target_pairs={{0,1},{1,0},{2,3},{3,2},{4,5},{5,4},{6,7},{7,6},{8,9},{9,8},{10,11... | collective-permute-start | bytes 4128776 | tf_op jit(solution)/shard_map/ppermute | solution.py:525
  142.7 23.8 %collective-permute-start.13 = (bf16[128,1536]{1,0:T(8,128)(2,1)S(1)}, bf16[128,1536]{1,0:T(8,128)(2,1)S(1)}, u32[]{:S(2)}, u32[]{:S(2)}) collective-permute-start(bf16[128,1536]{1,0:T(8,128)(2,1)S(1)} %pad_maximum_fusion.3), channel_id=1, source_target_pairs={{0,16},{1,17},{2,18},{3,19},{4,20},{5,21},{6,22},{7,23},{8,24},{9,... | collective-permute-start | bytes 1179656 | tf_op jit(solution)/shard_map/ppermute | solution.py:521
  146.2 20.2 %collective-permute-start.10 = (bf16[104,1536]{1,0:T(8,128)(2,1)S(1)}, bf16[104,1536]{1,0:T(8,128)(2,1)S(1)}, u32[]{:S(2)}, u32[]{:S(2)}) collective-permute-start(bf16[104,1536]{1,0:T(8,128)(2,1)S(1)} %get-tuple-element.142), channel_id=1, source_target_pairs={{0,2},{1,3},{2,0},{3,1},{4,6},{5,7},{6,4},{7,5},{8,10},{9,11},{10,... | collective-permute-start | bytes 958472 | tf_op jit(solution)/shard_map/ppermute | solution.py:521
  147.1 19.3 %collective-permute-start.11 = (bf16[104,1536]{1,0:T(8,128)(2,1)S(1)}, bf16[104,1536]{1,0:T(8,128)(2,1)S(1)}, u32[]{:S(2)}, u32[]{:S(2)}) collective-permute-start(bf16[104,1536]{1,0:T(8,128)(2,1)S(1)} %get-tuple-element.141), channel_id=1, source_target_pairs={{0,4},{1,5},{2,6},{3,7},{4,0},{5,1},{6,2},{7,3},{8,12},{9,13},{10,... | collective-permute-start | bytes 958472 | tf_op jit(solution)/shard_map/ppermute | solution.py:521
  148.6 17.9 %collective-permute-start.12 = (bf16[104,1536]{1,0:T(8,128)(2,1)S(1)}, bf16[104,1536]{1,0:T(8,128)(2,1)S(1)}, u32[]{:S(2)}, u32[]{:S(2)}) collective-permute-start(bf16[104,1536]{1,0:T(8,128)(2,1)S(1)} %get-tuple-element.140), channel_id=1, source_target_pairs={{0,6},{1,7},{2,4},{3,5},{4,2},{5,3},{6,0},{7,1},{8,14},{9,15},{10,... | collective-permute-start | bytes 958472 | tf_op jit(solution)/shard_map/ppermute | solution.py:521
  149.8 16.6 %collective-permute-start.14 = (bf16[192,768]{1,0:T(8,128)(2,1)S(1)}, bf16[192,768]{1,0:T(8,128)(2,1)S(1)}, u32[]{:S(2)}, u32[]{:S(2)}) collective-permute-start(bf16[192,768]{1,0:T(8,128)(2,1)S(1)} %add.71), channel_id=1, source_target_pairs={{0,8},{1,9},{2,10},{3,11},{4,12},{5,13},{6,14},{7,15},{8,0},{9,1},... | collective-permute-start | bytes 884744 | tf_op jit(solution)/shard_map/ppermute | solution.py:521
  166.5 2.4 %copy-start.6 = (bf16[16,1536]{1,0:T(8,128)(2,1)S(1)}, bf16[16,1536]{1,0:T(8,128)(2,1)}, u32[]{:S(2)}) copy-start(bf16[16,1536]{1,0:T(8,128)(2,1)} %get-tuple-element.129) | copy-start | bytes 147460
  167.3 19.6 %collective-permute-start.16 = (bf16[2,192,768]{2,1,0:T(8,128)(2,1)S(1)}, bf16[2,192,768]{2,1,0:T(8,128)(2,1)S(1)}, u32[]{:S(2)}, u32[]{:S(2)}) collective-permute-start(bf16[2,192,768]{2,1,0:T(8,128)(2,1)S(1)} %pad_maximum_fusion.1), channel_id=1, source_target_pairs={{0,4},{1,5},{2,6},{3,7},{4,0},{5,1},{6,2},{7,3},{8,12},{9,13},{10,... | collective-permute-start | bytes 1769480 | tf_op jit(solution)/shard_map/ppermute | solution.py:521
  168.9 17.4 %collective-permute-start.15 = (bf16[104,1536]{1,0:T(8,128)(2,1)S(1)}, bf16[104,1536]{1,0:T(8,128)(2,1)S(1)}, u32[]{:S(2)}, u32[]{:S(2)}) collective-permute-start(bf16[104,1536]{1,0:T(8,128)(2,1)S(1)} %fusion.2), channel_id=1, source_target_pairs={{0,16},{1,17},{2,18},{3,19},{4,20},{5,21},{6,22},{7,23},{8,24},{9,... | collective-permute-start | bytes 958472 | tf_op jit(solution)/shard_map/ppermute | solution.py:521
  169.6 16.6 %collective-permute-start.18 = (bf16[80,1536]{1,0:T(8,128)(2,1)}, bf16[80,1536]{1,0:T(8,128)(2,1)S(1)}, u32[]{:S(2)}, u32[]{:S(2)}) collective-permute-start(bf16[80,1536]{1,0:T(8,128)(2,1)} %pad_maximum_fusion.9), channel_id=1, source_target_pairs={{0,4},{1,5},{2,6},{3,7},{4,0},{5,1},{6,2},{7,3},{8,12},{9,13},{10,... | collective-permute-start | bytes 737288 | tf_op jit(solution)/shard_map/ppermute | solution.py:521
  170.9 6.6 %collective-permute-start.17 = (bf16[48,1536]{1,0:T(8,128)(2,1)}, bf16[48,1536]{1,0:T(8,128)(2,1)S(1)}, u32[]{:S(2)}, u32[]{:S(2)}) collective-permute-start(bf16[48,1536]{1,0:T(8,128)(2,1)} %get-tuple-element.176), channel_id=1, source_target_pairs={{0,8},{1,9},{2,10},{3,11},{4,12},{5,13},{6,14},{7,15},{8,0},{9,1},... | collective-permute-start | bytes 442376 | tf_op jit(solution)/shard_map/ppermute | solution.py:521
  186.2 0.7 copy-start.2
  187.0 13.2 %collective-permute-start.19 = (bf16[104,1536]{1,0:T(8,128)(2,1)S(1)}, bf16[104,1536]{1,0:T(8,128)(2,1)S(1)}, u32[]{:S(2)}, u32[]{:S(2)}) collective-permute-start(bf16[104,1536]{1,0:T(8,128)(2,1)S(1)} %add.76), channel_id=1, source_target_pairs={{0,4},{1,5},{2,6},{3,7},{4,0},{5,1},{6,2},{7,3},{8,12},{9,13},{10,... | collective-permute-start | bytes 958472 | tf_op jit(solution)/shard_map/ppermute | solution.py:521
  187.8 12.4 %collective-permute-start.20 = (bf16[104,1536]{1,0:T(8,128)(2,1)S(1)}, bf16[104,1536]{1,0:T(8,128)(2,1)}, u32[]{:S(2)}, u32[]{:S(2)}) collective-permute-start(bf16[104,1536]{1,0:T(8,128)(2,1)S(1)} %add.76), channel_id=1, source_target_pairs={{0,8},{1,9},{2,10},{3,11},{4,12},{5,13},{6,14},{7,15},{8,0},{9,1},... | collective-permute-start | bytes 958472 | tf_op jit(solution)/shard_map/ppermute | solution.py:521
  187.8 17.6 %collective-permute-start.21 = (bf16[104,1536]{1,0:T(8,128)(2,1)S(1)}, bf16[104,1536]{1,0:T(8,128)(2,1)}, u32[]{:S(2)}, u32[]{:S(2)}) collective-permute-start(bf16[104,1536]{1,0:T(8,128)(2,1)S(1)} %add.76), channel_id=1, source_target_pairs={{0,12},{1,13},{2,14},{3,15},{4,8},{5,9},{6,10},{7,11},{8,4},{9,5},... | collective-permute-start | bytes 958472 | tf_op jit(solution)/shard_map/ppermute | solution.py:521
  190.8 2.2 %copy-start.3 = (bf16[80,1536]{1,0:T(8,128)(2,1)S(1)}, bf16[80,1536]{1,0:T(8,128)(2,1)}, u32[]{:S(2)}) copy-start(bf16[80,1536]{1,0:T(8,128)(2,1)} %copy-done.2) | copy-start | bytes 737284
  192.4 2.3 %copy-start.4 = (bf16[1,16,1536]{2,1,0:T(8,128)(2,1)S(1)}, bf16[1,16,1536]{2,1,0:T(8,128)(2,1)}, u32[]{:S(2)}) copy-start(bf16[1,16,1536]{2,1,0:T(8,128)(2,1)} %get-tuple-element.161) | copy-start | bytes 147460
  193.1 16.1 %collective-permute-start.23 = (bf16[2,48,1536]{2,1,0:T(8,128)(2,1)S(1)}, bf16[2,48,1536]{2,1,0:T(8,128)(2,1)S(1)}, u32[]{:S(2)}, u32[]{:S(2)}) collective-permute-start(bf16[2,48,1536]{2,1,0:T(8,128)(2,1)S(1)} %pad_maximum_fusion.5), channel_id=1, source_target_pairs={{0,8},{1,9},{2,10},{3,11},{4,12},{5,13},{6,14},{7,15},{8,0},{9,1},... | collective-permute-start | bytes 884744 | tf_op jit(solution)/shard_map/ppermute | solution.py:521
  193.2 16.0 %collective-permute-start.22 = (bf16[2,48,1536]{2,1,0:T(8,128)(2,1)S(1)}, bf16[2,48,1536]{2,1,0:T(8,128)(2,1)S(1)}, u32[]{:S(2)}, u32[]{:S(2)}) collective-permute-start(bf16[2,48,1536]{2,1,0:T(8,128)(2,1)S(1)} %pad_maximum_fusion.4), channel_id=1, source_target_pairs={{0,4},{1,5},{2,6},{3,7},{4,0},{5,1},{6,2},{7,3},{8,12},{9,13},{10,... | collective-permute-start | bytes 884744 | tf_op jit(solution)/shard_map/ppermute | solution.py:521

commit v7 on v6

--- a/solution.py
+++ b/solution.py
@@ -140,7 +140,7 @@
     wet_ref[...] = we_ref[:, pl.ds(at, strip)].T
     wct_ref[...] = wc_ref[pl.ds(at, strip), :].T
     ebias = row_of(ebias_ref)
-    chunk = 768
+    chunk = 512
     cuts = [slice(chunk * j, chunk * (j + 1)) for j in range(ff // chunk)]
     expand = lambda cut: nn(second_low, we_ref[:, cut]) + ebias[:, cut]
     pres = [expand(cuts[0])]

time: 212 us -> 211 us (level)
  no operation moved by 1% of the time
where the time goes in v7:
time: 211 us; the launch traced here: 210 us
  Pallas kernels  93.3 us (44%)
  waiting for transfers between devices  67.2 us (32%)
  starting transfers between devices  28 us (13%)
  other arithmetic  13.9 us (7%)
  local copies, waits for them, and re-layouts  7.09 us (3%)
    ppermute x21, waiting for transfers between devices, move(): return lax.ppermute(array, AXES, pairs)  49.1 us
    pallas_call x1, Pallas kernels, backward_all(): pl.pallas_call(partial(backward_kernel, fused=fused), grid_spec=pltpu.Pre...  40.9 us
    pallas_call x1, Pallas kernels, forward_all(): pl.pallas_call(forward_kernel, grid_spec=pltpu.PrefetchScalarGridSpec(num...  37.5 us
    ppermute x21, starting transfers between devices, move(): return lax.ppermute(array, AXES, pairs)  20.7 us
    all_to_all x1, waiting for transfers between devices, body(): lax.all_to_all(outgoing, 'section', 0, 0, tiled=True)  11.1 us
    pallas_call x1, Pallas kernels, attention_grads(): pl.pallas_call(attention_kernel, grid_spec=pltpu.PrefetchScalarGridSpec(n...  8.2 us
    all_to_all x1, starting transfers between devices, body(): lax.all_to_all(outgoing, 'section', 0, 0, tiled=True)  7.28 us
    ppermute x3, waiting for transfers between devices, over_core(): return keep + lax.ppermute(give, 'dp', [(d, d ^ 1) for d in range(dps)])  6.98 us
  transfers between devices with their start and end apart: 25, of which 12 were waited for; matrix products, arithmetic and copies ran while one was open for 6% of the time, Pallas kernels for 7%

profile of v7, /device:TPU:0, one launch (start us, length us, event | category | flops | bytes accessed | tf_op | source)
XLA Modules:
  0.0 210.5 jit_solution(13708054727092716383)
XLA Ops:
  0.6 1.0 maximum_bitcast_fusion
  1.6 0.8 broadcast_in_dim.12
  2.4 7.3 %all-to-all-start = ((bf16[8,16,1536]{2,1,0:T(8,128)(2,1)}), bf16[8,16,1536]{2,1,0:T(8,128)(2,1)S(1)}, u32[]{:S(2)}, u32[]{:S(2)}) async-start(bf16[8,16,1536]{2,1,0:T(8,128)(2,1)} %bitcast.9), calls=%async_computation | async-start | bytes 786432 | tf_op jit(solution)/shard_map/all_to_all | solution.py:566
  10.3 11.1 %all-to-all-done = bf16[8,16,1536]{2,1,0:T(8,128)(2,1)S(1)} async-done(((bf16[8,16,1536]{2,1,0:T(8,128)(2,1)}), bf16[8,16,1536]{2,1,0:T(8,128)(2,1)S(1)}, u32[]{:S(2)}, u32[]{:S(2)}) %all-to-all-start) | async-done | bytes 393248 | tf_op jit(solution)/shard_map/all_to_all | solution.py:566
  21.4 0.8 fusion.23
  22.1 37.5 %shard_map.254 = (bf16[8,128,768]{2,1,0:T(8,128)(2,1)}, bf16[8,128,768]{2,1,0:T(8,128)(2,1)}, bf16[8,128,2304]{2,1,0:T(8,128)(2,1)}, bf16[8,1536,128]{2,1,0:T(8,...) custom-call(s32[4,4]{1,0:T(4,128)} %bitcast.125, ...), custom_call_target="tpu_custom_call" | custom-call | tf_op jit(solution)/shard_map/pallas_call | solution.py:320
  59.6 40.9 %shard_map.255 = (bf16[8,128,2304]{2,1,0:T(8,128)(2,1)}, bf16[8,128,768]{2,1,0:T(8,128)(2,1)}, bf16[8,128,3072]{2,1,0:T(8,128)(2,1)}, bf16[128,768]{1,0:T(8,128)...) custom-call(s32[5]{0:T(128)} %stack.65.spot_ref, ...), custom_call_target="tpu_custom_call" | custom-call | tf_op jit(solution)/shard_map/pallas_call | solution.py:364
  100.7 1.0 pad_maximum_fusion.2
  101.6 2.0 collective-permute-done
  103.7 1.5 add.58
  105.3 1.6 collective-permute-start.1
  106.8 1.4 collective-permute-start.2
  108.8 0.6 dynamic-slice_bitcast_fusion
  109.5 6.7 %shard_map.256 = (bf16[2,2,96,1536]{3,2,1,0:T(8,128)(2,1)}, bf16[2,2,96,1536]{3,2,1,0:T(8,128)(2,1)}) custom-call(s32[5]{0:T(128)} %stack.65.spot_ref, bf16[1024,768]{1,0:T(8,128)(2,1)} %bitcast.133, bf16[1024,3072]{1,0:T(8,128)(2,1)} %bitcast.132), custom_call_target="tpu_custom_call" | custom-call | flops 2415919104 | bytes 7077888 | tf_op jit(solution)/shard_map/pallas_call | solution.py:417
  116.1 5.8 %collective-permute-done.2 = bf16[192,768]{1,0:T(8,128)(2,1)S(1)} collective-permute-done((bf16[192,768]{1,0:T(8,128)(2,1)S(1)}, bf16[192,768]{1,0:T(8,128)(2,1)S(1)}, u32[]{:S(2)}, u32[]{:S(2)}) %collective-permute-start.2) | collective-permute-done | bytes 294944 | tf_op jit(solution)/shard_map/ppermute | solution.py:521
  122.1 0.9 collective-permute-start.8
  123.0 2.0 collective-permute-done.4
  125.4 1.2 collective-permute-start.5
  126.6 0.8 collective-permute-start.6
  127.4 1.5 collective-permute-start.7
  128.9 8.2 %shard_map.257 = (bf16[2,2,112,1536]{3,2,1,0:T(8,128)(2,1)}, bf16[2,2,112,1536]{3,2,1,0:T(8,128)(2,1)}) custom-call(s32[5]{0:T(128)} %stack.65.spot_ref, bf16[1024,768]{1,0:T(8,128)(2,1)} %bitcast.113, bf16[1024,2304]{1,0:T(8,128)(2,1)} %bitcast.111, bf16[1024,768]{1,0:T(8,128)(2,1)} %bitcast.114, bf16[1024,768]{1,0:T(8,128)(2,1)} %bitcast.115, ...), custom_call_target="tpu_custom_call" | custom-call | flops 2415919104 | bytes 7077888 | tf_op jit(solution)/shard_map/pallas_call | solution.py:479
  137.1 1.7 collective-permute-done.8
  138.8 2.9 %collective-permute-done.7 = bf16[96,1536]{1,0:T(8,128)(2,1)S(1)} collective-permute-done((bf16[96,1536]{1,0:T(8,128)(2,1)S(1)}, bf16[96,1536]{1,0:T(8,128)(2,1)S(1)}, u32[]{:S(2)}, u32[]{:S(2)}) %collective-permute-start.7) | collective-permute-done | bytes 294944 | tf_op jit(solution)/shard_map/ppermute | solution.py:521
  142.1 2.9 %collective-permute-done.9 = bf16[2,2,112,1536]{3,2,1,0:T(8,128)(2,1)S(1)} collective-permute-done((bf16[2,2,112,1536]{3,2,1,0:T(8,128)(2,1)}, bf16[2,2,112,1536]{3,2,1,0:T(8,128)(2,1)S(1)}, u32[]{:S(2)}, u32[]{:S(2)}) %collective-permute-start.9) | collective-permute-done | bytes 1376288 | tf_op jit(solution)/shard_map/ppermute | solution.py:525
  145.4 0.9 collective-permute-start.10
  146.4 1.4 collective-permute-start.11
  147.8 1.2 collective-permute-start.12
  149.4 16.2 %collective-permute-done.14 = bf16[192,768]{1,0:T(8,128)(2,1)S(1)} collective-permute-done((bf16[192,768]{1,0:T(8,128)(2,1)S(1)}, bf16[192,768]{1,0:T(8,128)(2,1)S(1)}, u32[]{:S(2)}, u32[]{:S(2)}) %collective-permute-start.14) | collective-permute-done | bytes 294944 | tf_op jit(solution)/shard_map/ppermute | solution.py:521
  165.8 0.7 slice_bitcast_fusion.19
  166.5 0.8 collective-permute-start.16
  167.5 0.6 slice_bitcast_fusion.17
  168.1 0.7 pad_maximum_fusion.9
  168.8 1.3 collective-permute-start.18
  170.1 2.0 collective-permute-start.17
  172.2 4.6 %collective-permute-done.17 = bf16[48,1536]{1,0:T(8,128)(2,1)S(1)} collective-permute-done((bf16[48,1536]{1,0:T(8,128)(2,1)}, bf16[48,1536]{1,0:T(8,128)(2,1)S(1)}, u32[]{:S(2)}, u32[]{:S(2)}) %collective-permute-start.17) | collective-permute-done | bytes 147488 | tf_op jit(solution)/shard_map/ppermute | solution.py:521
  176.7 8.7 %collective-permute-done.18 = bf16[80,1536]{1,0:T(8,128)(2,1)S(1)} collective-permute-done((bf16[80,1536]{1,0:T(8,128)(2,1)}, bf16[80,1536]{1,0:T(8,128)(2,1)S(1)}, u32[]{:S(2)}, u32[]{:S(2)}) %collective-permute-start.18) | collective-permute-done | bytes 245792 | tf_op jit(solution)/shard_map/ppermute | solution.py:521
  185.5 0.7 copy-done.2
  186.2 0.8 collective-permute-start.19
  187.0 2.8 %collective-permute-start.21 = (bf16[104,1536]{1,0:T(8,128)(2,1)S(1)}, bf16[104,1536]{1,0:T(8,128)(2,1)}, u32[]{:S(2)}, u32[]{:S(2)}) collective-permute-start(bf16[104,1536]{1,0:T(8,128)(2,1)S(1)} %add.76), channel_id=1, source_target_pairs={{0,12},{1,13},{2,14},{3,15},{4,8},{5,9},{6,10},{7,11},{8,4},{9,5},... | collective-permute-start | bytes 958472 | tf_op jit(solution)/shard_map/ppermute | solution.py:521
  190.0 1.6 pad_maximum_fusion
  192.4 0.8 collective-permute-start.22
  194.6 0.7 fusion.22
  195.3 4.1 %collective-permute-done.19 = bf16[104,1536]{1,0:T(8,128)(2,1)S(1)} collective-permute-done((bf16[104,1536]{1,0:T(8,128)(2,1)S(1)}, bf16[104,1536]{1,0:T(8,128)(2,1)S(1)}, u32[]{:S(2)}, u32[]{:S(2)}) %collective-permute-start.19) | collective-permute-done | bytes 319520 | tf_op jit(solution)/shard_map/ppermute | solution.py:521
  199.4 5.2 %collective-permute-done.21 = bf16[104,1536]{1,0:T(8,128)(2,1)} collective-permute-done((bf16[104,1536]{1,0:T(8,128)(2,1)S(1)}, bf16[104,1536]{1,0:T(8,128)(2,1)}, u32[]{:S(2)}, u32[]{:S(2)}) %collective-permute-start.21) | collective-permute-done | bytes 319520 | tf_op jit(solution)/shard_map/ppermute | solution.py:521
  204.6 1.4 fusion.10
  206.2 0.9 maximum_maximum_fusion.2
  207.1 1.3 maximum_maximum_fusion.1
  208.9 1.6 maximum_maximum_fusion
  (76 shorter events, 6.5 us)
Async XLA Ops:
  2.4 19.0 %all-to-all-start = ((bf16[8,16,1536]{2,1,0:T(8,128)(2,1)}), bf16[8,16,1536]{2,1,0:T(8,128)(2,1)S(1)}, u32[]{:S(2)}, u32[]{:S(2)}) async-start(bf16[8,16,1536]{2,1,0:T(8,128)(2,1)} %bitcast.9), calls=%async_computation | async-start | bytes 786432 | tf_op jit(solution)/shard_map/all_to_all | solution.py:566
  59.6 41.0 %copy-start.5 = (bf16[128,768]{1,0:T(8,128)(2,1)S(1)}, bf16[128,768]{1,0:T(8,128)(2,1)}, u32[]{:S(2)}) copy-start(bf16[128,768]{1,0:T(8,128)(2,1)} %get-tuple-element.96) | copy-start | bytes 589828
  100.5 3.1 %collective-permute-start = (bf16[2,2,192,768]{3,2,1,0:T(8,128)(2,1)}, bf16[2,2,192,768]{3,2,1,0:T(8,128)(2,1)S(1)}, u32[]{:S(2)}, u32[]{:S(2)}) collective-permute-start(bf16[2,2,192,768]{3,2,1,0:T(8,128)(2,1)} %get-tuple-element.90), channel_id=1, source_target_pairs={{0,1},{1,0},{2,3},{3,2},{4,5},{5,4},{6,7},{7,6},{8,9},{9,8},{10,11... | collective-permute-start | bytes 3538952 | tf_op jit(solution)/shard_map/ppermute | solution.py:525
  105.3 10.9 %collective-permute-start.1 = (bf16[192,768]{1,0:T(8,128)(2,1)S(1)}, bf16[192,768]{1,0:T(8,128)(2,1)S(1)}, u32[]{:S(2)}, u32[]{:S(2)}) collective-permute-start(bf16[192,768]{1,0:T(8,128)(2,1)S(1)} %get-tuple-element.160), channel_id=1, source_target_pairs={{0,2},{1,3},{2,0},{3,1},{4,6},{5,7},{6,4},{7,5},{8,10},{9,11},{10,... | collective-permute-start | bytes 884744 | tf_op jit(solution)/shard_map/ppermute | solution.py:521
  106.8 15.1 %collective-permute-start.2 = (bf16[192,768]{1,0:T(8,128)(2,1)S(1)}, bf16[192,768]{1,0:T(8,128)(2,1)S(1)}, u32[]{:S(2)}, u32[]{:S(2)}) collective-permute-start(bf16[192,768]{1,0:T(8,128)(2,1)S(1)} %get-tuple-element.159), channel_id=1, source_target_pairs={{0,4},{1,5},{2,6},{3,7},{4,0},{5,1},{6,2},{7,3},{8,12},{9,13},{10,... | collective-permute-start | bytes 884744 | tf_op jit(solution)/shard_map/ppermute | solution.py:521
  108.3 13.6 %collective-permute-start.3 = (bf16[192,768]{1,0:T(8,128)(2,1)S(1)}, bf16[192,768]{1,0:T(8,128)(2,1)S(1)}, u32[]{:S(2)}, u32[]{:S(2)}) collective-permute-start(bf16[192,768]{1,0:T(8,128)(2,1)S(1)} %get-tuple-element.158), channel_id=1, source_target_pairs={{0,6},{1,7},{2,4},{3,5},{4,2},{5,3},{6,0},{7,1},{8,14},{9,15},{10,... | collective-permute-start | bytes 884744 | tf_op jit(solution)/shard_map/ppermute | solution.py:521
  116.1 8.9 %copy-start.1 = (bf16[2,2,96,1536]{3,2,1,0:T(8,128)(2,1)S(1)}, bf16[2,2,96,1536]{3,2,1,0:T(8,128)(2,1)}, u32[]{:S(2)}) copy-start(bf16[2,2,96,1536]{3,2,1,0:T(8,128)(2,1)} %get-tuple-element.103) | copy-start | bytes 3538948
  121.9 3.1 %collective-permute-start.4 = (bf16[2,2,96,1536]{3,2,1,0:T(8,128)(2,1)}, bf16[2,2,96,1536]{3,2,1,0:T(8,128)(2,1)S(1)}, u32[]{:S(2)}, u32[]{:S(2)}) collective-permute-start(bf16[2,2,96,1536]{3,2,1,0:T(8,128)(2,1)} %get-tuple-element.104), channel_id=1, source_target_pairs={{0,1},{1,0},{2,3},{3,2},{4,5},{5,4},{6,7},{7,6},{8,9},{9,8},{10,11... | collective-permute-start | bytes 3538952 | tf_op jit(solution)/shard_map/ppermute | solution.py:525
  122.1 16.7 %collective-permute-start.8 = (bf16[192,768]{1,0:T(8,128)(2,1)S(1)}, bf16[192,768]{1,0:T(8,128)(2,1)S(1)}, u32[]{:S(2)}, u32[]{:S(2)}) collective-permute-start(bf16[192,768]{1,0:T(8,128)(2,1)S(1)} %fusion.8), channel_id=1, source_target_pairs={{0,16},{1,17},{2,18},{3,19},{4,20},{5,21},{6,22},{7,23},{8,24},{9,... | collective-permute-start | bytes 884744 | tf_op jit(solution)/shard_map/ppermute | solution.py:521
  125.4 13.4 %collective-permute-start.5 = (bf16[96,1536]{1,0:T(8,128)(2,1)S(1)}, bf16[96,1536]{1,0:T(8,128)(2,1)S(1)}, u32[]{:S(2)}, u32[]{:S(2)}) collective-permute-start(bf16[96,1536]{1,0:T(8,128)(2,1)S(1)} %get-tuple-element.157), channel_id=1, source_target_pairs={{0,2},{1,3},{2,0},{3,1},{4,6},{5,7},{6,4},{7,5},{8,10},{9,11},{10,... | collective-permute-start | bytes 884744 | tf_op jit(solution)/shard_map/ppermute | solution.py:521
  126.6 12.2 %collective-permute-start.6 = (bf16[96,1536]{1,0:T(8,128)(2,1)S(1)}, bf16[96,1536]{1,0:T(8,128)(2,1)S(1)}, u32[]{:S(2)}, u32[]{:S(2)}) collective-permute-start(bf16[96,1536]{1,0:T(8,128)(2,1)S(1)} %get-tuple-element.156), channel_id=1, source_target_pairs={{0,4},{1,5},{2,6},{3,7},{4,0},{5,1},{6,2},{7,3},{8,12},{9,13},{10,... | collective-permute-start | bytes 884744 | tf_op jit(solution)/shard_map/ppermute | solution.py:521
  127.4 14.3 %collective-permute-start.7 = (bf16[96,1536]{1,0:T(8,128)(2,1)S(1)}, bf16[96,1536]{1,0:T(8,128)(2,1)S(1)}, u32[]{:S(2)}, u32[]{:S(2)}) collective-permute-start(bf16[96,1536]{1,0:T(8,128)(2,1)S(1)} %get-tuple-element.155), channel_id=1, source_target_pairs={{0,6},{1,7},{2,4},{3,5},{4,2},{5,3},{6,0},{7,1},{8,14},{9,15},{10,... | collective-permute-start | bytes 884744 | tf_op jit(solution)/shard_map/ppermute | solution.py:521
  137.1 7.9 %copy-start = (bf16[2,2,112,1536]{3,2,1,0:T(8,128)(2,1)S(1)}, bf16[2,2,112,1536]{3,2,1,0:T(8,128)(2,1)}, u32[]{:S(2)}) copy-start(bf16[2,2,112,1536]{3,2,1,0:T(8,128)(2,1)} %get-tuple-element.116) | copy-start | bytes 4128772
  141.7 3.3 %collective-permute-start.9 = (bf16[2,2,112,1536]{3,2,1,0:T(8,128)(2,1)}, bf16[2,2,112,1536]{3,2,1,0:T(8,128)(2,1)S(1)}, u32[]{:S(2)}, u32[]{:S(2)}) collective-permute-start(bf16[2,2,112,1536]{3,2,1,0:T(8,128)(2,1)} %get-tuple-element.117), channel_id=1, source_target_pairs={{0,1},{1,0},{2,3},{3,2},{4,5},{5,4},{6,7},{7,6},{8,9},{9,8},{10,11... | collective-permute-start | bytes 4128776 | tf_op jit(solution)/shard_map/ppermute | solution.py:525
  141.9 23.8 %collective-permute-start.13 = (bf16[128,1536]{1,0:T(8,128)(2,1)S(1)}, bf16[128,1536]{1,0:T(8,128)(2,1)S(1)}, u32[]{:S(2)}, u32[]{:S(2)}) collective-permute-start(bf16[128,1536]{1,0:T(8,128)(2,1)S(1)} %pad_maximum_fusion.3), channel_id=1, source_target_pairs={{0,16},{1,17},{2,18},{3,19},{4,20},{5,21},{6,22},{7,23},{8,24},{9,... | collective-permute-start | bytes 1179656 | tf_op jit(solution)/shard_map/ppermute | solution.py:521
  145.4 20.2 %collective-permute-start.10 = (bf16[104,1536]{1,0:T(8,128)(2,1)S(1)}, bf16[104,1536]{1,0:T(8,128)(2,1)S(1)}, u32[]{:S(2)}, u32[]{:S(2)}) collective-permute-start(bf16[104,1536]{1,0:T(8,128)(2,1)S(1)} %get-tuple-element.142), channel_id=1, source_target_pairs={{0,2},{1,3},{2,0},{3,1},{4,6},{5,7},{6,4},{7,5},{8,10},{9,11},{10,... | collective-permute-start | bytes 958472 | tf_op jit(solution)/shard_map/ppermute | solution.py:521
  146.4 19.3 %collective-permute-start.11 = (bf16[104,1536]{1,0:T(8,128)(2,1)S(1)}, bf16[104,1536]{1,0:T(8,128)(2,1)S(1)}, u32[]{:S(2)}, u32[]{:S(2)}) collective-permute-start(bf16[104,1536]{1,0:T(8,128)(2,1)S(1)} %get-tuple-element.141), channel_id=1, source_target_pairs={{0,4},{1,5},{2,6},{3,7},{4,0},{5,1},{6,2},{7,3},{8,12},{9,13},{10,... | collective-permute-start | bytes 958472 | tf_op jit(solution)/shard_map/ppermute | solution.py:521
  147.8 17.9 %collective-permute-start.12 = (bf16[104,1536]{1,0:T(8,128)(2,1)S(1)}, bf16[104,1536]{1,0:T(8,128)(2,1)S(1)}, u32[]{:S(2)}, u32[]{:S(2)}) collective-permute-start(bf16[104,1536]{1,0:T(8,128)(2,1)S(1)} %get-tuple-element.140), channel_id=1, source_target_pairs={{0,6},{1,7},{2,4},{3,5},{4,2},{5,3},{6,0},{7,1},{8,14},{9,15},{10,... | collective-permute-start | bytes 958472 | tf_op jit(solution)/shard_map/ppermute | solution.py:521
  149.1 16.6 %collective-permute-start.14 = (bf16[192,768]{1,0:T(8,128)(2,1)S(1)}, bf16[192,768]{1,0:T(8,128)(2,1)S(1)}, u32[]{:S(2)}, u32[]{:S(2)}) collective-permute-start(bf16[192,768]{1,0:T(8,128)(2,1)S(1)} %add.71), channel_id=1, source_target_pairs={{0,8},{1,9},{2,10},{3,11},{4,12},{5,13},{6,14},{7,15},{8,0},{9,1},... | collective-permute-start | bytes 884744 | tf_op jit(solution)/shard_map/ppermute | solution.py:521
  165.7 2.4 %copy-start.6 = (bf16[16,1536]{1,0:T(8,128)(2,1)S(1)}, bf16[16,1536]{1,0:T(8,128)(2,1)}, u32[]{:S(2)}) copy-start(bf16[16,1536]{1,0:T(8,128)(2,1)} %get-tuple-element.129) | copy-start | bytes 147460
  166.5 19.6 %collective-permute-start.16 = (bf16[2,192,768]{2,1,0:T(8,128)(2,1)S(1)}, bf16[2,192,768]{2,1,0:T(8,128)(2,1)S(1)}, u32[]{:S(2)}, u32[]{:S(2)}) collective-permute-start(bf16[2,192,768]{2,1,0:T(8,128)(2,1)S(1)} %pad_maximum_fusion.1), channel_id=1, source_target_pairs={{0,4},{1,5},{2,6},{3,7},{4,0},{5,1},{6,2},{7,3},{8,12},{9,13},{10,... | collective-permute-start | bytes 1769480 | tf_op jit(solution)/shard_map/ppermute | solution.py:521
  168.1 17.4 %collective-permute-start.15 = (bf16[104,1536]{1,0:T(8,128)(2,1)S(1)}, bf16[104,1536]{1,0:T(8,128)(2,1)S(1)}, u32[]{:S(2)}, u32[]{:S(2)}) collective-permute-start(bf16[104,1536]{1,0:T(8,128)(2,1)S(1)} %fusion.2), channel_id=1, source_target_pairs={{0,16},{1,17},{2,18},{3,19},{4,20},{5,21},{6,22},{7,23},{8,24},{9,... | collective-permute-start | bytes 958472 | tf_op jit(solution)/shard_map/ppermute | solution.py:521
  168.8 16.6 %collective-permute-start.18 = (bf16[80,1536]{1,0:T(8,128)(2,1)}, bf16[80,1536]{1,0:T(8,128)(2,1)S(1)}, u32[]{:S(2)}, u32[]{:S(2)}) collective-permute-start(bf16[80,1536]{1,0:T(8,128)(2,1)} %pad_maximum_fusion.9), channel_id=1, source_target_pairs={{0,4},{1,5},{2,6},{3,7},{4,0},{5,1},{6,2},{7,3},{8,12},{9,13},{10,... | collective-permute-start | bytes 737288 | tf_op jit(solution)/shard_map/ppermute | solution.py:521
  170.1 6.6 %collective-permute-start.17 = (bf16[48,1536]{1,0:T(8,128)(2,1)}, bf16[48,1536]{1,0:T(8,128)(2,1)S(1)}, u32[]{:S(2)}, u32[]{:S(2)}) collective-permute-start(bf16[48,1536]{1,0:T(8,128)(2,1)} %get-tuple-element.176), channel_id=1, source_target_pairs={{0,8},{1,9},{2,10},{3,11},{4,12},{5,13},{6,14},{7,15},{8,0},{9,1},... | collective-permute-start | bytes 442376 | tf_op jit(solution)/shard_map/ppermute | solution.py:521
  185.5 0.7 copy-start.2
  186.2 13.2 %collective-permute-start.19 = (bf16[104,1536]{1,0:T(8,128)(2,1)S(1)}, bf16[104,1536]{1,0:T(8,128)(2,1)S(1)}, u32[]{:S(2)}, u32[]{:S(2)}) collective-permute-start(bf16[104,1536]{1,0:T(8,128)(2,1)S(1)} %add.76), channel_id=1, source_target_pairs={{0,4},{1,5},{2,6},{3,7},{4,0},{5,1},{6,2},{7,3},{8,12},{9,13},{10,... | collective-permute-start | bytes 958472 | tf_op jit(solution)/shard_map/ppermute | solution.py:521
  187.0 12.4 %collective-permute-start.20 = (bf16[104,1536]{1,0:T(8,128)(2,1)S(1)}, bf16[104,1536]{1,0:T(8,128)(2,1)}, u32[]{:S(2)}, u32[]{:S(2)}) collective-permute-start(bf16[104,1536]{1,0:T(8,128)(2,1)S(1)} %add.76), channel_id=1, source_target_pairs={{0,8},{1,9},{2,10},{3,11},{4,12},{5,13},{6,14},{7,15},{8,0},{9,1},... | collective-permute-start | bytes 958472 | tf_op jit(solution)/shard_map/ppermute | solution.py:521
  187.0 17.6 %collective-permute-start.21 = (bf16[104,1536]{1,0:T(8,128)(2,1)S(1)}, bf16[104,1536]{1,0:T(8,128)(2,1)}, u32[]{:S(2)}, u32[]{:S(2)}) collective-permute-start(bf16[104,1536]{1,0:T(8,128)(2,1)S(1)} %add.76), channel_id=1, source_target_pairs={{0,12},{1,13},{2,14},{3,15},{4,8},{5,9},{6,10},{7,11},{8,4},{9,5},... | collective-permute-start | bytes 958472 | tf_op jit(solution)/shard_map/ppermute | solution.py:521
  190.0 2.2 %copy-start.3 = (bf16[80,1536]{1,0:T(8,128)(2,1)S(1)}, bf16[80,1536]{1,0:T(8,128)(2,1)}, u32[]{:S(2)}) copy-start(bf16[80,1536]{1,0:T(8,128)(2,1)} %copy-done.2) | copy-start | bytes 737284
  191.6 2.3 %copy-start.4 = (bf16[1,16,1536]{2,1,0:T(8,128)(2,1)S(1)}, bf16[1,16,1536]{2,1,0:T(8,128)(2,1)}, u32[]{:S(2)}) copy-start(bf16[1,16,1536]{2,1,0:T(8,128)(2,1)} %get-tuple-element.161) | copy-start | bytes 147460
  192.3 16.1 %collective-permute-start.23 = (bf16[2,48,1536]{2,1,0:T(8,128)(2,1)S(1)}, bf16[2,48,1536]{2,1,0:T(8,128)(2,1)S(1)}, u32[]{:S(2)}, u32[]{:S(2)}) collective-permute-start(bf16[2,48,1536]{2,1,0:T(8,128)(2,1)S(1)} %pad_maximum_fusion.5), channel_id=1, source_target_pairs={{0,8},{1,9},{2,10},{3,11},{4,12},{5,13},{6,14},{7,15},{8,0},{9,1},... | collective-permute-start | bytes 884744 | tf_op jit(solution)/shard_map/ppermute | solution.py:521
  192.4 16.0 %collective-permute-start.22 = (bf16[2,48,1536]{2,1,0:T(8,128)(2,1)S(1)}, bf16[2,48,1536]{2,1,0:T(8,128)(2,1)S(1)}, u32[]{:S(2)}, u32[]{:S(2)}) collective-permute-start(bf16[2,48,1536]{2,1,0:T(8,128)(2,1)S(1)} %pad_maximum_fusion.4), channel_id=1, source_target_pairs={{0,4},{1,5},{2,6},{3,7},{4,0},{5,1},{6,2},{7,3},{8,12},{9,13},{10,... | collective-permute-start | bytes 884744 | tf_op jit(solution)/shard_map/ppermute | solution.py:521
